TPU v7x, 32 devices: a whole 2x2x4 slice. The times are simulated.
32 devices in a mesh: expert: 4 (over z), context: 4 (over x, core), dp: 2 (over y).
Axes of the slice: x: 2, y: 2, z: 4, core: 2. Of those that a mesh axis runs over, the one named last changes fastest.
Arguments:
- tokens: bfloat16 [16, 640, 768], P(('expert', 'dp'), 'context'), may hold values from -6 to 6
- lengths: int32 [16, 4], P(('expert', 'dp')), may hold values from 1 to 160, 577 in all within a row
- route_ids: int32 [16, 640, 2], P(('expert', 'dp'), 'context'), may hold values from 0 to 3, all different within a row; in each aligned block of 160 rows (0 to 159, 160 to 319, ..., all dimensions but the last counted through in order) at most 128 rows name the same one
- keep_mask: int32 [16, 640, 2], P(('expert', 'dp'), 'context'), may hold values 0 or 1
- w_qkv: bfloat16 [768, 2304], P(('expert', 'dp')), may hold values from -0.21875 to 0.21875
- w_attn_out: bfloat16 [768, 768], P(('expert', 'dp')), may hold values from -6 to 6
- w_router: bfloat16 [768, 4], P(('expert', 'dp')), may hold values from -0.375 to 0.375
- norm_gains: bfloat16 [2, 768], P(None, ('expert', 'dp')), may hold values from 0.25 to 1.75
- norm_biases: bfloat16 [2, 768], P(None, ('expert', 'dp')), may hold values from -1 to 1
- w_expert_in: bfloat16 [4, 768, 3072], P('expert'), may hold values from -0.21875 to 0.21875
- w_expert_down: bfloat16 [4, 3072, 768], P('expert'), may hold values from -1 to 1
- cotangent: bfloat16 [16, 640, 768], P(('expert', 'dp'), 'context'), may hold values from -6 to 6
Outputs:
- output: bfloat16 [16, 640, 768], P(('expert', 'dp'), 'context')
- grad_tokens: float32 [16, 640, 768], P(('expert', 'dp'), 'context')
- grad_qkv: float32 [768, 2304], P(('expert', 'dp'))
- grad_attn_out: float32 [768, 768], P(('expert', 'dp'))
- grad_router: float32 [768, 4], P(('expert', 'dp'))
- grad_gains: float32 [2, 768], P(None, ('expert', 'dp'))
- grad_biases: float32 [2, 768], P(None, ('expert', 'dp'))
- grad_expert_in: float32 [4, 768, 3072], P('expert', None, ('context', 'dp'))
- grad_expert_down: float32 [4, 3072, 768], P('expert', ('context', 'dp'))
Inputs may be any that keep to these rules, and one draw needn't show every extreme that they name: `route_ids`: each row names two different experts; in each aligned block of 160 rows (one image's block of slots) no expert is named more than 128 times. An image's 4 block lengths sum to 577; the largest is exactly 160.
All inputs are finite; a program needn't handle non-finite values. No bound on the sum of `keep_mask` on one device may be relied on, other than what follows from the above.
Results may differ from a plain program's by a relative error of at most 0.017.
Values may be sent and summed in bfloat16 or wider, within the bound.
A program may use at most 192 MiB of HBM per device.

v0:
```python
import jax
import jax.numpy as jnp
from jax import lax
from jax.sharding import PartitionSpec as P

HEADS = 12
MICRO = 2


epsilon = 1e-06
precise = lax.Precision.HIGHEST


def as_sent(array):

    def short(part):
        return part.astype(jnp.bfloat16) if part.dtype == jnp.float32 else part

    return jax.tree.map(short, array)


def norm_rows(values, gain, shift):
    centred = values - jnp.mean(values, axis=-1, keepdims=True)
    inverse = lax.rsqrt(jnp.mean(centred * centred, axis=-1, keepdims=True) + epsilon)
    unit_rows = centred * inverse
    return (unit_rows * gain + shift, unit_rows, inverse)


def norm_back(grad_out, unit_rows, inverse, gain):
    scaled = grad_out * gain
    centre_term = jnp.mean(scaled, axis=-1, keepdims=True)
    slope_term = jnp.mean(scaled * unit_rows, axis=-1, keepdims=True)
    return inverse * (scaled - centre_term - unit_rows * slope_term)


def slot_ranks(route_ids, n_experts):
    image_count, block_rows, top_count = route_ids.shape
    flat_ids = route_ids.reshape(image_count, block_rows * top_count)
    expert_range = jnp.arange(n_experts, dtype=jnp.int32)
    one_hot = (flat_ids[:, :, None] == expert_range[None, None, :]).astype(jnp.int32)
    earlier = jnp.cumsum(one_hot, axis=1) - one_hot
    return jnp.sum(earlier * one_hot, axis=2).reshape(image_count, block_rows, top_count)


def per_device(
    tokens,
    lengths,
    route_ids,
    keep_mask,
    w_qkv,
    w_attn_out,
    w_router,
    norm_gains,
    norm_biases,
    w_expert_in,
    w_expert_down,
    cotangent,
):
    ctx_count = lax.axis_size("context")
    ctx_rank = lax.axis_index("context")
    image_total, block_rows, model_width = tokens.shape
    micro_images = image_total // MICRO
    slot_count = ctx_count * block_rows
    head_dim = model_width // HEADS
    score_scale = head_dim ** (-0.5)
    n_experts = lax.axis_size("expert") * w_expert_in.shape[0]
    capacity = max(2, 16 * block_rows // (5 * n_experts))
    positions = jnp.arange(slot_count, dtype=jnp.int32)
    key_valid = positions[None, :] % block_rows < lengths[:, positions // block_rows]
    own_length = lax.dynamic_slice_in_dim(lengths, ctx_rank, 1, 1)
    own_valid = (jnp.arange(block_rows, dtype=jnp.int32)[None, :] < own_length).astype(jnp.float32)
    live_all = keep_mask.astype(jnp.float32) * own_valid[:, :, None]
    slot_all = slot_ranks(route_ids, n_experts)
    expert_range = jnp.arange(n_experts, dtype=jnp.int32)
    expert_in = w_expert_in[0]
    expert_down = w_expert_down[0]
    ff_width = expert_in.shape[1]
    pieces = (w_qkv, w_attn_out, w_router, norm_gains, norm_biases)
    acc_in = jnp.zeros((model_width, ff_width), jnp.float32)
    acc_down = jnp.zeros((ff_width, model_width), jnp.float32)
    outputs = []
    input_grads = []
    dense_acc = ()
    row_count = micro_images * block_rows
    buffer_rows = n_experts * micro_images * capacity
    for micro_index in range(MICRO):
        dense_full = (
            lax.all_gather(pieces[0], ("expert", "dp"), axis=0, tiled=True),
            lax.all_gather(pieces[1], ("expert", "dp"), axis=0, tiled=True),
            lax.all_gather(pieces[2], ("expert", "dp"), axis=0, tiled=True),
            lax.all_gather(pieces[3], ("expert", "dp"), axis=1, tiled=True),
            lax.all_gather(pieces[4], ("expert", "dp"), axis=1, tiled=True),
        )
        qkv_full, attn_full, router_full, gain_full, bias_full = dense_full
        gain_wide = gain_full.astype(jnp.float32)
        bias_wide = bias_full.astype(jnp.float32)
        first = micro_index * micro_images
        tokens_here = tokens[first : first + micro_images].astype(jnp.float32)
        ids_here = route_ids[first : first + micro_images]
        live_here = live_all[first : first + micro_images]
        slot_here = slot_all[first : first + micro_images]
        valid_here = own_valid[first : first + micro_images]
        keys_live = key_valid[first : first + micro_images]
        normed_one, unit_one, inverse_one = norm_rows(tokens_here, gain_wide[0], bias_wide[0])
        normed_low = normed_one.astype(jnp.bfloat16).reshape(row_count, model_width)
        projected = jnp.dot(normed_low, qkv_full, preferred_element_type=jnp.float32).astype(
            jnp.bfloat16
        )
        projected = projected.reshape(micro_images, block_rows, 3 * model_width)
        query_heads = projected[:, :, :model_width].reshape(
            micro_images, block_rows, HEADS, head_dim
        )
        kv_gathered = lax.all_gather(projected[:, :, model_width:], "context", axis=1, tiled=True)
        kv_heads = kv_gathered.reshape(micro_images, slot_count, 2, HEADS, head_dim)
        key_heads = kv_heads[:, :, 0]
        value_heads = kv_heads[:, :, 1]

        def score_block(query_side):
            raw_scores = (
                jnp.einsum(
                    "iqhd,ikhd->ihqk", query_side, key_heads, preferred_element_type=jnp.float32
                )
                * score_scale
            )
            return jnp.where(keys_live[:, None, None, :], raw_scores, -1e30)

        scores = score_block(query_heads)
        row_max = jnp.max(scores, axis=-1, keepdims=True)
        exponent = jnp.exp(scores - row_max)
        row_total = jnp.sum(exponent, axis=-1, keepdims=True)
        log_total = row_max + jnp.log(row_total)
        attn_low = (exponent / row_total).astype(jnp.bfloat16)
        attended = jnp.einsum(
            "ihqk,ikhd->iqhd", attn_low, value_heads, preferred_element_type=jnp.float32
        )
        attended_low = attended.astype(jnp.bfloat16).reshape(row_count, model_width)
        branch = jnp.dot(attended_low, attn_full, preferred_element_type=jnp.float32)
        hidden = tokens_here + branch.reshape(micro_images, block_rows, model_width)
        normed_two, unit_two, inverse_two = norm_rows(hidden, gain_wide[1], bias_wide[1])
        mixed_low = normed_two.astype(jnp.bfloat16)
        mixed_flat = mixed_low.reshape(row_count, model_width)
        logits = jnp.dot(mixed_flat, router_full, preferred_element_type=jnp.float32)
        router = jax.nn.softmax(logits, axis=-1).reshape(micro_images, block_rows, n_experts)
        choose = (ids_here[..., None] == expert_range).astype(jnp.float32)
        gate_weights = jnp.sum(choose * router[:, :, None, :], axis=-1) * live_here
        image_range = jnp.arange(micro_images, dtype=jnp.int32)[:, None, None]
        target = ((ids_here * micro_images + image_range) * capacity + slot_here).reshape(-1)
        copies = (mixed_low[:, :, None, :] * live_here[..., None].astype(jnp.bfloat16)).reshape(
            -1, model_width
        )
        send = jnp.zeros((buffer_rows, model_width), jnp.bfloat16).at[target].set(copies)
        send = send.reshape(n_experts, micro_images, capacity, model_width)
        arrived = lax.all_to_all(send, "expert", split_axis=0, concat_axis=0, tiled=True)
        lead_shape = arrived.shape[:3]
        flat_in = arrived.reshape(-1, model_width)
        inner_pre = jnp.dot(flat_in, expert_in, preferred_element_type=jnp.float32)
        active = jax.nn.gelu(inner_pre).astype(jnp.bfloat16)
        expert_out = jnp.dot(active, expert_down, preferred_element_type=jnp.float32).astype(
            jnp.bfloat16
        )
        produced = expert_out.reshape(lead_shape + (model_width,))
        inner_kept = inner_pre.reshape(lead_shape + (ff_width,))
        returned = lax.all_to_all(
            produced, "expert", split_axis=0, concat_axis=0, tiled=True
        ).reshape(buffer_rows, model_width)
        back_rows = (
            returned[target].reshape(micro_images, block_rows, 2, model_width).astype(jnp.float32)
        )
        mixture = jnp.sum(gate_weights[..., None] * back_rows, axis=2)
        outputs.append((valid_here[..., None] * (hidden + mixture)).astype(jnp.bfloat16))
        grad_out = (
            cotangent[first : first + micro_images].astype(jnp.float32) * valid_here[..., None]
        )
        grad_gate = jnp.sum(grad_out[:, :, None, :] * back_rows, axis=-1)
        grad_copies = (
            (gate_weights[..., None] * grad_out[:, :, None, :])
            .astype(jnp.bfloat16)
            .reshape(-1, model_width)
        )
        grad_send = jnp.zeros((buffer_rows, model_width), jnp.bfloat16).at[target].set(grad_copies)
        grad_send = grad_send.reshape(n_experts, micro_images, capacity, model_width)
        grad_arrived = lax.all_to_all(
            grad_send, "expert", split_axis=0, concat_axis=0, tiled=True
        ).reshape(-1, model_width)
        flat_arrived = arrived.reshape(-1, model_width)
        flat_inner = inner_kept.reshape(-1, ff_width)
        active, gelu_back = jax.vjp(jax.nn.gelu, flat_inner)
        acc_down = acc_down + jnp.einsum(
            "rf,rd->fd",
            active.astype(jnp.bfloat16),
            grad_arrived,
            preferred_element_type=jnp.float32,
        )
        grad_active = jnp.einsum(
            "rd,fd->rf", grad_arrived, expert_down, preferred_element_type=jnp.float32
        )
        grad_inner = gelu_back(grad_active)[0].astype(jnp.bfloat16)
        acc_in = acc_in + jnp.einsum(
            "rd,rf->df", flat_arrived, grad_inner, preferred_element_type=jnp.float32
        )
        grad_rows = jnp.einsum(
            "rf,df->rd", grad_inner, expert_in, preferred_element_type=jnp.float32
        ).astype(jnp.bfloat16)
        grad_rows = grad_rows.reshape(n_experts, micro_images, capacity, model_width)
        grad_back = lax.all_to_all(
            grad_rows, "expert", split_axis=0, concat_axis=0, tiled=True
        ).reshape(buffer_rows, model_width)
        copy_grads = (
            grad_back[target].reshape(micro_images, block_rows, 2, model_width).astype(jnp.float32)
        )
        grad_mixed = jnp.sum(copy_grads * live_here[..., None], axis=2)
        grad_probs = jnp.sum(choose * (grad_gate * live_here)[..., None], axis=2)
        grad_logits = router * (grad_probs - jnp.sum(router * grad_probs, axis=-1, keepdims=True))
        grad_logits = grad_logits.reshape(row_count, n_experts)
        router_wide = router_full.astype(jnp.float32)
        grad_mixed = grad_mixed + jnp.einsum(
            "re,de->rd", grad_logits, router_wide, precision=precise
        ).reshape(micro_images, block_rows, model_width)
        grad_route = jnp.einsum(
            "rd,re->de", mixed_flat.astype(jnp.float32), grad_logits, precision=precise
        )
        gain_grad_two = jnp.sum(grad_mixed * unit_two, axis=(0, 1))
        bias_grad_two = jnp.sum(grad_mixed, axis=(0, 1))
        grad_hidden = grad_out + norm_back(grad_mixed, unit_two, inverse_two, gain_wide[1])
        grad_branch = grad_hidden.astype(jnp.bfloat16).reshape(row_count, model_width)
        grad_attn = jnp.einsum(
            "rd,re->de", attended_low, grad_branch, preferred_element_type=jnp.float32
        )
        grad_attended = jnp.einsum(
            "re,de->rd", grad_branch, attn_full, preferred_element_type=jnp.float32
        ).astype(jnp.bfloat16)
        grad_heads = grad_attended.reshape(micro_images, block_rows, HEADS, head_dim)
        attn_probs = jnp.exp(score_block(query_heads) - log_total)
        grad_weights = jnp.einsum(
            "iqhd,ikhd->ihqk", grad_heads, value_heads, preferred_element_type=jnp.float32
        )
        row_dot = jnp.sum(attn_probs * grad_weights, axis=-1, keepdims=True)
        grad_scores = (attn_probs * (grad_weights - row_dot)).astype(jnp.bfloat16)
        grad_query = (
            jnp.einsum(
                "ihqk,ikhd->iqhd", grad_scores, key_heads, preferred_element_type=jnp.float32
            )
            * score_scale
        )
        grad_key = (
            jnp.einsum(
                "ihqk,iqhd->ikhd", grad_scores, query_heads, preferred_element_type=jnp.float32
            )
            * score_scale
        )
        grad_value = jnp.einsum(
            "ihqk,iqhd->ikhd",
            attn_probs.astype(jnp.bfloat16),
            grad_heads,
            preferred_element_type=jnp.float32,
        )
        kv_terms = jnp.concatenate(
            [
                grad_key.reshape(micro_images, slot_count, model_width),
                grad_value.reshape(micro_images, slot_count, model_width),
            ],
            axis=2,
        )
        kv_summed = lax.psum_scatter(
            kv_terms.astype(jnp.bfloat16), "context", scatter_dimension=1, tiled=True
        ).astype(jnp.float32)
        grad_projected = jnp.concatenate(
            [grad_query.reshape(micro_images, block_rows, model_width), kv_summed], axis=2
        )
        grad_projected = grad_projected.astype(jnp.bfloat16).reshape(row_count, 3 * model_width)
        grad_qkv = jnp.einsum(
            "rd,re->de", normed_low, grad_projected, preferred_element_type=jnp.float32
        )
        grad_normed = jnp.einsum(
            "re,de->rd", grad_projected, qkv_full, preferred_element_type=jnp.float32
        )
        grad_normed = grad_normed.reshape(micro_images, block_rows, model_width)
        gain_grad_one = jnp.sum(grad_normed * unit_one, axis=(0, 1))
        bias_grad_one = jnp.sum(grad_normed, axis=(0, 1))
        input_grads.append(
            grad_hidden + norm_back(grad_normed, unit_one, inverse_one, gain_wide[0])
        )
        local_dense = (
            grad_qkv,
            grad_attn,
            grad_route,
            jnp.stack([gain_grad_one, gain_grad_two]),
            jnp.stack([bias_grad_one, bias_grad_two]),
        )
        local_dense = (
            lax.psum_scatter(local_dense[0], ("expert", "dp"), scatter_dimension=0, tiled=True),
            lax.psum_scatter(local_dense[1], ("expert", "dp"), scatter_dimension=0, tiled=True),
            lax.psum_scatter(local_dense[2], ("expert", "dp"), scatter_dimension=0, tiled=True),
            lax.psum_scatter(local_dense[3], ("expert", "dp"), scatter_dimension=1, tiled=True),
            lax.psum_scatter(local_dense[4], ("expert", "dp"), scatter_dimension=1, tiled=True),
        )
        if micro_index == 0:
            dense_acc = local_dense
        else:
            dense_acc = tuple((left + right for left, right in zip(dense_acc, local_dense)))
    dense_sums = jax.tree.map(
        lambda part: part.astype(jnp.float32), lax.psum(as_sent(dense_acc), "context")
    )
    expert_sums = (
        lax.psum_scatter(
            acc_in[None].astype(jnp.bfloat16), ("context", "dp"), scatter_dimension=2, tiled=True
        ).astype(jnp.float32),
        lax.psum_scatter(
            acc_down[None].astype(jnp.bfloat16), ("context", "dp"), scatter_dimension=1, tiled=True
        ).astype(jnp.float32),
    )
    return (
        jnp.concatenate(outputs, axis=0),
        jnp.concatenate(input_grads, axis=0),
        dense_sums[0],
        dense_sums[1],
        dense_sums[2],
        dense_sums[3],
        dense_sums[4],
        expert_sums[0],
        expert_sums[1],
    )


def solution(mesh):
    placed = (
        P(("expert", "dp"), "context", None),
        P(("expert", "dp"), None),
        P(("expert", "dp"), "context", None),
        P(("expert", "dp"), "context", None),
        P(("expert", "dp"), None),
        P(("expert", "dp"), None),
        P(("expert", "dp"), None),
        P(None, ("expert", "dp")),
        P(None, ("expert", "dp")),
        P("expert", None, None),
        P("expert", None, None),
        P(("expert", "dp"), "context", None),
    )
    return jax.shard_map(
        per_device,
        mesh=mesh,
        in_specs=placed,
        out_specs=(
            P(("expert", "dp"), "context", None),
            P(("expert", "dp"), "context", None),
            P(("expert", "dp"), None),
            P(("expert", "dp"), None),
            P(("expert", "dp"), None),
            P(None, ("expert", "dp")),
            P(None, ("expert", "dp")),
            P("expert", None, ("context", "dp")),
            P("expert", ("context", "dp"), None),
        ),
        check_vma=False,
    )
```

profile of v0, /device:TPU:0, one launch (start us, length us, event | category | flops | bytes accessed | tf_op | source)
XLA Modules:
  0.0 1060.4 jit_solution(415507879520559526)
XLA Ops:
  8.0 22.3 %all-gather.1 = bf16[8,96,2]{1,2,0:T(2,128)(2,1)S(1)} all-gather(bf16[1,96,2]{1,2,0:T(2,128)(2,1)} %bitcast.413), channel_id=1, replica_groups=mesh['expert'=4,'context'=4,'dp'=2] {'expert','dp'}, dimensions={0}, use_global_device_ids=true | all-gather | bytes 3456 | tf_op jit(solution)/shard_map/all_gather | solution.py:92
  30.4 16.4 %all-gather = bf16[8,96,2]{1,2,0:T(2,128)(2,1)S(1)} all-gather(bf16[1,96,2]{1,2,0:T(2,128)(2,1)} %bitcast.414), channel_id=1, replica_groups=mesh['expert'=4,'context'=4,'dp'=2] {'expert','dp'}, dimensions={0}, use_global_device_ids=true | all-gather | bytes 3456 | tf_op jit(solution)/shard_map/all_gather | solution.py:91
  49.6 28.6 %all-gather.8.cloned.1.call-done = bf16[768,2304]{1,0:T(8,128)(2,1)} async-done(((bf16[96,2304]{1,0:T(8,128)(2,1)}), bf16[768,2304]{1,0:T(8,128)(2,1)}) %all-gather.8.cloned.1.call-update) | async-done | bytes 3538960 | tf_op jit(solution)/shard_map/all_gather | solution.py:88
  95.6 6.9 all-gather.10.cloned.1.call-done
  111.0 34.9 %all-gather.12.cloned.1.call-done = bf16[768,768]{1,0:T(8,128)(2,1)} async-done(((bf16[96,768]{1,0:T(8,128)(2,1)}), bf16[768,768]{1,0:T(8,128)(2,1)}) %all-gather.12.cloned.1.call-update) | async-done | bytes 1179664 | tf_op jit(solution)/shard_map/all_gather | solution.py:89
  148.0 20.5 %all-gather.14.cloned.1.call-done = bf16[1,640,1536]{2,1,0:T(8,128)(2,1)} async-done(((bf16[1,160,1536]{2,1,0:T(8,128)(2,1)}), bf16[1,640,1536]{2,1,0:T(8,128)(2,1)}) %all-gather.14.cloned.1.call-update) | async-done | bytes 1966096 | tf_op jit(solution)/shard_map/all_gather | solution.py:113
  184.5 4.6 all-to-all-start
  197.1 21.0 %all-gather.2 = bf16[8,96,4]{1,2,0:T(4,128)(2,1)S(1)} all-gather(bf16[1,96,4]{1,2,0:T(4,128)(2,1)S(1)} %bitcast.412), channel_id=1, replica_groups=mesh['expert'=4,'context'=4,'dp'=2] {'expert','dp'}, dimensions={0}, use_global_device_ids=true | all-gather | bytes 6912 | tf_op jit(solution)/shard_map/all_gather | solution.py:90
  225.8 4.7 fusion.28
  233.2 6.9 fusion.62
  242.6 3.9 all-to-all-start.1
  246.5 4.5 fusion.26
  253.6 6.9 fusion.65
  260.6 3.6 all-to-all-done.1
  277.0 9.5 all-to-all-done.3
  295.1 3.5 scatter_custom_fusion.3
  298.6 4.4 all-to-all-start.6
  309.6 13.1 %all-to-all-done.6 = bf16[4,1,128,768]{3,2,1,0:T(8,128)(2,1)} async-done(((bf16[4,1,128,768]{3,2,1,0:T(8,128)(2,1)}), bf16[4,1,128,768]{3,2,1,0:T(8,128)(2,1)}, u32[]{:S(2)}, u32[]{:S(2)}) %all-to-all-start.6) | async-done | bytes 786464 | tf_op jit(solution)/shard_map/all_to_all | solution.py:182
  322.7 3.5 all-to-all-start.4
  326.2 8.7 fusion.13
  336.6 3.5 fusion.59
  340.1 5.7 all-to-all-done.4
  345.7 3.7 all-to-all-start.7
  349.5 8.6 fusion.6
  359.7 5.9 fusion.56
  414.2 3.5 fusion.53
  417.7 4.5 multiply_reduce_fusion
  425.4 8.9 copy.163
  434.4 3.8 copy.182
  443.0 5.1 multiply_reduce_fusion.1
  452.4 9.0 copy.161
  461.5 3.9 copy.183
  481.5 20.3 %reduce-scatter.28.cloned.1.call-done = bf16[160,1536]{1,0:T(8,128)(2,1)} async-done(((bf16[640,1536]{1,0:T(8,128)(2,1)}), bf16[160,1536]{1,0:T(8,128)(2,1)}) %reduce-scatter.28.cloned.1.call-update) | async-done | bytes 491536
  505.5 4.1 convolution_add_fusion
  509.9 8.6 fusion.186
  524.4 7.6 fusion.30
  532.1 20.4 %copy.165 = bf16[1,768,3072]{1,0,2:T(2,128)(2,1)} copy(bf16[1,768,3072]{2,1,0:T(8,128)(2,1)} %fusion.30) | data formatting | bytes 9437184
  552.4 6.7 copy.181
  559.5 5.4 fusion.173
  564.9 8.9 fusion.31
  575.9 62.8 %reduce-scatter.26.cloned.1.call-done = f32[96,768]{1,0:T(8,128)} async-done(((f32[768,768]{1,0:T(8,128)}), f32[96,768]{1,0:T(8,128)}) %reduce-scatter.26.cloned.1.call-update) | async-done | bytes 294928 | tf_op jit(solution)/shard_map/reduce_scatter | solution.py:292
  640.3 130.2 %reduce-scatter.24.cloned.1.call-done = f32[96,2304]{1,0:T(8,128)} async-done(((f32[768,2304]{1,0:T(8,128)}), f32[96,2304]{1,0:T(8,128)}) %reduce-scatter.24.cloned.1.call-update) | async-done | bytes 884752 | tf_op jit(solution)/shard_map/reduce_scatter | solution.py:291
  773.9 61.1 %reduce-scatter.36.cloned.1.call-done = f32[96,2]{1,0:T(8,128)} async-done(((f32[768,2]{1,0:T(8,128)}), f32[96,2]{1,0:T(8,128)}) %reduce-scatter.36.cloned.1.call-update) | async-done | bytes 784
  835.9 63.2 %reduce-scatter.38.cloned.1.call-done = f32[96,2]{1,0:T(8,128)} async-done(((f32[768,2]{1,0:T(8,128)}), f32[96,2]{1,0:T(8,128)}) %reduce-scatter.38.cloned.1.call-update) | async-done | bytes 784
  900.0 5.7 all-reduce.1
  907.4 48.4 %reduce-scatter.32.cloned.1.call-done = bf16[384,768]{1,0:T(8,128)(2,1)} async-done(((bf16[3072,768]{1,0:T(8,128)(2,1)}), bf16[384,768]{1,0:T(8,128)(2,1)}) %reduce-scatter.32.cloned.1.call-update) | async-done | bytes 589840
  960.2 52.9 %reduce-scatter.22.cloned.1.call-done = bf16[1,384,768]{2,1,0:T(8,128)(2,1)} async-done(((bf16[1,3072,768]{2,1,0:T(8,128)(2,1)}), bf16[1,384,768]{2,1,0:T(8,128)(2,1)}) %reduce-scatter.22.cloned.1.call-update) | async-done | bytes 589840 | tf_op jit(solution)/shard_map/reduce_scatter | solution.py:308
  1015.3 34.5 %all-reduce.5.cloned.1.call-done = (bf16[96,2304]{1,0:T(8,128)(2,1)}, bf16[96,768]{1,0:T(8,128)(2,1)}) async-done(((bf16[96,2304]{1,0:T(8,128)(2,1)}, bf16[96,768]{1,0:T(8,128)(2,1)}), (bf16[96,2304]{1,0:T(8,128)(2,1)}, bf16[96,768]{1,0:T(8,128)(2,1)})) %all-reduce.5.cloned.1.call-update) | async-done | bytes 589840 | tf_op jit(solution)/shard_map/psum | solution.py:302
  (443 shorter events, 208.8 us)
Async XLA Ops:
  7.2 83.0 %copy-start.4 = (bf16[2,160,768]{2,1,0:T(8,128)(2,1)S(1)}, bf16[2,160,768]{2,1,0:T(8,128)(2,1)}, u32[]{:S(2)}) copy-start(bf16[2,160,768]{2,1,0:T(8,128)(2,1)} %param.12) | copy-start | bytes 1474564
  7.2 75.6 %copy-start.90 = (s32[2,160,2]{1,2,0:T(2,128)S(1)}, s32[2,160,2]{1,2,0:T(2,128)}, u32[]{:S(2)}) copy-start(s32[2,160,2]{1,2,0:T(2,128)} %param.14) | copy-start | bytes 7684
  7.2 78.6 %copy-start.88 = (s32[2,4]{1,0:T(2,128)S(1)}, s32[2,4]{1,0:T(2,128)}, u32[]{:S(2)}) copy-start(s32[2,4]{1,0:T(2,128)} %param.13) | copy-start | bytes 100
  7.2 80.3 %copy-start.89 = (s32[2,160,2]{1,2,0:T(2,128)S(1)}, s32[2,160,2]{1,2,0:T(2,128)}, u32[]{:S(2)}) copy-start(s32[2,160,2]{1,2,0:T(2,128)} %param.15) | copy-start | bytes 7684
  7.2 71.0 %all-gather.8.cloned.1.call-start = ((), (), s32[]{:S(2)}) async-start(), calls=%async_computation.17 | async-start | bytes 3981312 | tf_op jit(solution)/shard_map/all_gather | solution.py:88
  8.0 94.6 %all-gather.10.cloned.1.call-start = ((), (), s32[]{:S(2)}) async-start(), calls=%async_computation.18 | async-start | bytes 2457600 | tf_op jit(solution)/shard_map/all_gather | solution.py:113
  48.2 34.9 %copy-start.48 = (f32[160]{0:T(256)}, f32[160]{0:T(256)S(1)}, u32[]{:S(2)}) copy-start(f32[160]{0:T(256)S(1)} %get-tuple-element.97) | copy-start | bytes 1924
  48.2 44.8 %copy-start.52 = (f32[160]{0:T(256)}, f32[160]{0:T(256)S(1)}, u32[]{:S(2)}) copy-start(f32[160]{0:T(256)S(1)} %get-tuple-element.96) | copy-start | bytes 1924
  49.6 33.5 %copy-start.50 = (f32[160]{0:T(256)}, f32[160]{0:T(256)S(1)}, u32[]{:S(2)}) copy-start(f32[160]{0:T(256)S(1)} %add_rsqrt_fusion.3) | copy-start | bytes 1924
  82.0 63.8 %all-gather.12.cloned.1.call-start = ((), (), s32[]{:S(2)}) async-start(), calls=%async_computation.19 | async-start | bytes 1327104 | tf_op jit(solution)/shard_map/all_gather | solution.py:89
  82.7 85.7 %all-gather.14.cloned.1.call-start = ((), (), s32[]{:S(2)}) async-start(), calls=%async_computation.20 | async-start | bytes 2457600 | tf_op jit(solution)/shard_map/all_gather | solution.py:113
  93.9 125.0 %copy-start.84 = (s32[320]{0:T(512)}, s32[320]{0:T(512)S(1)}, u32[]{:S(2)}) copy-start(s32[320]{0:T(512)S(1)} %fusion.162) | copy-start | bytes 3844
  147.7 31.1 %copy-start.54 = (f32[160]{0:T(256)}, f32[160]{0:T(256)S(1)}, u32[]{:S(2)}) copy-start(f32[160]{0:T(256)S(1)} %broadcast_multiply_fusion.10) | copy-start | bytes 1924
  147.9 30.9 %copy-start.71 = (f32[160]{0:T(256)}, f32[160]{0:T(256)S(1)}, u32[]{:S(2)}) copy-start(f32[160]{0:T(256)S(1)} %add_rsqrt_fusion.2) | copy-start | bytes 1924
  179.1 39.2 %copy-start.39 = (s32[160,2]{1,0:T(8,128)S(1)}, s32[160,2]{1,0:T(8,128)}, u32[]{:S(2)}) copy-start(s32[160,2]{1,0:T(8,128)} %get-tuple-element.59) | copy-start | bytes 3844
  184.5 37.9 %all-to-all-start = ((bf16[4,1,128,768]{3,2,1,0:T(8,128)(2,1)}), bf16[4,1,128,768]{3,2,1,0:T(8,128)(2,1)}, u32[]{:S(2)}, u32[]{:S(2)}) async-start(bf16[4,1,128,768]{3,2,1,0:T(8,128)(2,1)} %bitcast.383), calls=%async_computation | async-start | bytes 1572864 | tf_op jit(solution)/shard_map/all_to_all | solution.py:153
  189.5 41.0 %copy-start.80 = (f32[1,160]{1,0:T(1,128)}, f32[1,160]{1,0:T(1,128)S(1)}, u32[]{:S(2)}) copy-start(f32[1,160]{1,0:T(1,128)S(1)} %get-tuple-element.76) | copy-start | bytes 1924
  191.5 39.0 %copy-start.18 = (f32[160,768]{1,0:T(8,128)}, f32[160,768]{1,0:T(8,128)S(1)}, u32[]{:S(2)}) copy-start(f32[160,768]{1,0:T(8,128)S(1)} %get-tuple-element.55) | copy-start | bytes 1474564
  218.9 51.1 %copy-start.64 = (s32[1024]{0:T(1024)}, s32[1024]{0:T(1024)S(1)}, u32[]{:S(2)}) copy-start(s32[1024]{0:T(1024)S(1)} %pad_clamp_fusion.1) | copy-start | bytes 12292
  218.9 67.6 %copy-start.65 = (s32[1024]{0:T(1024)}, s32[1024]{0:T(1024)S(1)}, u32[]{:S(2)}) copy-start(s32[1024]{0:T(1024)S(1)} %pad_clamp_fusion) | copy-start | bytes 12292
  222.3 20.3 %all-to-all-start.2 = ((bf16[4,1,128,768]{3,2,1,0:T(8,128)(2,1)}), bf16[4,1,128,768]{3,2,1,0:T(8,128)(2,1)S(1)}, u32[]{:S(2)}, u32[]{:S(2)}) async-start(bf16[4,1,128,768]{3,2,1,0:T(8,128)(2,1)} %bitcast.384), calls=%async_computation.2 | async-start | bytes 1572864 | tf_op jit(solution)/shard_map/all_to_all | solution.py:153
  242.6 21.6 %all-to-all-start.1 = ((bf16[4,1,128,768]{3,2,1,0:T(8,128)(2,1)}), bf16[4,1,128,768]{3,2,1,0:T(8,128)(2,1)S(1)}, u32[]{:S(2)}, u32[]{:S(2)}) async-start(bf16[4,1,128,768]{3,2,1,0:T(8,128)(2,1)} %bitcast.399), calls=%async_computation.1 | async-start | bytes 1572864 | tf_op jit(solution)/shard_map/all_to_all | solution.py:163
  264.2 22.3 %all-to-all-start.3 = ((bf16[4,1,128,768]{3,2,1,0:T(8,128)(2,1)}), bf16[4,1,128,768]{3,2,1,0:T(8,128)(2,1)S(1)}, u32[]{:S(2)}, u32[]{:S(2)}) async-start(bf16[4,1,128,768]{3,2,1,0:T(8,128)(2,1)} %bitcast.398), calls=%async_computation.3 | async-start | bytes 1572864 | tf_op jit(solution)/shard_map/all_to_all | solution.py:163
  269.1 20.0 %copy-start.47 = (f32[160,4]{0,1:T(4,128)}, f32[160,4]{0,1:T(4,128)S(1)}, u32[]{:S(2)}) copy-start(f32[160,4]{0,1:T(4,128)S(1)} %get-tuple-element.89) | copy-start | bytes 7684
  294.8 27.9 %copy-start.58 = (f32[1,160,2]{1,2,0:T(2,128)}, f32[1,160,2]{1,2,0:T(2,128)S(1)}, u32[]{:S(2)}) copy-start(f32[1,160,2]{1,2,0:T(2,128)S(1)} %get-tuple-element.72) | copy-start | bytes 3844
  294.8 27.9 %copy-start.59 = (f32[1,160,2]{1,2,0:T(2,128)}, f32[1,160,2]{1,2,0:T(2,128)S(1)}, u32[]{:S(2)}) copy-start(f32[1,160,2]{1,2,0:T(2,128)S(1)} %get-tuple-element.73) | copy-start | bytes 3844
  298.6 24.0 %all-to-all-start.6 = ((bf16[4,1,128,768]{3,2,1,0:T(8,128)(2,1)}), bf16[4,1,128,768]{3,2,1,0:T(8,128)(2,1)}, u32[]{:S(2)}, u32[]{:S(2)}) async-start(bf16[4,1,128,768]{3,2,1,0:T(8,128)(2,1)} %bitcast.81), calls=%async_computation.6 | async-start | bytes 1572864 | tf_op jit(solution)/shard_map/all_to_all | solution.py:182
  306.4 30.1 %slice-start.4 = ((s8[4718592]{0:T(1024)(128)(4,1)}), s8[524288]{0:T(1024)(128)(4,1)S(1)}, s32[]{:S(2)}) async-start(s8[4718592]{0:T(1024)(128)(4,1)} %bitcast.350), calls=%async_computation.35 | async-start | bytes 1048576
  322.7 23.1 %all-to-all-start.4 = ((bf16[4,1,128,768]{3,2,1,0:T(8,128)(2,1)}), bf16[4,1,128,768]{3,2,1,0:T(8,128)(2,1)S(1)}, u32[]{:S(2)}, u32[]{:S(2)}) async-start(bf16[4,1,128,768]{3,2,1,0:T(8,128)(2,1)} %bitcast.382), calls=%async_computation.4 | async-start | bytes 1572864 | tf_op jit(solution)/shard_map/all_to_all | solution.py:182
  345.7 23.3 %all-to-all-start.7 = ((bf16[4,1,128,768]{3,2,1,0:T(8,128)(2,1)}), bf16[4,1,128,768]{3,2,1,0:T(8,128)(2,1)S(1)}, u32[]{:S(2)}, u32[]{:S(2)}) async-start(bf16[4,1,128,768]{3,2,1,0:T(8,128)(2,1)} %bitcast.400), calls=%async_computation.7 | async-start | bytes 1572864 | tf_op jit(solution)/shard_map/all_to_all | solution.py:205
  369.0 29.4 %all-to-all-start.5 = ((bf16[4,1,128,768]{3,2,1,0:T(8,128)(2,1)}), bf16[4,1,128,768]{3,2,1,0:T(8,128)(2,1)S(1)}, u32[]{:S(2)}, u32[]{:S(2)}) async-start(bf16[4,1,128,768]{3,2,1,0:T(8,128)(2,1)} %bitcast.397), calls=%async_computation.5 | async-start | bytes 1572864 | tf_op jit(solution)/shard_map/all_to_all | solution.py:205
  372.5 106.5 %reduce-scatter.30.cloned.1.call-start = ((), (), s32[]{:S(2)}) async-start(), calls=%async_computation.25 | async-start | bytes 2457600
  438.2 63.5 %reduce-scatter.28.cloned.1.call-start = ((), (), s32[]{:S(2)}) async-start(), calls=%async_computation.24 | async-start | bytes 2457600
  465.4 108.5 %reduce-scatter.34.cloned.1.call-start = ((), (), s32[]{:S(2)}) async-start(), calls=%async_computation.27 | async-start | bytes 442368
  467.9 170.8 %reduce-scatter.26.cloned.1.call-start = ((), (), s32[]{:S(2)}) async-start(), calls=%async_computation.23 | async-start | bytes 2654208 | tf_op jit(solution)/shard_map/reduce_scatter | solution.py:292
  472.5 298.0 %reduce-scatter.24.cloned.1.call-start = ((), (), s32[]{:S(2)}) async-start(), calls=%async_computation.22 | async-start | bytes 7962624 | tf_op jit(solution)/shard_map/reduce_scatter | solution.py:291
  475.6 28.5 %copy-start.5 = (bf16[2,160,768]{2,1,0:T(8,128)(2,1)S(1)}, bf16[2,160,768]{2,1,0:T(8,128)(2,1)}, u32[]{:S(2)}) copy-start(bf16[2,160,768]{2,1,0:T(8,128)(2,1)} %param.12) | copy-start | bytes 1474564
  475.6 28.5 %copy-start.49 = (f32[160]{0:T(256)S(1)}, f32[160]{0:T(256)}, u32[]{:S(2)}) copy-start(f32[160]{0:T(256)} %copy-done.48) | copy-start | bytes 1924
  475.6 28.5 %copy-start.51 = (f32[160]{0:T(256)S(1)}, f32[160]{0:T(256)}, u32[]{:S(2)}) copy-start(f32[160]{0:T(256)} %copy-done.50) | copy-start | bytes 1924
  479.0 26.4 %copy-start.30 = (bf16[12,64,160]{2,1,0:T(8,128)(2,1)}, bf16[12,64,160]{2,1,0:T(8,128)(2,1)S(1)}, u32[]{:S(2)}) copy-start(bf16[12,64,160]{2,1,0:T(8,128)(2,1)S(1)} %fusion.70) | copy-start | bytes 737284
  509.6 325.4 %reduce-scatter.36.cloned.1.call-start = ((), (), s32[]{:S(2)}) async-start(), calls=%async_computation.28 | async-start | bytes 442368
  523.3 375.8 %reduce-scatter.38.cloned.1.call-start = ((), (), s32[]{:S(2)}) async-start(), calls=%async_computation.29 | async-start | bytes 442368
  524.4 431.4 %reduce-scatter.32.cloned.1.call-start = ((), (), s32[]{:S(2)}) async-start(), calls=%async_computation.26 | async-start | bytes 5308416
  559.2 454.0 %reduce-scatter.22.cloned.1.call-start = ((), (), s32[]{:S(2)}) async-start(), calls=%async_computation.21 | async-start | bytes 5308416 | tf_op jit(solution)/shard_map/reduce_scatter | solution.py:308
  573.9 198.7 %copy-start.12 = (f32[1,160,768]{2,1,0:T(8,128)S(1)}, f32[1,160,768]{2,1,0:T(8,128)}, u32[]{:S(2)}) copy-start(f32[1,160,768]{2,1,0:T(8,128)} %get-tuple-element.50) | copy-start | bytes 1474564
  573.9 198.7 %copy-start.14 = (f32[1,160,768]{2,1,0:T(8,128)S(1)}, f32[1,160,768]{2,1,0:T(8,128)}, u32[]{:S(2)}) copy-start(f32[1,160,768]{2,1,0:T(8,128)} %copy-done.13) | copy-start | bytes 1474564
  573.9 198.7 %copy-start.70 = (f32[160]{0:T(256)S(1)}, f32[160]{0:T(256)}, u32[]{:S(2)}) copy-start(f32[160]{0:T(256)} %copy-done.68) | copy-start | bytes 1924
  573.9 475.9 %all-reduce.5.cloned.1.call-start = ((), (), s32[]{:S(2)}) async-start(), calls=%async_computation.30 | async-start | bytes 1179648 | tf_op jit(solution)/shard_map/psum | solution.py:302
  (76 other events, 494.4 us)
Sparse Core Ops, SparseCore 0:
  10.2 67.9 all-gather.7
  82.1 20.3 all-gather.9
  104.7 41.0 all-gather.11
  147.8 20.6 all-gather.13
  438.4 30.1 reduce-scatter.29
  471.1 30.6 reduce-scatter.27
  505.6 61.4 reduce-scatter.33
  570.6 68.0 reduce-scatter.25
  642.4 128.0 reduce-scatter.23
  774.5 60.4 reduce-scatter.35
  838.6 60.4 reduce-scatter.37
  902.8 52.9 reduce-scatter.31
  959.2 53.8 reduce-scatter.21
  1016.2 33.5 all-reduce.4
where the time goes:
time: 1070 us; the launch traced here: 1060 us
  waiting for transfers between devices  604 us (56%)
  matrix products  140 us (13%)
  local copies, waits for them, and re-layouts  137 us (13%)
  other arithmetic  66.2 us (6%)
  blocking collectives  65.4 us (6%)
  starting transfers between devices  31.8 us (3%)
  between operations  16.2 us (2%)
    unnamed x20, waiting for transfers between devices  195 us
    reduce_scatter x1, waiting for transfers between devices, per_device(): lax.psum_scatter(local_dense[0], ('expert', 'dp'), scatter_dimension=0, t...  130 us
    unnamed x225, local copies, waits for them, and re-layouts  77.4 us
    reduce_scatter x1, waiting for transfers between devices, per_device(): lax.psum_scatter(local_dense[1], ('expert', 'dp'), scatter_dimension=0, t...  62.8 us
    reduce_scatter x1, waiting for transfers between devices, per_device(): lax.psum_scatter(acc_down[None].astype(jnp.bfloat16), ('context', 'dp'),...  52.9 us
    all_gather x1, waiting for transfers between devices, per_device(): lax.all_gather(pieces[1], ('expert', 'dp'), axis=0, tiled=True)  34.9 us
    psum x1, waiting for transfers between devices, per_device(): lax.psum(as_sent(dense_acc), 'context')  34.5 us
    all_gather x1, waiting for transfers between devices, per_device(): lax.all_gather(pieces[0], ('expert', 'dp'), axis=0, tiled=True)  28.6 us
  transfers between devices with their start and end apart: 22, of which 18 were waited for; matrix products, arithmetic and copies ran while one was open for 24% of the time, Pallas kernels for 0%

commit v1 on v0

v1 whole, which is shorter than its diff:
```python
import functools
import itertools
import types

import jax
import jax.numpy as jnp
from jax import lax
from jax.experimental import pallas as pl
from jax.experimental.pallas import tpu as pltpu
from jax.sharding import PartitionSpec as P

HEADS = 12
EPS = 1e-06
F32 = jnp.float32
BF16 = jnp.bfloat16
MESH = pl.DeviceIdType.MESH
NN = (((1,), (0,)), ((), ()))
NT = (((1,), (1,)), ((), ()))
TN = (((0,), (0,)), ((), ()))
VMEM_LIMIT = 60 * 2**20
LOGIT_LANE = 4


def mm(left, right, dims=NN):
    return lax.dot_general(left, right, dims, preferred_element_type=F32)


def lane_of(shape):
    return lax.broadcasted_iota(jnp.int32, shape, 1)


def row_of(shape):
    return lax.broadcasted_iota(jnp.int32, shape, 0)


class Links:
    def __init__(self, send, recv):
        self.send, self.recv, self.ids = send, recv, itertools.count()

    def new(self):
        return next(self.ids)

    def make(self, at, src, dst, device):
        return pltpu.make_async_remote_copy(
            src_ref=src,
            dst_ref=dst,
            send_sem=self.send.at[at],
            recv_sem=self.recv.at[at],
            device_id=device,
            device_id_type=MESH,
        )


def greet(devices):
    barrier = pltpu.get_barrier_semaphore()
    for device in devices:
        pl.semaphore_signal(barrier, inc=1, device_id=device, device_id_type=MESH)
    pl.semaphore_wait(barrier, len(devices))


def normalize(values):
    centred = values - jnp.mean(values, axis=-1, keepdims=True)
    inverse = lax.rsqrt(jnp.mean(centred * centred, axis=-1, keepdims=True) + EPS)
    return centred * inverse, inverse


def normalize_back(grad_out, unit_rows, inverse, gain):
    scaled = grad_out * gain
    centre_term = jnp.mean(scaled, axis=-1, keepdims=True)
    slope_term = jnp.mean(scaled * unit_rows, axis=-1, keepdims=True)
    return inverse * (scaled - centre_term - unit_rows * slope_term)


def to_column(row):
    size = row.shape[1]
    eye = row_of((size, size)) == lane_of((size, size))
    return jnp.sum(jnp.where(eye, row, 0.0), axis=1, keepdims=True)


def to_row(column):
    size = column.shape[0]
    eye = row_of((size, size)) == lane_of((size, size))
    return jnp.sum(jnp.where(eye, column, 0.0), axis=0, keepdims=True)


def key_bias(c, len_ref, image):
    at = row_of((c.S, 1))
    bias = jnp.full((c.S, 1), -1e30, F32)
    for block in range(c.C):
        start = block * c.B
        inside = jnp.logical_and(at >= start, at < start + len_ref[image, block])
        bias = jnp.where(inside, 0.0, bias)
    return bias


def two_heads(pair):
    first = lane_of(pair.shape) < pair.shape[1] // 2
    zero = jnp.zeros_like(pair)
    return jnp.concatenate([jnp.where(first, pair, zero), jnp.where(first, zero, pair)], axis=0)


def one_pair(stacked):
    half = stacked.shape[0] // 2
    first = lane_of((half, stacked.shape[1])) < stacked.shape[1] // 2
    return jnp.where(first, stacked[:half], stacked[half:])


def front_kernel(c, *refs):
    refs = list(refs)
    take = lambda count: [refs.pop(0) for _ in range(count)]
    len_ref, tok_ref, route_ref, keep_ref, cot_ref = take(5)
    if c.gather:
        wqkv_ref, wout_ref, small_ref = take(3)
        w_ref, vec_ref = take(2)
    else:
        w_ref, vec_ref = take(2)
    q_ref, kv_ref, lse_ref, att_ref, hid_ref, mix_ref, meta_ref, router_ref = take(8)
    send_ref, gsend_ref, dyarr_ref = take(3)
    smalls, dysend, norm_ref, ssem, rsem = take(5)
    links = Links(ssem, rsem)
    z, x, y = lax.axis_index("expert"), lax.axis_index("context"), lax.axis_index("dp")
    core = lax.rem(x, 2)
    shard = z * c.Y + y
    core_dev, far_dev, y_dev = (z, x ^ 1, y), (z, x ^ 2, y), (z, x, 1 - y)
    plane = [(lax.div(shard ^ k, c.Y), x, lax.rem(shard ^ k, c.Y)) for k in range(1, c.E * c.Y)]
    experts = [(z ^ k, x, y) for k in range(1, c.E)]
    greet([core_dev, far_dev] + (plane if c.gather else experts))
    ends = []

    def go(at, src, dst, device):
        copy = links.make(at, src, dst, device)
        copy.start()
        ends.append(copy)

    if c.gather:
        small_ids = [links.new() for _ in plane]
        smalls[shard] = small_ref[...]
        for at, device in zip(small_ids, plane):
            go(at, smalls.at[shard], smalls.at[shard], device)

        def rows_of(z_at, y_at):
            return pl.ds(pl.multiple_of((z_at * c.Y + y_at) * c.sh, 32), c.sh)

        own_rows = rows_of(z, y)
        for part in range(3):
            w_ref[part, own_rows, :] = wqkv_ref[:, part * c.D : (part + 1) * c.D]
        w_ref[3, own_rows, :] = wout_ref[...]

        def unit(z_at, y_at):
            return w_ref.at[pl.ds(2 * core, 2), rows_of(z_at, y_at), :]

        def other_unit(z_at, y_at):
            return w_ref.at[pl.ds(2 - 2 * core, 2), rows_of(z_at, y_at), :]

        up = [links.new() for _ in range(c.E)]
        down = [links.new() for _ in range(c.E)]
        y_up = [links.new() for _ in range(c.E)]
        y_down = [links.new() for _ in range(c.E)]
        core_up = [[links.new() for _ in range(c.E)] for _ in range(2)]
        core_down = [[links.new() for _ in range(c.E)] for _ in range(2)]
        above, below = (lax.rem(z + 1, c.E), x, y), (lax.rem(z + c.E - 1, c.E), x, y)

        def copy_of(at, z_at, y_at, device):
            return links.make(at, unit(z_at, y_at), unit(z_at, y_at), device)

        pending = []

        def send_if(condition, at, z_at, y_at, device):
            pl.when(condition)(lambda: copy_of(at, z_at, y_at, device).start())
            pending.append((condition, at, z_at, y_at, device))

        always = z >= 0
        send_if(z < c.E - 1, up[1], z, y, above)
        send_if(z > 0, down[1], z, y, below)
        send_if(always, y_up[0], z, y, y_dev)

    unit_rows = [None] * c.N
    choices = []
    for image in range(c.N):
        rows = slice(image * c.B, (image + 1) * c.B)
        names = route_ref[rows, :]
        live = jnp.where(row_of((c.B, 1)) < len_ref[image, x], 1.0, 0.0)
        kept = keep_ref[rows, :].astype(F32) * live
        first, second = names[:, 0:1], names[:, 1:2]
        lane = lane_of((c.B, 128))
        named = jnp.where(lane == first, kept[:, 0:1], 0.0) + jnp.where(
            lane == second, kept[:, 1:2], 0.0
        )
        earlier = jnp.where(lane_of((c.B, c.B)) < row_of((c.B, c.B)), 1.0, 0.0).astype(BF16)
        rank = mm(earlier, named.astype(BF16))
        rank_first = jnp.sum(jnp.where(lane == first, rank, 0.0), axis=1, keepdims=True)
        rank_second = jnp.sum(jnp.where(lane == second, rank, 0.0), axis=1, keepdims=True)
        slot_first = first * c.cap + rank_first.astype(jnp.int32)
        slot_second = second * c.cap + rank_second.astype(jnp.int32)
        at = lane_of((c.B, c.E * c.cap))
        place = jnp.where(at == slot_first, kept[:, 0:1], 0.0) + jnp.where(
            at == slot_second, kept[:, 1:2], 0.0
        )
        place = place.astype(BF16)
        choices.append((first, second, kept, slot_first, slot_second, place))
        dysend[image] = mm(place, cot_ref[rows, :], TN).astype(BF16).reshape(c.E, c.cap, c.D)
        dyarr_ref[z, image] = dysend[image, z]

    if c.gather:
        for at, device in zip(small_ids, plane):
            other = lax.div(shard, 1)
            links.make(at, smalls.at[other], smalls.at[other], device).wait_recv()
        wide = jnp.concatenate([smalls[k] for k in range(c.E * c.Y)], axis=1).astype(BF16)
        span = c.E * c.Y * 128
        src, dst = row_of((span, c.D)), lane_of((span, c.D))
        inside = lax.rem(src, 128)
        pick = jnp.logical_and(inside < c.sh, lax.div(src, 128) * c.sh + inside == dst)
        vec_ref[...] = mm(wide, jnp.where(pick, 1.0, 0.0).astype(BF16))
    vec = vec_ref[...]
    for image in range(c.N):
        rows = slice(image * c.B, (image + 1) * c.B)
        unit_one, _ = normalize(tok_ref[rows, :].astype(F32))
        norm_ref[rows, :] = (unit_one * vec[0:1] + vec[2:3]).astype(BF16)

    if c.gather:

        def got(at, z_at, y_at):
            copy_of(at, z_at, y_at, core_dev).wait_recv()

        def pass_y(at, z_at, core_at, condition):
            pl.when(condition)(lambda: got(at, z_at, 1 - y))
            send_if(condition, core_at, z_at, 1 - y, core_dev)

        for j in range(1, c.E):
            lower, upper = z >= j, z + j <= c.E - 1
            pl.when(lower)(lambda: got(up[j], z - j, y))
            if j < c.E - 1:
                send_if(jnp.logical_and(lower, z < c.E - 1), up[j + 1], z - j, y, above)
            send_if(lower, y_up[j], z - j, y, y_dev)
            send_if(lower, core_up[0][j], z - j, y, core_dev)
            pl.when(upper)(lambda: got(down[j], z + j, y))
            if j < c.E - 1:
                send_if(jnp.logical_and(upper, z > 0), down[j + 1], z + j, y, below)
            send_if(upper, y_down[j], z + j, y, y_dev)
            send_if(upper, core_down[0][j], z + j, y, core_dev)
            if j == 1:
                pass_y(y_up[0], z, core_up[1][0], always)
            else:
                pass_y(y_up[j - 1], z - j + 1, core_up[1][j - 1], z >= j - 1)
                pass_y(y_down[j - 1], z + j - 1, core_down[1][j - 1], z + j - 1 <= c.E - 1)
        last = c.E - 1
        pass_y(y_up[last], z - last, core_up[1][last], z >= last)
        pass_y(y_down[last], z + last, core_down[1][last], z + last <= c.E - 1)

        def got_core(at, z_at, y_at):
            there = other_unit(z_at, y_at)
            links.make(at, there, there, core_dev).wait_recv()

        for side in range(2):
            y_at = y if side == 0 else 1 - y
            if side:
                got_core(core_up[side][0], z, y_at)
            for j in range(1, c.E):
                pl.when(z >= j)(lambda: got_core(core_up[side][j], z - j, y_at))
                pl.when(z + j <= c.E - 1)(lambda: got_core(core_down[side][j], z + j, y_at))

    normed = norm_ref[...]
    own_at = pl.ds(pl.multiple_of(x * c.B, 32), c.B)
    kv_ids = [[links.new() for _ in range(3)] for _ in range(c.N)]
    keys = mm(normed, w_ref[1]).astype(BF16)
    values = mm(normed, w_ref[2]).astype(BF16)
    for image in range(c.N):
        rows = slice(image * c.B, (image + 1) * c.B)
        kv_ref[image, own_at, 0 : c.D] = keys[rows]
        kv_ref[image, own_at, c.D : 2 * c.D] = values[rows]
        block = kv_ref.at[image, own_at, :]
        go(kv_ids[image][0], block, block, far_dev)
        go(kv_ids[image][1], block, block, core_dev)
    dy_ids = [links.new() for _ in experts]
    for k, (at, device) in enumerate(zip(dy_ids, experts), 1):
        go(at, dysend.at[:, z ^ k], dyarr_ref.at[z], device)
    q_ref[...] = mm(normed, w_ref[0]).astype(BF16)

    block_of = lambda image, who: kv_ref.at[image, pl.ds(pl.multiple_of(who * c.B, 32), c.B), :]

    for image in range(c.N):
        rows = pl.ds(image * c.B, c.B)
        far_block = block_of(image, x ^ 2)
        links.make(kv_ids[image][0], far_block, far_block, far_dev).wait_recv()
        go(kv_ids[image][2], far_block, far_block, core_dev)
        near_block = block_of(image, x ^ 1)
        links.make(kv_ids[image][1], near_block, near_block, core_dev).wait_recv()
        cross_block = block_of(image, x ^ 3)
        links.make(kv_ids[image][2], cross_block, cross_block, core_dev).wait_recv()
        bias = key_bias(c, len_ref, image)

        def pair_step(pair, carry):
            lanes = pl.ds(pl.multiple_of(pair * 128, 128), 128)
            value_lanes = pl.ds(pl.multiple_of(c.D + pair * 128, 128), 128)
            queries = two_heads(q_ref[rows, lanes]) * jnp.asarray(c.scale, BF16)
            scores = mm(kv_ref[image, :, lanes], queries, NT) + bias
            top = jnp.max(scores, axis=0, keepdims=True)
            exponent = jnp.exp(scores - top)
            total = jnp.sum(exponent, axis=0, keepdims=True)
            probs = (exponent * (1.0 / total)).astype(BF16)
            lse_ref[image, pair] = jnp.broadcast_to(top + jnp.log(total), (8, 2 * c.B))
            mixed_values = mm(kv_ref[image, :, value_lanes].T, probs)
            att_ref[rows, lanes] = one_pair(mixed_values.T).astype(BF16)
            return carry

        lax.fori_loop(0, c.D // 128, pair_step, 0)

    branch = mm(att_ref[...], w_ref[3])
    hidden = tok_ref[...].astype(F32) + branch
    hid_ref[...] = hidden
    unit_two, _ = normalize(hidden)
    mixed = (unit_two * vec[1:2] + vec[3:4]).astype(BF16)
    mix_ref[...] = mixed
    pad = jnp.zeros((128 - c.r8, c.D), BF16)
    logits = mm(mixed, jnp.concatenate([vec.astype(BF16), pad], axis=0), NT)
    lane = lane_of((c.N * c.B, 128))
    valid = jnp.logical_and(lane >= LOGIT_LANE, lane < LOGIT_LANE + c.E)
    logits = jnp.where(valid, logits, -1e30)
    weight = jnp.exp(logits - jnp.max(logits, axis=1, keepdims=True))
    router = weight / jnp.sum(weight, axis=1, keepdims=True)
    router_ref[...] = router
    gsend_ref[...] = jnp.zeros_like(gsend_ref)
    lane = lane_of((c.B, 128))
    for image in range(c.N):
        rows = slice(image * c.B, (image + 1) * c.B)
        first, second, kept, slot_first, slot_second, place = choices[image]
        here = router[rows]
        gate_first = kept[:, 0:1] * jnp.sum(
            jnp.where(lane == LOGIT_LANE + first, here, 0.0), axis=1, keepdims=True
        )
        gate_second = kept[:, 1:2] * jnp.sum(
            jnp.where(lane == LOGIT_LANE + second, here, 0.0), axis=1, keepdims=True
        )
        send_ref[image] = mm(place, mixed[rows], TN).astype(BF16).reshape(c.E, c.cap, c.D)
        at = lane_of((c.B, c.cap))
        for expert in range(c.E):
            gates = jnp.where(at == slot_first - expert * c.cap, gate_first, 0.0)
            gates = gates + jnp.where(at == slot_second - expert * c.cap, gate_second, 0.0)
            gsend_ref[expert, image : image + 1, :] = jnp.sum(gates, axis=0, keepdims=True)
        columns = (
            slot_first.astype(F32),
            slot_second.astype(F32),
            kept[:, 0:1],
            kept[:, 1:2],
            gate_first,
            gate_second,
            first.astype(F32),
            second.astype(F32),
        )
        meta = jnp.zeros((c.B, 128), F32)
        for index, column in enumerate(columns):
            meta = jnp.where(lane == index, column, meta)
        meta_ref[rows, :] = meta

    for k, (at, device) in enumerate(zip(dy_ids, experts), 1):
        links.make(at, dyarr_ref.at[z ^ k], dyarr_ref.at[z ^ k], device).wait_recv()
    for copy in ends:
        copy.wait_send()
    if c.gather:
        for condition, at, z_at, y_at, device in pending:
            pl.when(condition)(lambda: copy_of(at, z_at, y_at, device).wait_send())


def spec(space):
    return pl.BlockSpec(memory_space=space)


def run_front(c, lengths, tok, route, keep, cot, weights):
    shape = jax.ShapeDtypeStruct
    made = [shape((4, c.D, c.D), BF16), shape((c.r8, c.D), F32)] if c.gather else []
    made += [
        shape((c.T, c.D), BF16),
        shape((c.N, c.S, 2 * c.D), BF16),
        shape((c.N, c.D // 128, 8, 2 * c.B), F32),
        shape((c.T, c.D), BF16),
        shape((c.T, c.D), F32),
        shape((c.T, c.D), BF16),
        shape((c.T, 128), F32),
        shape((c.T, 128), F32),
        shape((c.N, c.E, c.cap, c.D), BF16),
        shape((c.E, 8, c.cap), F32),
        shape((c.E, c.N, c.cap, c.D), BF16),
    ]
    count = 96 if c.gather else 2 * c.E + 16
    out = pl.pallas_call(
        functools.partial(front_kernel, c),
        out_shape=made,
        in_specs=[spec(pltpu.SMEM)] + [spec(pltpu.VMEM)] * (4 + len(weights)),
        out_specs=[spec(pltpu.VMEM)] * len(made),
        scratch_shapes=[
            pltpu.VMEM((c.E * c.Y, c.r8, 128), F32),
            pltpu.VMEM((c.N, c.E, c.cap, c.D), BF16),
            pltpu.VMEM((c.T, c.D), BF16),
            pltpu.SemaphoreType.DMA((count,)),
            pltpu.SemaphoreType.DMA((count,)),
        ],
        compiler_params=pltpu.CompilerParams(
            collective_id=0, has_side_effects=True, vmem_limit_bytes=VMEM_LIMIT
        ),
        name="front",
    )(lengths, tok, route, keep, cot, *weights)
    return out if c.gather else list(weights) + list(out)


def gelu_both(pre):
    inner = 0.7978845608028654 * (pre + 0.044715 * pre * pre * pre)
    bend = jnp.tanh(inner)
    half = 0.5 * (1.0 + bend)
    slope = 0.7978845608028654 * (1.0 + 0.134145 * pre * pre)
    return pre * half, half + 0.5 * pre * (1.0 - bend * bend) * slope


def expert_kernel(
    c,
    send_ref,
    gsend_ref,
    dyarr_ref,
    win_hbm,
    wdown_hbm,
    xback_ref,
    gback_ref,
    yloc_ref,
    grad_ref,
    win,
    wdown,
    arr,
    garr,
    act_all,
    dpre_all,
    dout_all,
    dxs,
    dgs,
    turned,
    wsem,
    ssem,
    rsem,
):
    links = Links(ssem, rsem)
    z, x, y = lax.axis_index("expert"), lax.axis_index("context"), lax.axis_index("dp")
    experts = [(z ^ k, x, y) for k in range(1, c.E)]
    load_in = pltpu.make_async_copy(win_hbm, win, wsem.at[0])
    load_down = pltpu.make_async_copy(wdown_hbm, wdown, wsem.at[1])
    load_in.start()
    load_down.start()
    greet(experts)
    ids = [[links.new() for _ in range(4)] for _ in range(c.E)]
    ends = []

    def go(at, src, dst, device):
        copy = links.make(at, src, dst, device)
        copy.start()
        ends.append(copy)

    for k in range(1, c.E):
        go(ids[k][0], send_ref.at[:, z ^ k], arr.at[z], experts[k - 1])
        go(ids[k][1], gsend_ref.at[z ^ k], garr.at[z], experts[k - 1])
    for image in range(c.N):
        arr[z, image] = send_ref[image, z]
    garr[z] = gsend_ref[z]
    load_in.wait()
    load_down.wait()
    dgs[...] = jnp.zeros_like(dgs)
    group = c.E // c.chunks
    height = group * c.N * c.cap
    for g in range(c.chunks):
        slab = lax.div(z, group) ^ g
        for k in range(g * group, (g + 1) * group):
            if k:
                there = z ^ k
                links.make(ids[k][0], arr.at[there], arr.at[there], experts[k - 1]).wait_recv()
                links.make(ids[k][1], garr.at[there], garr.at[there], experts[k - 1]).wait_recv()
        start = pl.multiple_of(slab * height, 32)
        rows = pl.ds(start, height)
        for member in range(group):
            source = slab * group + member
            for image in range(c.N):
                gates = to_column(garr[source, image : image + 1, :])
                offset = (member * c.N + image) * c.cap
                part = pl.ds(pl.multiple_of(start + offset, 16), c.cap)
                dout_all[part, :] = (gates * dyarr_ref[source, image].astype(F32)).astype(BF16)
        inputs = arr[pl.ds(slab * group, group)].reshape(height, c.D)
        douts = dout_all[rows, :]

        def ff_step(step, carry):
            lanes = pl.ds(pl.multiple_of(step * c.FB, 128), c.FB)
            pre = mm(inputs, win[:, lanes])
            act, slope = gelu_both(pre)
            act_all[rows, lanes] = act.astype(BF16)
            dact = mm(douts, wdown[lanes, :], NT)
            dpre_all[rows, lanes] = (dact * slope).astype(BF16)
            return carry

        lax.fori_loop(0, c.FF // c.FB, ff_step, 0)
        dx = mm(dpre_all[rows, :], win[...], NT).astype(BF16)
        dxs[pl.ds(slab * group, group)] = dx.reshape(group, c.N, c.cap, c.D)
        made = mm(act_all[rows, :], wdown[...]).astype(BF16)
        yloc_ref[pl.ds(slab * group, group)] = made.reshape(group, c.N, c.cap, c.D)
        for member in range(group):
            source = slab * group + member
            for image in range(c.N):
                offset = (member * c.N + image) * c.cap
                dots = made[offset : offset + c.cap].astype(F32) * dyarr_ref[source, image].astype(
                    F32
                )
                dgs[source, image : image + 1, :] = to_row(jnp.sum(dots, axis=1, keepdims=True))
        for k in range(g * group, (g + 1) * group):
            if k:
                there = z ^ k
                go(ids[k][2], dxs.at[there], xback_ref.at[:, z], experts[k - 1])
                go(ids[k][3], dgs.at[there], gback_ref.at[z], experts[k - 1])
    for image in range(c.N):
        xback_ref[image, z] = dxs[z, image]
    gback_ref[z] = dgs[z]

    total = c.E * c.N * c.cap
    turned[0] = arr[...].reshape(total, c.D).T
    turned[1] = dout_all[...].T

    def grad_step(step, carry):
        lanes = pl.ds(pl.multiple_of(step * c.FB, 128), c.FB)
        grad_ref[0, :, lanes] = mm(turned[0], dpre_all[:, lanes]).astype(BF16)
        grad_ref[1, :, lanes] = mm(turned[1], act_all[:, lanes]).astype(BF16)
        return carry

    lax.fori_loop(0, c.FF // c.FB, grad_step, 0)
    for k in range(1, c.E):
        there = z ^ k
        links.make(ids[k][2], xback_ref.at[:, there], xback_ref.at[:, there], experts[k - 1]).wait_recv()
        links.make(ids[k][3], gback_ref.at[there], gback_ref.at[there], experts[k - 1]).wait_recv()
    for copy in ends:
        copy.wait_send()


def run_experts(c, send, gsend, dyarr, w_in, w_down):
    shape = jax.ShapeDtypeStruct
    total = c.E * c.N * c.cap
    count = 4 * c.E
    return pl.pallas_call(
        functools.partial(expert_kernel, c),
        out_shape=[
            shape((c.N, c.E, c.cap, c.D), BF16),
            shape((c.E, 8, c.cap), F32),
            shape((c.E, c.N, c.cap, c.D), BF16),
            shape((2, c.D, c.FF), BF16),
        ],
        in_specs=[spec(pltpu.VMEM)] * 3 + [spec(pl.ANY)] * 2,
        out_specs=[spec(pltpu.VMEM)] * 4,
        scratch_shapes=[
            pltpu.VMEM((c.D, c.FF), BF16),
            pltpu.VMEM((c.FF, c.D), BF16),
            pltpu.VMEM((c.E, c.N, c.cap, c.D), BF16),
            pltpu.VMEM((c.E, 8, c.cap), F32),
            pltpu.VMEM((total, c.FF), BF16),
            pltpu.VMEM((total, c.FF), BF16),
            pltpu.VMEM((total, c.D), BF16),
            pltpu.VMEM((c.E, c.N, c.cap, c.D), BF16),
            pltpu.VMEM((c.E, 8, c.cap), F32),
            pltpu.VMEM((2, c.D, total), BF16),
            pltpu.SemaphoreType.DMA((2,)),
            pltpu.SemaphoreType.DMA((count,)),
            pltpu.SemaphoreType.DMA((count,)),
        ],
        compiler_params=pltpu.CompilerParams(
            collective_id=1, has_side_effects=True, vmem_limit_bytes=VMEM_LIMIT
        ),
        name="experts",
    )(send, gsend, dyarr, w_in, w_down)


def back_plain(c, tok, cot, lengths, weights, vec, q, kv, lse, att, hid, mix, meta, router, xback, gback, yloc, grads):
    precise = lax.Precision.HIGHEST
    rank = lax.axis_index("context")
    own = lax.dynamic_slice_in_dim(lengths, rank, 1, 1)
    live = (jnp.arange(c.B, dtype=jnp.int32)[None, :] < own).astype(F32).reshape(c.T, 1)
    slots = meta[:, 0:2].astype(jnp.int32)
    kept, gates, names = meta[:, 2:4], meta[:, 4:6], meta[:, 6:8].astype(jnp.int32)
    image = jnp.repeat(jnp.arange(c.N, dtype=jnp.int32), c.B)[:, None]
    spots = image * (c.E * c.cap) + slots
    made = lax.all_to_all(yloc, "expert", split_axis=0, concat_axis=0, tiled=True)
    made = made.transpose(1, 0, 2, 3).reshape(c.N * c.E * c.cap, c.D)
    rows = made[spots].astype(F32)
    dy = cot.astype(F32) * live
    out = (live * (hid + jnp.sum(gates[:, :, None] * rows, axis=1))).astype(BF16)
    copies = xback.reshape(c.N * c.E * c.cap, c.D)[spots].astype(F32)
    dgate = gback[:, : c.N].transpose(1, 0, 2).reshape(-1)[spots] * kept
    d_mixed = jnp.sum(copies * kept[:, :, None], axis=1)
    probs = router[:, LOGIT_LANE : LOGIT_LANE + c.E]
    choose = (names[:, :, None] == jnp.arange(c.E)).astype(F32)
    d_router = jnp.sum(choose * dgate[:, :, None], axis=1)
    d_logits = probs * (d_router - jnp.sum(probs * d_router, axis=1, keepdims=True))
    w_router = vec[LOGIT_LANE : LOGIT_LANE + c.E]
    d_mixed = d_mixed + jnp.dot(d_logits, w_router, precision=precise)
    g_router = jnp.einsum("rd,re->de", mix.astype(F32), d_logits, precision=precise)
    unit_two, inverse_two = normalize(hid)
    gains_two, biases_two = jnp.sum(d_mixed * unit_two, axis=0), jnp.sum(d_mixed, axis=0)
    d_hidden = dy + normalize_back(d_mixed, unit_two, inverse_two, vec[1])
    d_branch = d_hidden.astype(BF16)
    g_out = mm(att, d_branch, TN)
    d_att = mm(d_branch, weights[3], NT).astype(BF16)
    hd = c.D // HEADS
    qh = q.reshape(c.N, c.B, HEADS, hd)
    kh = kv[:, :, : c.D].reshape(c.N, c.S, HEADS, hd)
    vh = kv[:, :, c.D :].reshape(c.N, c.S, HEADS, hd)
    dh = d_att.reshape(c.N, c.B, HEADS, hd)
    ein = functools.partial(jnp.einsum, preferred_element_type=F32)
    at = jnp.arange(c.S, dtype=jnp.int32)
    key_live = at[None, :] % c.B < lengths[:, at // c.B]
    scores = jnp.where(key_live[:, None, None, :], ein("iqhd,ikhd->ihqk", qh, kh) * c.scale, -1e30)
    total = lse[:, :, 0, :].reshape(c.N, c.D // 128, 2, c.B).reshape(c.N, HEADS, c.B, 1)
    p = jnp.exp(scores - total)
    dp = ein("iqhd,ikhd->ihqk", dh, vh)
    ds = (p * (dp - jnp.sum(p * dp, axis=-1, keepdims=True))).astype(BF16)
    dq = ein("ihqk,ikhd->iqhd", ds, kh) * c.scale
    dk = ein("ihqk,iqhd->ikhd", ds, qh) * c.scale
    dv = ein("ihqk,iqhd->ikhd", p.astype(BF16), dh)
    terms = jnp.concatenate([dk.reshape(c.N, c.S, c.D), dv.reshape(c.N, c.S, c.D)], axis=2)
    summed = lax.psum_scatter(terms.astype(BF16), "context", scatter_dimension=1, tiled=True)
    d_proj = jnp.concatenate(
        [dq.reshape(c.T, c.D).astype(BF16), summed.reshape(c.T, 2 * c.D).astype(BF16)], axis=1
    )
    unit_one, inverse_one = normalize(tok.astype(F32))
    normed = (unit_one * vec[0] + vec[2]).astype(BF16)
    g_qkv = mm(normed, d_proj, TN)
    qkv = jnp.concatenate([weights[0], weights[1], weights[2]], axis=1)
    d_normed = mm(d_proj, qkv, NT)
    gains_one, biases_one = jnp.sum(d_normed * unit_one, axis=0), jnp.sum(d_normed, axis=0)
    g_tok = d_hidden + normalize_back(d_normed, unit_one, inverse_one, vec[0])
    both = ("expert", "dp")
    dense = [
        lax.psum_scatter(g_qkv, both, scatter_dimension=0, tiled=True),
        lax.psum_scatter(g_out, both, scatter_dimension=0, tiled=True),
        lax.psum_scatter(g_router, both, scatter_dimension=0, tiled=True),
        lax.psum_scatter(jnp.stack([gains_one, gains_two]), both, scatter_dimension=1, tiled=True),
        lax.psum_scatter(jnp.stack([biases_one, biases_two]), both, scatter_dimension=1, tiled=True),
    ]
    dense = [part.astype(F32) for part in lax.psum([p.astype(BF16) for p in dense], "context")]
    sums = lax.psum_scatter(grads, ("context", "dp"), scatter_dimension=2, tiled=True).astype(F32)
    shape = (c.N, c.B, c.D)
    return (
        out.reshape(shape),
        g_tok.reshape(shape),
        *dense,
        sums[0][None],
        sums[1].T[None],
    )


def pack_small(c, w_router, norm_gains, norm_biases):
    rows = jnp.concatenate([norm_gains, norm_biases, w_router.T], axis=0).astype(F32)
    return jnp.pad(rows, ((0, c.r8 - rows.shape[0]), (0, 128 - rows.shape[1])))


def per_device(
    mesh_shape,
    tokens,
    lengths,
    route_ids,
    keep_mask,
    w_qkv,
    w_attn_out,
    w_router,
    norm_gains,
    norm_biases,
    w_expert_in,
    w_expert_down,
    cotangent,
):
    images, block, width = tokens.shape
    experts = mesh_shape["expert"] * w_expert_in.shape[0]
    c = types.SimpleNamespace(
        E=experts,
        Y=mesh_shape["dp"],
        C=mesh_shape["context"],
        N=images,
        B=block,
        D=width,
        T=images * block,
        S=mesh_shape["context"] * block,
        FF=w_expert_in.shape[2],
        FB=512,
        cap=max(2, 16 * block // (5 * experts)),
        sh=w_qkv.shape[0],
        r8=-(-(LOGIT_LANE + experts) // 8) * 8,
        scale=(width // HEADS) ** -0.5,
        chunks=4,
    )
    c.gather = c.sh % 32 == 0
    tok = tokens.reshape(c.T, width)
    cot = cotangent.reshape(c.T, width)
    route = route_ids.reshape(c.T, 2)
    keep = keep_mask.reshape(c.T, 2)
    both = ("expert", "dp")
    if c.gather:
        given = (w_qkv, w_attn_out, pack_small(c, w_router, norm_gains, norm_biases))
    else:
        qkv = lax.all_gather(w_qkv, both, axis=0, tiled=True)
        out = lax.all_gather(w_attn_out, both, axis=0, tiled=True)
        small = pack_small(c, w_router, norm_gains, norm_biases)[:, : c.sh]
        vec = lax.all_gather(small, both, axis=1, tiled=True)
        stacked = jnp.concatenate([qkv, out], axis=1).reshape(width, 4, width).transpose(1, 0, 2)
        given = (stacked, vec)
    front = run_front(c, lengths, tok, route, keep, cot, given)
    weights, vec, q, kv, lse, att, hid, mix, meta, router, send, gsend, dyarr = front
    back = run_experts(c, send, gsend, dyarr, w_expert_in[0], w_expert_down[0])
    return back_plain(
        c, tok, cot, lengths, weights, vec, q, kv, lse, att, hid, mix, meta, router, *back
    )


def solution(mesh):
    rows = P(("expert", "dp"), "context", None)
    shard = P(("expert", "dp"), None)
    column = P(None, ("expert", "dp"))
    expert = P("expert", None, None)
    return jax.shard_map(
        functools.partial(per_device, dict(mesh.shape)),
        mesh=mesh,
        in_specs=(rows, shard, rows, rows, shard, shard, shard, column, column, expert, expert, rows),
        out_specs=(
            rows,
            rows,
            shard,
            shard,
            shard,
            column,
            column,
            P("expert", None, ("context", "dp")),
            P("expert", ("context", "dp"), None),
        ),
        check_vma=False,
    )
```

time: 1070 us -> 845 us (0.79)
  Pallas kernels: 0 us -> 149 us
  waiting for transfers between devices: 604 us -> 471 us
  matrix products: 140 us -> 49.6 us
  blocking collectives: 65.4 us -> 5.65 us
  other arithmetic: 66.2 us -> 30.4 us
  local copies, waits for them, and re-layouts: 137 us -> 109 us
  starting transfers between devices: 31.8 us -> 11.1 us
    pallas_call x0 -> x2, Pallas kernels: none -> 149 us  [the longest x1 75.9 us: run_front(): pl.pallas_call(functools.partial(front_kernel, c), out_shape=made, in_spe...]
    dot_general x42 -> x10, matrix products: 140 us -> 47 us  [the longest x4 13.9 us: mm(): return lax.dot_general(left, right, dims, preferred_element_type=F32)]
    all_gather x4 -> x0, waiting for transfers between devices: 90.9 us -> none  [the longest x1 34.9 us: per_device(): lax.all_gather(pieces[1], ('expert', 'dp'), axis=0, tiled=True)]
    all_gather x3 -> x0, blocking collectives: 59.7 us -> none  [the longest x1 22.3 us: per_device(): lax.all_gather(pieces[4], ('expert', 'dp'), axis=1, tiled=True)]
    all_to_all x8 -> x1, waiting for transfers between devices: 37.7 us -> 0.01 us  [back_plain(): lax.all_to_all(yloc, 'expert', split_axis=0, concat_axis=0, tiled=True)]
    unnamed x225 -> x79, local copies, waits for them, and re-layouts: 77.4 us -> 48.1 us
    all_to_all x8 -> x1, starting transfers between devices: 30.6 us -> 10.8 us  [back_plain(): lax.all_to_all(yloc, 'expert', split_axis=0, concat_axis=0, tiled=True)]
    unnamed x20 -> x12, waiting for transfers between devices: 195 us -> 214 us
  transfers between devices with their start and end apart: 22 -> 9, of which waited for: 18 -> 8; matrix products, arithmetic and copies ran while one was open for 24% -> 14% of each run, Pallas kernels for 0% -> 0%
where the time goes in v1:
time: 845 us; the launch traced here: 840 us
  waiting for transfers between devices  471 us (56%)
  Pallas kernels  149 us (18%)
  local copies, waits for them, and re-layouts  109 us (13%)
  matrix products  49.6 us (6%)
  other arithmetic  30.4 us (4%)
  between operations  15 us (2%)
  starting transfers between devices  11.1 us (1%)
    unnamed x12, waiting for transfers between devices  214 us
    reduce_scatter x1, waiting for transfers between devices, back_plain(): lax.psum_scatter(g_qkv, both, scatter_dimension=0, tiled=True)  130 us
    pallas_call x1, Pallas kernels, run_front(): pl.pallas_call(functools.partial(front_kernel, c), out_shape=made, in_spe...  75.9 us
    pallas_call x1, Pallas kernels, run_experts(): pl.pallas_call(functools.partial(expert_kernel, c), out_shape=[shape((c.N...  72.9 us
    reduce_scatter x1, waiting for transfers between devices, back_plain(): lax.psum_scatter(g_out, both, scatter_dimension=0, tiled=True)  71.3 us
    unnamed x79, local copies, waits for them, and re-layouts  48.1 us
    psum x1, waiting for transfers between devices, back_plain(): lax.psum([p.astype(BF16) for p in dense], 'context')  29.1 us
    reduce_scatter x1, waiting for transfers between devices, back_plain(): lax.psum_scatter(terms.astype(BF16), 'context', scatter_dimension=1, tile...  26.5 us
  transfers between devices with their start and end apart: 9, of which 8 were waited for; matrix products, arithmetic and copies ran while one was open for 14% of the time, Pallas kernels for 0%

profile of v1, /device:TPU:0, one launch (start us, length us, event | category | flops | bytes accessed | tf_op | source)
XLA Modules:
  0.0 840.1 jit_solution(12330073531095956844)
XLA Ops:
  11.5 75.9 %front.1 = (bf16[4,768,768]{2,1,0:T(8,128)(2,1)}, f32[8,768]{1,0:T(8,128)}, bf16[320,768]{1,0:T(8,128)(2,1)}, bf16[2,640,1536]{2,1,0:T(8,128)(2,1)}, f32[2,6,8,3...) custom-call(s32[2,4]{1,0:T(2,128)} %refs_0_.1, ...), custom_call_target="tpu_custom_call" | custom-call | tf_op jit(solution)/shard_map/front/pallas_call | solution.py:385
  87.4 72.9 %experts.1 = (bf16[2,4,128,768]{3,2,1,0:T(8,128)(2,1)}, f32[4,8,128]{2,1,0:T(8,128)}, bf16[4,2,128,768]{3,2,1,0:T(8,128)(2,1)}, bf16[2,768,3072]{2,1,0:T(8,128)(2,1)}) custom-call(bf16[2,4,128,768]{3,2,1,0:T(8,128)(2,1)} %get-tuple-element.28.send_ref, f32[4,8,128]{2,1,0:T(8,128)} %get-tuple-element.29.gsend_ref, ...), custom_call_target="tpu_custom_call" | custom-call | tf_op jit(solution)/shard_map/experts/pallas_call | solution.py:538
  160.3 10.8 %all-to-all-start = ((bf16[4,2,128,768]{3,2,1,0:T(8,128)(2,1)}), bf16[4,2,128,768]{3,2,1,0:T(8,128)(2,1)}, u32[]{:S(2)}, u32[]{:S(2)}) async-start(bf16[4,2,128,768]{3,2,1,0:T(8,128)(2,1)} %get-tuple-element.31), calls=%async_computation | async-start | bytes 3145728 | tf_op jit(solution)/shard_map/all_to_all | solution.py:579
  172.0 3.8 fusion.45
  180.9 1.8 reshape.302
  182.7 1.7 copy.107
  184.4 2.3 copy.109
  186.7 2.9 copy.103
  190.4 3.4 gather_fusion.1
  193.8 2.8 gather_fusion.2
  201.0 3.4 reshape.292
  206.3 6.3 fusion.46
  214.1 3.4 gather_fusion
  217.5 3.4 reshape.291
  221.0 6.6 multiply_reduce_fusion.1
  227.7 1.9 multiply_reduce_fusion.3
  230.9 1.9 convolution_convert_fusion
  232.7 1.8 reshape.303
  234.6 2.7 copy.110
  237.2 7.8 fusion.13
  245.1 4.1 copy.115
  249.2 8.1 multiply_reduce_fusion
  257.3 2.9 multiply_convert_fusion
  260.3 2.8 multiply_convert_fusion.1
  263.1 4.1 copy.114
  267.2 4.3 pad_maximum_fusion
  272.5 2.6 fusion.29
  275.2 3.3 fusion.26
  280.4 6.2 fusion.16
  286.6 2.2 copy.118
  289.6 26.5 %reduce-scatter.16.cloned.1.call-done = bf16[2,160,1536]{2,1,0:T(8,128)(2,1)} async-done(((bf16[2,640,1536]{2,1,0:T(8,128)(2,1)}), bf16[2,160,1536]{2,1,0:T(8,128)(2,1)}) %reduce-scatter.16.cloned.1.call-update) | async-done | bytes 983056 | tf_op jit(solution)/shard_map/reduce_scatter | solution.py:617
  316.0 6.3 fusion.21
  322.4 2.3 slice_bitcast_fusion.3
  324.8 2.5 multiply_reduce_fusion.4
  329.3 24.1 %copy.125 = bf16[2,768,3072]{1,0,2:T(2,128)(2,1)} copy(bf16[2,768,3072]{2,1,0:T(8,128)(2,1)} %get-tuple-element.42) | data formatting | bytes 18874368
  353.4 9.0 %copy.132 = bf16[384,8,2,768]{3,1,2,0:T(8,128)(2,1)} copy(bf16[384,8,2,768]{3,2,1,0:T(2,128)(2,1)} %bitcast.72) | data formatting | bytes 18874368
  362.5 19.1 %reduce-scatter.22.cloned.1.call-done = f32[96,4]{1,0:T(8,128)} async-done(((f32[768,4]{1,0:T(8,128)}), f32[96,4]{1,0:T(8,128)}) %reduce-scatter.22.cloned.1.call-update) | async-done | bytes 1552
  382.5 71.3 %reduce-scatter.20.cloned.1.call-done = f32[96,768]{1,0:T(8,128)} async-done(((f32[768,768]{1,0:T(8,128)}), f32[96,768]{1,0:T(8,128)}) %reduce-scatter.20.cloned.1.call-update) | async-done | bytes 294928 | tf_op jit(solution)/shard_map/reduce_scatter | solution.py:631
  455.4 130.4 %reduce-scatter.18.cloned.1.call-done = f32[96,2304]{1,0:T(8,128)} async-done(((f32[768,2304]{1,0:T(8,128)}), f32[96,2304]{1,0:T(8,128)}) %reduce-scatter.18.cloned.1.call-update) | async-done | bytes 884752 | tf_op jit(solution)/shard_map/reduce_scatter | solution.py:630
  585.8 2.0 convert_element_type.116
  589.2 60.3 %reduce-scatter.26.cloned.1.call-done = f32[96,2]{1,0:T(8,128)} async-done(((f32[768,2]{1,0:T(8,128)}), f32[96,2]{1,0:T(8,128)}) %reduce-scatter.26.cloned.1.call-update) | async-done | bytes 784
  650.3 63.3 %reduce-scatter.24.cloned.1.call-done = f32[96,2]{1,0:T(8,128)} async-done(((f32[768,2]{1,0:T(8,128)}), f32[96,2]{1,0:T(8,128)}) %reduce-scatter.24.cloned.1.call-update) | async-done | bytes 784
  714.4 5.7 all-reduce.1
  721.8 70.8 %reduce-scatter.28.cloned.1.call-done = bf16[384,1536]{1,0:T(8,128)(2,1)} async-done(((bf16[3072,1536]{1,0:T(8,128)(2,1)}), bf16[384,1536]{1,0:T(8,128)(2,1)}) %reduce-scatter.28.cloned.1.call-update) | async-done | bytes 1179664
  792.6 2.9 reshape.301
  795.5 2.0 copy.126
  800.2 29.1 %all-reduce.5.cloned.1.call-done = (bf16[96,2304]{1,0:T(8,128)(2,1)}, bf16[96,768]{1,0:T(8,128)(2,1)}) async-done(((bf16[96,2304]{1,0:T(8,128)(2,1)}, bf16[96,768]{1,0:T(8,128)(2,1)}), (bf16[96,2304]{1,0:T(8,128)(2,1)}, bf16[96,768]{1,0:T(8,128)(2,1)})) %all-reduce.5.cloned.1.call-update) | async-done | bytes 589840 | tf_op jit(solution)/shard_map/psum | solution.py:636
  831.0 2.0 convert_element_type.117
  (154 shorter events, 37.7 us)
Async XLA Ops:
  160.3 10.8 %copy-start.28 = (s32[2,4]{1,0:T(2,128)S(1)}, s32[2,4]{1,0:T(2,128)}, u32[]{:S(2)}) copy-start(s32[2,4]{1,0:T(2,128)} %refs_0_.1) | copy-start | bytes 100
  160.3 52.3 %all-to-all-start = ((bf16[4,2,128,768]{3,2,1,0:T(8,128)(2,1)}), bf16[4,2,128,768]{3,2,1,0:T(8,128)(2,1)}, u32[]{:S(2)}, u32[]{:S(2)}) async-start(bf16[4,2,128,768]{3,2,1,0:T(8,128)(2,1)} %get-tuple-element.31), calls=%async_computation | async-start | bytes 3145728 | tf_op jit(solution)/shard_map/all_to_all | solution.py:579
  171.1 144.9 %reduce-scatter.16.cloned.1.call-start = ((), (), s32[]{:S(2)}) async-start(), calls=%async_computation.8 | async-start | bytes 4915200 | tf_op jit(solution)/shard_map/reduce_scatter | solution.py:617
  172.0 5.6 copy-start.6
  186.7 3.6 copy-start.1
  193.8 3.0 copy-start.7
  193.8 6.2 copy-start.9
  196.5 7.8 copy-start.2
  205.4 7.2 copy-start.21
  217.5 3.4 copy-start.16
  217.5 3.4 copy-start.17
  220.9 6.7 copy-start.3
  220.9 6.7 copy-start.10
  220.9 6.7 copy-start.12
  220.9 6.7 copy-start.19
  220.9 6.7 copy-start.22
  220.9 6.7 copy-start.25
  227.6 2.0 copy-start.8
  227.6 2.0 copy-start.29
  230.9 6.4 copy-start.18
  230.9 6.4 copy-start.20
  249.2 8.2 slice-start
  249.2 8.2 slice-start.1
  249.2 8.2 slice-start.2
  257.3 2.9 copy-start.5
  260.3 2.8 copy-start
  271.5 0.9 copy-start.11
  271.5 1.0 copy-start.13
  271.5 110.1 %reduce-scatter.22.cloned.1.call-start = ((), (), s32[]{:S(2)}) async-start(), calls=%async_computation.11 | async-start | bytes 442368
  275.2 178.6 %reduce-scatter.20.cloned.1.call-start = ((), (), s32[]{:S(2)}) async-start(), calls=%async_computation.10 | async-start | bytes 2654208 | tf_op jit(solution)/shard_map/reduce_scatter | solution.py:631
  275.2 3.4 copy-start.4
  278.5 307.3 %reduce-scatter.18.cloned.1.call-start = ((), (), s32[]{:S(2)}) async-start(), calls=%async_computation.9 | async-start | bytes 7962624 | tf_op jit(solution)/shard_map/reduce_scatter | solution.py:630
  286.6 29.4 %copy-start.23 = (f32[320]{0:T(512)S(1)}, f32[320]{0:T(512)}, u32[]{:S(2)}) copy-start(f32[320]{0:T(512)} %div.47) | copy-start | bytes 3844
  286.6 29.4 %copy-start.24 = (f32[320]{0:T(512)S(1)}, f32[320]{0:T(512)}, u32[]{:S(2)}) copy-start(f32[320]{0:T(512)} %rsqrt.21) | copy-start | bytes 3844
  322.3 2.4 copy-start.27
  322.3 2.4 copy-start.26
  322.4 327.1 %reduce-scatter.26.cloned.1.call-start = ((), (), s32[]{:S(2)}) async-start(), calls=%async_computation.13 | async-start | bytes 442368
  322.4 2.4 copy-start.15
  328.2 385.3 %reduce-scatter.24.cloned.1.call-start = ((), (), s32[]{:S(2)}) async-start(), calls=%async_computation.12 | async-start | bytes 442368
  329.2 463.4 %reduce-scatter.28.cloned.1.call-start = ((), (), s32[]{:S(2)}) async-start(), calls=%async_computation.14 | async-start | bytes 10616832
  362.4 225.4 %copy-start.14 = (f32[320,768]{1,0:T(8,128)S(1)}, f32[320,768]{1,0:T(8,128)}, u32[]{:S(2)}) copy-start(f32[320,768]{1,0:T(8,128)} %get-tuple-element.118) | copy-start | bytes 2949124
  362.4 466.9 %all-reduce.5.cloned.1.call-start = ((), (), s32[]{:S(2)}) async-start(), calls=%async_computation.15 | async-start | bytes 1179648 | tf_op jit(solution)/shard_map/psum | solution.py:636
Sparse Core Ops, SparseCore 0:
  271.7 44.3 reduce-scatter.15
  320.2 61.3 reduce-scatter.21
  385.5 68.1 reduce-scatter.19
  457.7 128.0 reduce-scatter.17
  589.0 60.4 reduce-scatter.25
  653.1 60.3 reduce-scatter.23
  717.0 75.5 reduce-scatter.27
  795.7 33.6 all-reduce.4

commit v2 on v1

--- a/solution.py
+++ b/solution.py
@@ -567,81 +567,497 @@
     )(send, gsend, dyarr, w_in, w_down)
 
 
-def back_plain(c, tok, cot, lengths, weights, vec, q, kv, lse, att, hid, mix, meta, router, xback, gback, yloc, grads):
-    precise = lax.Precision.HIGHEST
-    rank = lax.axis_index("context")
-    own = lax.dynamic_slice_in_dim(lengths, rank, 1, 1)
-    live = (jnp.arange(c.B, dtype=jnp.int32)[None, :] < own).astype(F32).reshape(c.T, 1)
-    slots = meta[:, 0:2].astype(jnp.int32)
-    kept, gates, names = meta[:, 2:4], meta[:, 4:6], meta[:, 6:8].astype(jnp.int32)
-    image = jnp.repeat(jnp.arange(c.N, dtype=jnp.int32), c.B)[:, None]
-    spots = image * (c.E * c.cap) + slots
-    made = lax.all_to_all(yloc, "expert", split_axis=0, concat_axis=0, tiled=True)
-    made = made.transpose(1, 0, 2, 3).reshape(c.N * c.E * c.cap, c.D)
-    rows = made[spots].astype(F32)
-    dy = cot.astype(F32) * live
-    out = (live * (hid + jnp.sum(gates[:, :, None] * rows, axis=1))).astype(BF16)
-    copies = xback.reshape(c.N * c.E * c.cap, c.D)[spots].astype(F32)
-    dgate = gback[:, : c.N].transpose(1, 0, 2).reshape(-1)[spots] * kept
-    d_mixed = jnp.sum(copies * kept[:, :, None], axis=1)
-    probs = router[:, LOGIT_LANE : LOGIT_LANE + c.E]
-    choose = (names[:, :, None] == jnp.arange(c.E)).astype(F32)
-    d_router = jnp.sum(choose * dgate[:, :, None], axis=1)
-    d_logits = probs * (d_router - jnp.sum(probs * d_router, axis=1, keepdims=True))
-    w_router = vec[LOGIT_LANE : LOGIT_LANE + c.E]
-    d_mixed = d_mixed + jnp.dot(d_logits, w_router, precision=precise)
-    g_router = jnp.einsum("rd,re->de", mix.astype(F32), d_logits, precision=precise)
-    unit_two, inverse_two = normalize(hid)
-    gains_two, biases_two = jnp.sum(d_mixed * unit_two, axis=0), jnp.sum(d_mixed, axis=0)
-    d_hidden = dy + normalize_back(d_mixed, unit_two, inverse_two, vec[1])
+def in_parts(values, count):
+    parts = []
+    for _ in range(count):
+        parts.append(values.astype(BF16))
+        values = values - parts[-1].astype(F32)
+    return parts
+
+
+def back_kernel(c, *refs):
+    refs = list(refs)
+    take = lambda count: [refs.pop(0) for _ in range(count)]
+    len_ref, tok_ref, cot_ref, vec_ref, q_ref, lse_ref, att_ref, hid_ref, mix_ref = take(9)
+    meta_ref, router_ref, xback_ref, gback_ref = take(4)
+    w_hbm, kv_hbm, yloc_hbm, grad_hbm = take(4)
+    out_ref, gtok_ref, gin_ref, gdown_ref = take(4)
+    if c.gather:
+        gqkv_ref, gout_ref, gsmall_ref = take(3)
+    else:
+        dd, gsmall_ref = take(2)
+    w_ref, kv_ref, made = take(3)
+    gsum, gcore, gy, gx = take(4)
+    dkv, kvcore, kvfar, dproj, datt, dhid, norm_t, router_sum = take(8)
+    if c.gather:
+        dd, dcore, done_x, done_y, done_z, whole, small, small_in = take(8)
+    lsem, ssem, rsem = take(3)
+    links = Links(ssem, rsem)
+    z, x, y = lax.axis_index("expert"), lax.axis_index("context"), lax.axis_index("dp")
+    core, side = lax.rem(x, 2), lax.div(x, 2)
+    core_dev, far_dev, y_dev = (z, x ^ 1, y), (z, x ^ 2, y), (z, x, 1 - y)
+    experts = [(z ^ k, x, y) for k in range(1, c.E)]
+    ends = []
+
+    def go(at, src, dst, device):
+        copy = links.make(at, src, dst, device)
+        copy.start()
+        ends.append(copy)
+
+    def got(at, dst, device):
+        links.make(at, dst, dst, device).wait_recv()
+
+    half = c.FF // 4
+    piece = half // 2
+    loads = [
+        pltpu.make_async_copy(w_hbm, w_ref, lsem.at[0]),
+        pltpu.make_async_copy(kv_hbm, kv_ref, lsem.at[1]),
+    ]
+    own_start = pl.multiple_of(core * half, 128)
+    for part in range(2):
+        columns = pl.ds(pl.multiple_of(part * 2 * half + own_start, 128), half)
+        loads.append(
+            pltpu.make_async_copy(grad_hbm.at[:, :, columns], gsum.at[part], lsem.at[2 + part])
+        )
+    loads.append(pltpu.make_async_copy(yloc_hbm.at[z], made.at[:, z], lsem.at[4]))
+    for load in loads:
+        load.start()
+    greet([core_dev, far_dev, y_dev] + experts)
+
+    made_ids = [links.new() for _ in experts]
+    for k, (at, device) in enumerate(zip(made_ids, experts), 1):
+        go(at, yloc_hbm.at[z ^ k], made.at[:, z], device)
+    gcore_ids = [[links.new() for _ in range(2)] for _ in range(2)]
+    other_start = (1 - core) * half
+    for part in range(2):
+        columns = pl.ds(pl.multiple_of(part * 2 * half + other_start, 128), half)
+        for which in range(2):
+            go(
+                gcore_ids[part][which],
+                grad_hbm.at[which, :, columns],
+                gcore.at[part, which],
+                core_dev,
+            )
+    gy_ids = [[links.new() for _ in range(2)] for _ in range(2)]
+    gx_ids = [links.new() for _ in range(2)]
+    own_piece = pl.ds(pl.multiple_of(y * piece, 128), piece)
+    other_piece = pl.ds(pl.multiple_of((1 - y) * piece, 128), piece)
+
+    def grads_after_core():
+        loads[2].wait()
+        loads[3].wait()
+        for order in range(2):
+            part = 1 - side if order == 0 else side
+            for which in range(2):
+                for p in range(2):
+                    if order == 0:
+                        got(gcore_ids[p][which], gcore.at[p, which], core_dev)
+                gsum[part, which] = (
+                    gsum[part, which].astype(F32) + gcore[part, which].astype(F32)
+                ).astype(BF16)
+                go(
+                    gy_ids[order][which],
+                    gsum.at[part, which, :, other_piece],
+                    gy.at[order, which],
+                    y_dev,
+                )
+
+    def grads_after_y_far():
+        part = 1 - side
+        for which in range(2):
+            got(gy_ids[0][which], gy.at[0, which], y_dev)
+            gsum[part, which, :, own_piece] = (
+                gsum[part, which, :, own_piece].astype(F32) + gy[0, which].astype(F32)
+            ).astype(BF16)
+            go(gx_ids[which], gsum.at[part, which, :, own_piece], gx.at[which], far_dev)
+
+    def grads_end():
+        for which in range(2):
+            got(gy_ids[1][which], gy.at[1, which], y_dev)
+            got(gx_ids[which], gx.at[which], far_dev)
+            total = gsum[side, which, :, own_piece].astype(F32) + gy[1, which].astype(F32)
+            total = total + gx[which].astype(F32)
+            if which == 0:
+                gin_ref[...] = total
+            else:
+                gdown_ref[...] = total.T
+
+    if c.gather:
+        n_dense = 4
+        core_cols = c.D // 2
+        keep_cols = pl.ds(pl.multiple_of(core * core_cols, 128), core_cols)
+        give_cols = pl.ds(pl.multiple_of((1 - core) * core_cols, 128), core_cols)
+        rows_half = c.sh // 2
+        keep_rows = pl.ds(pl.multiple_of(side * rows_half, 16), rows_half)
+        give_rows = pl.ds(pl.multiple_of((1 - side) * rows_half, 16), rows_half)
+        ids_core = [links.new() for _ in range(n_dense)]
+        ids_x = [links.new() for _ in range(n_dense)]
+        ids_y = [links.new() for _ in range(n_dense)]
+        ids_z = [[links.new() for _ in experts] for _ in range(n_dense)]
+        ids_far = [links.new() for _ in range(n_dense)]
+        ids_own = [links.new() for _ in range(n_dense)]
+        ids_cross = [links.new() for _ in range(n_dense)]
+
+        def dense_start(m, value):
+            dd[m] = value.astype(BF16).reshape(c.E, c.Y, c.sh, c.D)
+            go(ids_core[m], dd.at[m, :, :, :, give_cols], dcore.at[m], core_dev)
+
+        def dense_x(m):
+            got(ids_core[m], dcore.at[m], core_dev)
+            dd[m, :, :, :, keep_cols] = (
+                dd[m, :, :, :, keep_cols].astype(F32) + dcore[m].astype(F32)
+            ).astype(BF16)
+            go(ids_x[m], dd.at[m, :, :, give_rows, keep_cols], done_x.at[m], far_dev)
+
+        def dense_y(m):
+            got(ids_x[m], done_x.at[m], far_dev)
+            dd[m, :, :, keep_rows, keep_cols] = (
+                dd[m, :, :, keep_rows, keep_cols].astype(F32) + done_x[m].astype(F32)
+            ).astype(BF16)
+            go(ids_y[m], dd.at[m, :, 1 - y, keep_rows, keep_cols], done_y.at[m], y_dev)
+
+        def dense_z(m):
+            got(ids_y[m], done_y.at[m], y_dev)
+            dd[m, :, y, keep_rows, keep_cols] = (
+                dd[m, :, y, keep_rows, keep_cols].astype(F32) + done_y[m].astype(F32)
+            ).astype(BF16)
+            for k, device in enumerate(experts, 1):
+                go(
+                    ids_z[m][k - 1],
+                    dd.at[m, z ^ k, y, keep_rows, keep_cols],
+                    done_z.at[m, z],
+                    device,
+                )
+
+        def dense_share(m):
+            total = dd[m, z, y, keep_rows, keep_cols].astype(F32)
+            for k, device in enumerate(experts, 1):
+                got(ids_z[m][k - 1], done_z.at[m, z ^ k], device)
+                total = total + done_z[m, z ^ k].astype(F32)
+            whole[m, side, core] = total
+            own = whole.at[m, side, core]
+            go(ids_far[m], own, own, far_dev)
+            go(ids_own[m], own, own, core_dev)
+
+        def dense_cross(m):
+            there = whole.at[m, 1 - side, core]
+            got(ids_far[m], there, far_dev)
+            go(ids_cross[m], there, there, core_dev)
+
+        def dense_end(m):
+            there = whole.at[m, side, 1 - core]
+            got(ids_own[m], there, core_dev)
+            there = whole.at[m, 1 - side, 1 - core]
+            got(ids_cross[m], there, core_dev)
+            for s in range(2):
+                for k in range(2):
+                    rows = slice(s * rows_half, (s + 1) * rows_half)
+                    if m == 3:
+                        gout_ref[rows, k * core_cols : (k + 1) * core_cols] = whole[m, s, k]
+                    else:
+                        start = m * c.D + k * core_cols
+                        gqkv_ref[rows, start : start + core_cols] = whole[m, s, k]
+
+    else:
+
+        def dense_start(m, value):
+            dd[m] = value.astype(BF16)
+
+    vec = vec_ref[...]
+    lane = lane_of((c.B, 128))
+    d_mixed, dy_rows, lives = [], [], []
+    d_logits = []
+    for image in range(c.N):
+        rows = slice(image * c.B, (image + 1) * c.B)
+        meta = meta_ref[rows, :]
+        slots = [meta[:, j : j + 1].astype(jnp.int32) for j in range(2)]
+        kept = [meta[:, 2 + j : 3 + j] for j in range(2)]
+        names = [meta[:, 6 + j : 7 + j].astype(jnp.int32) for j in range(2)]
+        at = lane_of((c.B, c.E * c.cap))
+        place = jnp.where(at == slots[0], kept[0], 0.0) + jnp.where(at == slots[1], kept[1], 0.0)
+        copies = xback_ref[image].reshape(c.E * c.cap, c.D)
+        d_mixed.append(mm(place.astype(BF16), copies))
+        d_router = jnp.zeros((c.B, 128), F32)
+        at = lane_of((c.B, c.cap))
+        for j in range(2):
+            d_gate = jnp.zeros((c.B, c.cap), F32)
+            for expert in range(c.E):
+                row = gback_ref[expert, image : image + 1, :]
+                d_gate = d_gate + jnp.where(at == slots[j] - expert * c.cap, row, 0.0)
+            d_gate = jnp.sum(d_gate, axis=1, keepdims=True) * kept[j]
+            d_router = d_router + jnp.where(lane == LOGIT_LANE + names[j], d_gate, 0.0)
+        router = router_ref[rows, :]
+        dot = jnp.sum(router * d_router, axis=1, keepdims=True)
+        d_logits.append(router * (d_router - dot))
+        live = jnp.where(row_of((c.B, 1)) < len_ref[image, x], 1.0, 0.0)
+        lives.append(live)
+        dy_rows.append(cot_ref[rows, :].astype(F32) * live)
+    d_mixed = jnp.concatenate(d_mixed, axis=0)
+    d_logits = jnp.concatenate(d_logits, axis=0)
+    dy_rows = jnp.concatenate(dy_rows, axis=0)
+    logit_rows = jnp.concatenate([vec, jnp.zeros((128 - c.r8, c.D), F32)], axis=0)
+    lane_here = row_of((128, c.D))
+    is_router = jnp.logical_and(lane_here >= LOGIT_LANE, lane_here < LOGIT_LANE + c.E)
+    w_router = jnp.where(is_router, logit_rows, 0.0)
+    high, low = in_parts(d_logits, 2)
+    w_router = w_router.astype(BF16)
+    d_mixed = d_mixed + mm(high, w_router) + mm(low, w_router)
+    router_sum[...] = mm(high, mix_ref[...], TN) + mm(low, mix_ref[...], TN)
+    unit_two, inverse_two = normalize(hid_ref[...])
+    gains_two = jnp.sum(d_mixed * unit_two, axis=0, keepdims=True)
+    biases_two = jnp.sum(d_mixed, axis=0, keepdims=True)
+    d_hidden = dy_rows + normalize_back(d_mixed, unit_two, inverse_two, vec[1:2])
+    dhid[...] = d_hidden
     d_branch = d_hidden.astype(BF16)
-    g_out = mm(att, d_branch, TN)
-    d_att = mm(d_branch, weights[3], NT).astype(BF16)
-    hd = c.D // HEADS
-    qh = q.reshape(c.N, c.B, HEADS, hd)
-    kh = kv[:, :, : c.D].reshape(c.N, c.S, HEADS, hd)
-    vh = kv[:, :, c.D :].reshape(c.N, c.S, HEADS, hd)
-    dh = d_att.reshape(c.N, c.B, HEADS, hd)
-    ein = functools.partial(jnp.einsum, preferred_element_type=F32)
-    at = jnp.arange(c.S, dtype=jnp.int32)
-    key_live = at[None, :] % c.B < lengths[:, at // c.B]
-    scores = jnp.where(key_live[:, None, None, :], ein("iqhd,ikhd->ihqk", qh, kh) * c.scale, -1e30)
-    total = lse[:, :, 0, :].reshape(c.N, c.D // 128, 2, c.B).reshape(c.N, HEADS, c.B, 1)
-    p = jnp.exp(scores - total)
-    dp = ein("iqhd,ikhd->ihqk", dh, vh)
-    ds = (p * (dp - jnp.sum(p * dp, axis=-1, keepdims=True))).astype(BF16)
-    dq = ein("ihqk,ikhd->iqhd", ds, kh) * c.scale
-    dk = ein("ihqk,iqhd->ikhd", ds, qh) * c.scale
-    dv = ein("ihqk,iqhd->ikhd", p.astype(BF16), dh)
-    terms = jnp.concatenate([dk.reshape(c.N, c.S, c.D), dv.reshape(c.N, c.S, c.D)], axis=2)
-    summed = lax.psum_scatter(terms.astype(BF16), "context", scatter_dimension=1, tiled=True)
-    d_proj = jnp.concatenate(
-        [dq.reshape(c.T, c.D).astype(BF16), summed.reshape(c.T, 2 * c.D).astype(BF16)], axis=1
+    dense_start(3, mm(att_ref[...], d_branch, TN))
+    loads[0].wait()
+    datt[...] = mm(d_branch, w_ref[3], NT).astype(BF16)
+    unit_one, inverse_one = normalize(tok_ref[...].astype(F32))
+    norm_t[...] = (unit_one * vec[0:1] + vec[2:3]).astype(BF16).T
+    grads_after_core()
+    loads[1].wait()
+
+    kvcore_ids = [[links.new() for _ in range(2)] for _ in range(c.N)]
+    kvfar_ids = [links.new() for _ in range(c.N)]
+
+    def block_rows(who):
+        return pl.ds(pl.multiple_of(who * c.B, 32), c.B)
+
+    def attend_back(image, first_pair, last_pair):
+        rows = pl.ds(image * c.B, c.B)
+        bias = key_bias(c, len_ref, image)
+
+        def pair_step(pair, carry):
+            lanes = pl.ds(pl.multiple_of(pair * 128, 128), 128)
+            value_lanes = pl.ds(pl.multiple_of(c.D + pair * 128, 128), 128)
+            scale = jnp.asarray(c.scale, BF16)
+            queries = two_heads(q_ref[rows, lanes]) * scale
+            grads = two_heads(datt[rows, lanes])
+            keys = kv_ref[image, :, lanes]
+            probs = jnp.exp(mm(keys, queries, NT) + bias - lse_ref[image, pair][0:1])
+            d_probs = mm(kv_ref[image, :, value_lanes], grads, NT)
+            dot = jnp.sum(probs * d_probs, axis=0, keepdims=True)
+            d_scores = (probs * (d_probs - dot)).astype(BF16)
+            dkv[image, :, value_lanes] = mm(probs.astype(BF16), grads).astype(BF16)
+            dkv[image, :, lanes] = mm(d_scores, queries).astype(BF16)
+            d_queries = mm(keys.T, d_scores).T
+            dproj[rows, lanes] = (one_pair(d_queries) * c.scale).astype(BF16)
+            return carry
+
+        lax.fori_loop(first_pair, last_pair, pair_step, 0)
+
+    def kv_to_core(image):
+        for s in range(2):
+            block = dkv.at[image, block_rows(2 * s + 1 - core), :]
+            go(kvcore_ids[image][s], block, kvcore.at[image, s], core_dev)
+
+    def kv_to_far(image):
+        for s in range(2):
+            got(kvcore_ids[image][s], kvcore.at[image, s], core_dev)
+        rows = block_rows(2 * (1 - side) + core)
+        dkv[image, rows, :] = (
+            dkv[image, rows, :].astype(F32) + kvcore[image, 1 - side].astype(F32)
+        ).astype(BF16)
+        go(kvfar_ids[image], dkv.at[image, rows, :], kvfar.at[image], far_dev)
+
+    def kv_end(image):
+        got(kvfar_ids[image], kvfar.at[image], far_dev)
+        total = dkv[image, block_rows(2 * side + core), :].astype(F32)
+        total = total + kvcore[image, side].astype(F32) + kvfar[image].astype(F32)
+        rows = pl.ds(image * c.B, c.B)
+        dproj[rows, c.D : 3 * c.D] = total.astype(BF16)
+
+    pairs = c.D // 128
+    attend_back(0, 0, pairs)
+    kv_to_core(0)
+    if c.gather:
+        dense_x(3)
+    attend_back(1, 0, pairs // 2)
+    kv_to_far(0)
+    if c.gather:
+        dense_y(3)
+    attend_back(1, pairs // 2, pairs)
+    kv_to_core(1)
+    dense_start(0, mm(norm_t[...], dproj[:, 0 : c.D]))
+    grads_after_y_far()
+    kv_to_far(1)
+    kv_end(0)
+    if c.gather:
+        dense_x(0)
+        dense_z(3)
+    kv_end(1)
+    dense_start(1, mm(norm_t[...], dproj[:, c.D : 2 * c.D]))
+    dense_start(2, mm(norm_t[...], dproj[:, 2 * c.D : 3 * c.D]))
+    if c.gather:
+        dense_y(0)
+        dense_x(1)
+        dense_x(2)
+    d_normed = mm(dproj[:, 0 : c.D], w_ref[0], NT)
+    d_normed = d_normed + mm(dproj[:, c.D : 2 * c.D], w_ref[1], NT)
+    d_normed = d_normed + mm(dproj[:, 2 * c.D : 3 * c.D], w_ref[2], NT)
+    unit_one, inverse_one = normalize(tok_ref[...].astype(F32))
+    gains_one = jnp.sum(d_normed * unit_one, axis=0, keepdims=True)
+    biases_one = jnp.sum(d_normed, axis=0, keepdims=True)
+    small_here = jnp.concatenate([gains_one, gains_two, biases_one, biases_two], axis=0)
+    small_here = jnp.concatenate(
+        [small_here, router_sum[LOGIT_LANE : LOGIT_LANE + c.r8 - 4]], axis=0
     )
-    unit_one, inverse_one = normalize(tok.astype(F32))
-    normed = (unit_one * vec[0] + vec[2]).astype(BF16)
-    g_qkv = mm(normed, d_proj, TN)
-    qkv = jnp.concatenate([weights[0], weights[1], weights[2]], axis=1)
-    d_normed = mm(d_proj, qkv, NT)
-    gains_one, biases_one = jnp.sum(d_normed * unit_one, axis=0), jnp.sum(d_normed, axis=0)
-    g_tok = d_hidden + normalize_back(d_normed, unit_one, inverse_one, vec[0])
-    both = ("expert", "dp")
-    dense = [
-        lax.psum_scatter(g_qkv, both, scatter_dimension=0, tiled=True),
-        lax.psum_scatter(g_out, both, scatter_dimension=0, tiled=True),
-        lax.psum_scatter(g_router, both, scatter_dimension=0, tiled=True),
-        lax.psum_scatter(jnp.stack([gains_one, gains_two]), both, scatter_dimension=1, tiled=True),
-        lax.psum_scatter(jnp.stack([biases_one, biases_two]), both, scatter_dimension=1, tiled=True),
+    if c.gather:
+        small[0] = small_here
+        small_ids = [links.new() for _ in range(3)]
+        small_z = [links.new() for _ in experts]
+        go(small_ids[0], small.at[0], small_in.at[0], core_dev)
+    gtok_ref[...] = dhid[...] + normalize_back(d_normed, unit_one, inverse_one, vec[0:1])
+
+    def block_output():
+        loads[4].wait()
+        for k, (at, device) in enumerate(zip(made_ids, experts), 1):
+            got(at, made.at[:, z ^ k], device)
+        for image in range(c.N):
+            rows = slice(image * c.B, (image + 1) * c.B)
+            meta = meta_ref[rows, :]
+            slots = [meta[:, j : j + 1].astype(jnp.int32) for j in range(2)]
+            at = lane_of((c.B, c.E * c.cap))
+            gates = jnp.where(at == slots[0], meta[:, 4:5], 0.0)
+            gates = gates + jnp.where(at == slots[1], meta[:, 5:6], 0.0)
+            high, low = in_parts(gates, 2)
+            rows_made = made[image].reshape(c.E * c.cap, c.D)
+            mixture = mm(high, rows_made) + mm(low, rows_made)
+            out_ref[rows, :] = (lives[image] * (hid_ref[rows, :] + mixture)).astype(BF16)
+
+    if c.gather:
+
+        def small_step(step, device):
+            source = core_dev if step == 0 else far_dev if step == 1 else y_dev
+            got(small_ids[step], small_in.at[step], source)
+            small[step + 1] = small[step] + small_in[step]
+            if step < 2:
+                go(small_ids[step + 1], small.at[step + 1], small_in.at[step + 1], device)
+
+        small_step(0, far_dev)
+        dense_z(0)
+        dense_share(3)
+        dense_y(1)
+        dense_y(2)
+        small_step(1, y_dev)
+        block_output()
+        small_step(2, None)
+        for k, (at, device) in enumerate(zip(small_z, experts), 1):
+            go(at, small.at[3], small_in.at[3 + z], device)
+        dense_z(1)
+        dense_z(2)
+        dense_cross(3)
+        dense_share(0)
+        dense_end(3)
+        total = small[3]
+        for k, (at, device) in enumerate(zip(small_z, experts), 1):
+            got(at, small_in.at[3 + (z ^ k)], device)
+            total = total + small_in[3 + (z ^ k)]
+        src, dst = row_of((c.D, 128)), lane_of((c.D, 128))
+        pick = jnp.logical_and(dst < c.sh, src == dst + (z * c.Y + y) * c.sh)
+        pick = jnp.where(pick, 1.0, 0.0).astype(BF16)
+        gsmall_ref[...] = sum(mm(part, pick) for part in in_parts(total, 3))
+        dense_cross(0)
+        dense_share(1)
+        dense_share(2)
+        dense_end(0)
+        dense_cross(1)
+        dense_cross(2)
+        grads_end()
+        dense_end(1)
+        dense_end(2)
+    else:
+        gsmall_ref[...] = small_here
+        block_output()
+        grads_end()
+    for copy in ends:
+        copy.wait_send()
+
+
+def run_back(c, tok, cot, lengths, weights, vec, q, kv, lse, att, hid, mix, meta, router, xback, gback, yloc, grads):
+    shape = jax.ShapeDtypeStruct
+    piece = c.FF // 8
+    made = [
+        shape((c.T, c.D), BF16),
+        shape((c.T, c.D), F32),
+        shape((c.D, piece), F32),
+        shape((piece, c.D), F32),
     ]
-    dense = [part.astype(F32) for part in lax.psum([p.astype(BF16) for p in dense], "context")]
-    sums = lax.psum_scatter(grads, ("context", "dp"), scatter_dimension=2, tiled=True).astype(F32)
-    shape = (c.N, c.B, c.D)
+    dense_scratch = []
+    if c.gather:
+        made += [
+            shape((c.sh, 3 * c.D), F32),
+            shape((c.sh, c.D), F32),
+            shape((c.r8, 128), F32),
+        ]
+        half_rows, half_cols = c.sh // 2, c.D // 2
+        dense_scratch = [
+            pltpu.VMEM((4, c.E, c.Y, c.sh, c.D), BF16),
+            pltpu.VMEM((4, c.E, c.Y, c.sh, half_cols), BF16),
+            pltpu.VMEM((4, c.E, c.Y, half_rows, half_cols), BF16),
+            pltpu.VMEM((4, c.E, half_rows, half_cols), BF16),
+            pltpu.VMEM((4, c.E, half_rows, half_cols), BF16),
+            pltpu.VMEM((4, 2, 2, half_rows, half_cols), F32),
+            pltpu.VMEM((4, c.r8, c.D), F32),
+            pltpu.VMEM((3 + c.E, c.r8, c.D), F32),
+        ]
+    else:
+        made += [shape((4, c.D, c.D), BF16), shape((c.r8, c.D), F32)]
+    count = 5 * c.E + 64
+    results = pl.pallas_call(
+        functools.partial(back_kernel, c),
+        out_shape=made,
+        in_specs=[spec(pltpu.SMEM)] + [spec(pltpu.VMEM)] * 12 + [spec(pl.ANY)] * 4,
+        out_specs=[spec(pltpu.VMEM)] * len(made),
+        scratch_shapes=[
+            pltpu.VMEM((4, c.D, c.D), BF16),
+            pltpu.VMEM((c.N, c.S, 2 * c.D), BF16),
+            pltpu.VMEM((c.N, c.E, c.cap, c.D), BF16),
+            pltpu.VMEM((2, 2, c.D, 2 * piece), BF16),
+            pltpu.VMEM((2, 2, c.D, 2 * piece), BF16),
+            pltpu.VMEM((2, 2, c.D, piece), BF16),
+            pltpu.VMEM((2, c.D, piece), BF16),
+            pltpu.VMEM((c.N, c.S, 2 * c.D), BF16),
+            pltpu.VMEM((c.N, 2, c.B, 2 * c.D), BF16),
+            pltpu.VMEM((c.N, c.B, 2 * c.D), BF16),
+            pltpu.VMEM((c.T, 3 * c.D), BF16),
+            pltpu.VMEM((c.T, c.D), BF16),
+            pltpu.VMEM((c.T, c.D), F32),
+            pltpu.VMEM((c.D, c.T), BF16),
+            pltpu.VMEM((128, c.D), F32),
+            *dense_scratch,
+            pltpu.SemaphoreType.DMA((5,)),
+            pltpu.SemaphoreType.DMA((count,)),
+            pltpu.SemaphoreType.DMA((count,)),
+        ],
+        compiler_params=pltpu.CompilerParams(
+            collective_id=2, has_side_effects=True, vmem_limit_bytes=VMEM_LIMIT
+        ),
+        name="back",
+    )(lengths, tok, cot, vec, q, lse, att, hid, mix, meta, router, xback, gback, weights, kv, yloc, grads)
+    out, g_tok, g_in, g_down = results[:4]
+    if c.gather:
+        g_qkv, g_out, small = results[4:]
+        small = small[:, : c.sh]
+    else:
+        dense, small = results[4:]
+        both = ("expert", "dp")
+        flat = dense.astype(F32).transpose(1, 0, 2).reshape(c.D, 4 * c.D)
+        flat = lax.psum_scatter(flat, both, scatter_dimension=0, tiled=True)
+        small = lax.psum_scatter(small, both, scatter_dimension=1, tiled=True)
+        flat, small = lax.psum((flat, small), "context")
+        g_qkv, g_out = flat[:, : 3 * c.D], flat[:, 3 * c.D :]
+    rows = (c.N, c.B, c.D)
     return (
-        out.reshape(shape),
-        g_tok.reshape(shape),
-        *dense,
-        sums[0][None],
-        sums[1].T[None],
+        out.reshape(rows),
+        g_tok.reshape(rows),
+        g_qkv,
+        g_out,
+        small[LOGIT_LANE : LOGIT_LANE + c.E].T,
+        small[0:2],
+        small[2:4],
+        g_in[None],
+        g_down[None],
     )
 
 
@@ -702,7 +1118,7 @@
     front = run_front(c, lengths, tok, route, keep, cot, given)
     weights, vec, q, kv, lse, att, hid, mix, meta, router, send, gsend, dyarr = front
     back = run_experts(c, send, gsend, dyarr, w_expert_in[0], w_expert_down[0])
-    return back_plain(
+    return run_back(
         c, tok, cot, lengths, weights, vec, q, kv, lse, att, hid, mix, meta, router, *back
     )
 

time: 845 us -> 293 us (0.35)
  waiting for transfers between devices: 471 us -> 0 us
  Pallas kernels: 149 us -> 275 us
  local copies, waits for them, and re-layouts: 109 us -> 12.1 us
  matrix products: 49.6 us -> 0 us
  other arithmetic: 30.4 us -> 1.3 us
  between operations: 15 us -> 1.13 us
  starting transfers between devices: 11.1 us -> 0 us
    reduce_scatter x3 -> x0, waiting for transfers between devices: 228 us -> none  [the longest x1 130 us: back_plain(): lax.psum_scatter(g_qkv, both, scatter_dimension=0, tiled=True)]
    unnamed x12 -> x0, waiting for transfers between devices: 214 us -> none
    pallas_call x0 -> x1, Pallas kernels: none -> 126 us  [run_back(): pl.pallas_call(functools.partial(back_kernel, c), out_shape=made, in_spec...]
    dot_general x10 -> x0, matrix products: 47 us -> none  [the longest x4 13.9 us: mm(): return lax.dot_general(left, right, dims, preferred_element_type=F32)]
    unnamed x79 -> x18, local copies, waits for them, and re-layouts: 48.1 us -> 9.45 us
    psum x1 -> x0, waiting for transfers between devices: 29.1 us -> none  [back_plain(): lax.psum([p.astype(BF16) for p in dense], 'context')]
    reshape x6 -> x0, local copies, waits for them, and re-layouts: 16.2 us -> none  [the longest x2 4.49 us: back_plain(): dh = d_att.reshape(c.N, c.B, HEADS, hd)]
    convert_element_type x11 -> x0, other arithmetic: 13.1 us -> none  [the longest x5 5.33 us: back_plain(): part.astype(F32)]
  transfers between devices with their start and end apart: 9 -> 0, of which waited for: 8 -> 0; matrix products, arithmetic and copies ran while one was open for 14% -> 0% of each run, Pallas kernels for 0% -> 0%
where the time goes in v2:
time: 293 us; the launch traced here: 290 us
  Pallas kernels  275 us (94%)
  local copies, waits for them, and re-layouts  12.1 us (4%)
    pallas_call x1, Pallas kernels, run_back(): pl.pallas_call(functools.partial(back_kernel, c), out_shape=made, in_spec...  126 us
    pallas_call x1, Pallas kernels, run_front(): pl.pallas_call(functools.partial(front_kernel, c), out_shape=made, in_spe...  75.9 us
    pallas_call x1, Pallas kernels, run_experts(): pl.pallas_call(functools.partial(expert_kernel, c), out_shape=[shape((c.N...  72.9 us
    unnamed x18, local copies, waits for them, and re-layouts  9.45 us

profile of v2, /device:TPU:0, one launch (start us, length us, event | category | flops | bytes accessed | tf_op | source)
XLA Modules:
  0.0 289.6 jit_solution(9617985138559309213)
XLA Ops:
  0.6 1.3 fusion.5.refs_7_
  1.9 1.5 copy.21
  3.4 1.5 copy.22
  4.9 75.9 %front.1 = (bf16[4,768,768]{2,1,0:T(8,128)(2,1)}, f32[8,768]{1,0:T(8,128)}, bf16[320,768]{1,0:T(8,128)(2,1)}, bf16[2,640,1536]{2,1,0:T(8,128)(2,1)}, f32[2,6,8,3...) custom-call(s32[2,4]{1,0:T(2,128)} %refs_0_.3, ...), custom_call_target="tpu_custom_call" | custom-call | tf_op jit(solution)/shard_map/front/pallas_call | solution.py:385
  80.9 72.9 %experts.1 = (bf16[2,4,128,768]{3,2,1,0:T(8,128)(2,1)}, f32[4,8,128]{2,1,0:T(8,128)}, bf16[4,2,128,768]{3,2,1,0:T(8,128)(2,1)}, bf16[2,768,3072]{2,1,0:T(8,128)(2,1)}) custom-call(bf16[2,4,128,768]{3,2,1,0:T(8,128)(2,1)} %get-tuple-element.41.send_ref, f32[4,8,128]{2,1,0:T(8,128)} %get-tuple-element.42.gsend_ref, ...), custom_call_target="tpu_custom_call" | custom-call | tf_op jit(solution)/shard_map/experts/pallas_call | solution.py:538
  153.8 126.2 %back.1 = (bf16[320,768]{1,0:T(8,128)(2,1)}, f32[320,768]{1,0:T(8,128)}, f32[768,384]{1,0:T(8,128)}, f32[384,768]{1,0:T(8,128)}, f32[96,2304]{1,0:T(8,128)}, /*index=5*/f32[96,768]{1,0:T(8,128)}, f32[8,128]{1,0:T(8,128)}) custom-call(s32[2,4]{1,0:T(2,128)} %refs_0_.3, bf16[320,768]{1,0:T(8,128)(2,1)} %bitcast.16, bf16[320,768]{1,0:T(8,128)(2,1)} %bitcast.18, ...), custom_call_target="tpu_custom_call" | custom-call | tf_op jit(solution)/shard_map/back/pallas_call | solution.py:1007
  280.0 0.0 copy-start.2
  280.0 0.0 copy-start.3
  280.0 1.4 slice_bitcast_fusion
  281.4 1.3 fusion.6
  282.7 1.8 copy.29
  284.6 0.0 copy-done.2
  284.6 0.0 copy-start.4
  284.6 0.9 copy.30
  285.5 0.0 copy-done.3
  285.5 0.0 copy-start.1
  285.5 0.9 copy.31
  286.4 0.0 copy-done.4
  286.4 0.0 copy-start
  286.4 0.7 copy.32
  287.2 0.0 copy-done.1
  287.2 1.0 copy.33
  288.2 0.0 copy-done
  288.2 1.0 copy.34
Async XLA Ops:
  280.0 4.6 %copy-start.2 = (f32[320,768]{1,0:T(8,128)S(1)}, f32[320,768]{1,0:T(8,128)}, u32[]{:S(2)}) copy-start(f32[320,768]{1,0:T(8,128)} %get-tuple-element.51) | copy-start | bytes 2949124
  280.0 5.5 %copy-start.3 = (f32[96,2304]{1,0:T(8,128)S(1)}, f32[96,2304]{1,0:T(8,128)}, u32[]{:S(2)}) copy-start(f32[96,2304]{1,0:T(8,128)} %get-tuple-element.70) | copy-start | bytes 2654212
  284.6 1.9 copy-start.4
  285.5 1.6 copy-start.1
  286.4 1.7 copy-start

commit v3 on v2

--- a/solution.py
+++ b/solution.py
@@ -105,18 +105,93 @@
     return jnp.where(first, stacked[:half], stacked[half:])
 
 
+class Gather:
+    def __init__(self, c, links, w_ref, rows_of, z, y, own_part, other_part):
+        self.c, self.links, self.w_ref, self.rows_of = c, links, w_ref, rows_of
+        self.z, self.y, self.own_part, self.other_part = z, y, own_part, other_part
+        span = range(c.E)
+        self.up = [links.new() for _ in span]
+        self.down = [links.new() for _ in span]
+        self.y_up = [links.new() for _ in span]
+        self.y_down = [links.new() for _ in span]
+        self.core_up = [[links.new() for _ in span] for _ in range(2)]
+        self.core_down = [[links.new() for _ in span] for _ in range(2)]
+        self.sent = []
+
+    def route(self, above, below, y_dev, core_dev):
+        self.above, self.below, self.y_dev, self.core_dev = above, below, y_dev, core_dev
+
+    def unit(self, at, z_at, y_at, device, part=None):
+        ref = self.w_ref.at[self.own_part if part is None else part, self.rows_of(z_at, y_at), :]
+        return self.links.make(at, ref, ref, device)
+
+    def send(self, condition, *where):
+        pl.when(condition)(lambda: self.unit(*where).start())
+        self.sent.append((condition, where))
+
+    def got(self, condition, at, z_at, y_at, part=None):
+        pl.when(condition)(lambda: self.unit(at, z_at, y_at, self.core_dev, part).wait_recv())
+
+    def open(self):
+        z, y = self.z, self.y
+        self.send(z < self.c.E - 1, self.up[1], z, y, self.above)
+        self.send(z > 0, self.down[1], z, y, self.below)
+        self.send(z >= 0, self.y_up[0], z, y, self.y_dev)
+
+    def pass_y(self, j):
+        z, y = self.z, 1 - self.y
+        lower, upper = z >= j, z + j <= self.c.E - 1
+        self.got(lower, self.y_up[j], z - j, y)
+        self.send(lower, self.core_up[1][j], z - j, y, self.core_dev)
+        if j:
+            self.got(upper, self.y_down[j], z + j, y)
+            self.send(upper, self.core_down[1][j], z + j, y, self.core_dev)
+
+    def step(self, j):
+        z, y, last = self.z, self.y, self.c.E - 1
+        if j <= last:
+            lower, upper = z >= j, z + j <= last
+            self.got(lower, self.up[j], z - j, y)
+            if j < last:
+                self.send(jnp.logical_and(lower, z < last), self.up[j + 1], z - j, y, self.above)
+            self.send(lower, self.y_up[j], z - j, y, self.y_dev)
+            self.send(lower, self.core_up[0][j], z - j, y, self.core_dev)
+            self.got(upper, self.down[j], z + j, y)
+            if j < last:
+                self.send(jnp.logical_and(upper, z > 0), self.down[j + 1], z + j, y, self.below)
+            self.send(upper, self.y_down[j], z + j, y, self.y_dev)
+            self.send(upper, self.core_down[0][j], z + j, y, self.core_dev)
+        self.pass_y(j - 1)
+
+    def finish(self):
+        z, last = self.z, self.c.E - 1
+        for side in range(2):
+            y = self.y if side == 0 else 1 - self.y
+            if side:
+                self.got(z >= 0, self.core_up[1][0], z, y, self.other_part)
+            for j in range(1, self.c.E):
+                self.got(z >= j, self.core_up[side][j], z - j, y, self.other_part)
+                self.got(z + j <= last, self.core_down[side][j], z + j, y, self.other_part)
+
+    def close(self):
+        for condition, where in self.sent:
+            pl.when(condition)(lambda: self.unit(*where).wait_send())
+
+
 def front_kernel(c, *refs):
     refs = list(refs)
     take = lambda count: [refs.pop(0) for _ in range(count)]
     len_ref, tok_ref, route_ref, keep_ref, cot_ref = take(5)
     if c.gather:
         wqkv_ref, wout_ref, small_ref = take(3)
-        w_ref, vec_ref = take(2)
+        w_hbm, vec_ref = take(2)
     else:
         w_ref, vec_ref = take(2)
-    q_ref, kv_ref, lse_ref, att_ref, hid_ref, mix_ref, meta_ref, router_ref = take(8)
+    q_ref, kv_hbm, lse_ref, att_ref, hid_ref, mix_ref, meta_ref, router_ref = take(8)
     send_ref, gsend_ref, dyarr_ref = take(3)
-    smalls, dysend, norm_ref, ssem, rsem = take(5)
+    if c.gather:
+        smalls, w_ref = take(2)
+    kv_ref, dysend, norm_ref, lsem, ssem, rsem = take(6)
     links = Links(ssem, rsem)
     z, x, y = lax.axis_index("expert"), lax.axis_index("context"), lax.axis_index("dp")
     core = lax.rem(x, 2)
@@ -146,45 +221,25 @@
             w_ref[part, own_rows, :] = wqkv_ref[:, part * c.D : (part + 1) * c.D]
         w_ref[3, own_rows, :] = wout_ref[...]
 
-        def unit(z_at, y_at):
-            return w_ref.at[pl.ds(2 * core, 2), rows_of(z_at, y_at), :]
-
-        def other_unit(z_at, y_at):
-            return w_ref.at[pl.ds(2 - 2 * core, 2), rows_of(z_at, y_at), :]
-
-        up = [links.new() for _ in range(c.E)]
-        down = [links.new() for _ in range(c.E)]
-        y_up = [links.new() for _ in range(c.E)]
-        y_down = [links.new() for _ in range(c.E)]
-        core_up = [[links.new() for _ in range(c.E)] for _ in range(2)]
-        core_down = [[links.new() for _ in range(c.E)] for _ in range(2)]
         above, below = (lax.rem(z + 1, c.E), x, y), (lax.rem(z + c.E - 1, c.E), x, y)
-
-        def copy_of(at, z_at, y_at, device):
-            return links.make(at, unit(z_at, y_at), unit(z_at, y_at), device)
-
-        pending = []
-
-        def send_if(condition, at, z_at, y_at, device):
-            pl.when(condition)(lambda: copy_of(at, z_at, y_at, device).start())
-            pending.append((condition, at, z_at, y_at, device))
-
-        always = z >= 0
-        send_if(z < c.E - 1, up[1], z, y, above)
-        send_if(z > 0, down[1], z, y, below)
-        send_if(always, y_up[0], z, y, y_dev)
+        stages = [Gather(c, links, w_ref, rows_of, z, y, *parts) for parts in (
+            (1 + core, 2 - core), (3 * core, 3 - 3 * core))]
+        for stage in stages:
+            stage.route(above, below, y_dev, core_dev)
+        stages[0].open()
 
     unit_rows = [None] * c.N
     choices = []
     for image in range(c.N):
         rows = slice(image * c.B, (image + 1) * c.B)
-        names = route_ref[rows, :]
         live = jnp.where(row_of((c.B, 1)) < len_ref[image, x], 1.0, 0.0)
-        kept = keep_ref[rows, :].astype(F32) * live
-        first, second = names[:, 0:1], names[:, 1:2]
+        kept = [to_column(keep_ref[image, j : j + 1, :].astype(F32)) * live for j in range(2)]
+        first, second = [
+            to_column(route_ref[image, j : j + 1, :].astype(F32)).astype(jnp.int32) for j in range(2)
+        ]
         lane = lane_of((c.B, 128))
-        named = jnp.where(lane == first, kept[:, 0:1], 0.0) + jnp.where(
-            lane == second, kept[:, 1:2], 0.0
+        named = jnp.where(lane == first, kept[0], 0.0) + jnp.where(
+            lane == second, kept[1], 0.0
         )
         earlier = jnp.where(lane_of((c.B, c.B)) < row_of((c.B, c.B)), 1.0, 0.0).astype(BF16)
         rank = mm(earlier, named.astype(BF16))
@@ -193,13 +248,12 @@
         slot_first = first * c.cap + rank_first.astype(jnp.int32)
         slot_second = second * c.cap + rank_second.astype(jnp.int32)
         at = lane_of((c.B, c.E * c.cap))
-        place = jnp.where(at == slot_first, kept[:, 0:1], 0.0) + jnp.where(
-            at == slot_second, kept[:, 1:2], 0.0
+        place = jnp.where(at == slot_first, kept[0], 0.0) + jnp.where(
+            at == slot_second, kept[1], 0.0
         )
         place = place.astype(BF16)
         choices.append((first, second, kept, slot_first, slot_second, place))
         dysend[image] = mm(place, cot_ref[rows, :], TN).astype(BF16).reshape(c.E, c.cap, c.D)
-        dyarr_ref[z, image] = dysend[image, z]
 
     if c.gather:
         for at, device in zip(small_ids, plane):
@@ -218,46 +272,11 @@
         norm_ref[rows, :] = (unit_one * vec[0:1] + vec[2:3]).astype(BF16)
 
     if c.gather:
-
-        def got(at, z_at, y_at):
-            copy_of(at, z_at, y_at, core_dev).wait_recv()
-
-        def pass_y(at, z_at, core_at, condition):
-            pl.when(condition)(lambda: got(at, z_at, 1 - y))
-            send_if(condition, core_at, z_at, 1 - y, core_dev)
-
-        for j in range(1, c.E):
-            lower, upper = z >= j, z + j <= c.E - 1
-            pl.when(lower)(lambda: got(up[j], z - j, y))
-            if j < c.E - 1:
-                send_if(jnp.logical_and(lower, z < c.E - 1), up[j + 1], z - j, y, above)
-            send_if(lower, y_up[j], z - j, y, y_dev)
-            send_if(lower, core_up[0][j], z - j, y, core_dev)
-            pl.when(upper)(lambda: got(down[j], z + j, y))
-            if j < c.E - 1:
-                send_if(jnp.logical_and(upper, z > 0), down[j + 1], z + j, y, below)
-            send_if(upper, y_down[j], z + j, y, y_dev)
-            send_if(upper, core_down[0][j], z + j, y, core_dev)
-            if j == 1:
-                pass_y(y_up[0], z, core_up[1][0], always)
-            else:
-                pass_y(y_up[j - 1], z - j + 1, core_up[1][j - 1], z >= j - 1)
-                pass_y(y_down[j - 1], z + j - 1, core_down[1][j - 1], z + j - 1 <= c.E - 1)
-        last = c.E - 1
-        pass_y(y_up[last], z - last, core_up[1][last], z >= last)
-        pass_y(y_down[last], z + last, core_down[1][last], z + last <= c.E - 1)
-
-        def got_core(at, z_at, y_at):
-            there = other_unit(z_at, y_at)
-            links.make(at, there, there, core_dev).wait_recv()
-
-        for side in range(2):
-            y_at = y if side == 0 else 1 - y
-            if side:
-                got_core(core_up[side][0], z, y_at)
-            for j in range(1, c.E):
-                pl.when(z >= j)(lambda: got_core(core_up[side][j], z - j, y_at))
-                pl.when(z + j <= c.E - 1)(lambda: got_core(core_down[side][j], z + j, y_at))
+        stages[0].step(1)
+        stages[1].open()
+        for j in range(2, c.E + 1):
+            stages[0].step(j)
+        stages[0].finish()
 
     normed = norm_ref[...]
     own_at = pl.ds(pl.multiple_of(x * c.B, 32), c.B)
@@ -271,9 +290,19 @@
         block = kv_ref.at[image, own_at, :]
         go(kv_ids[image][0], block, block, far_dev)
         go(kv_ids[image][1], block, block, core_dev)
+    if c.gather:
+        for j in range(1, c.E + 1):
+            stages[1].step(j)
     dy_ids = [links.new() for _ in experts]
     for k, (at, device) in enumerate(zip(dy_ids, experts), 1):
         go(at, dysend.at[:, z ^ k], dyarr_ref.at[z], device)
+    own_dy = pltpu.make_async_copy(dysend.at[:, z], dyarr_ref.at[z], lsem.at[0])
+    own_dy.start()
+    leaving = [own_dy]
+    if c.gather:
+        stages[1].finish()
+        leaving.append(pltpu.make_async_copy(w_ref, w_hbm, lsem.at[1]))
+        leaving[-1].start()
     q_ref[...] = mm(normed, w_ref[0]).astype(BF16)
 
     block_of = lambda image, who: kv_ref.at[image, pl.ds(pl.multiple_of(who * c.B, 32), c.B), :]
@@ -287,6 +316,8 @@
         links.make(kv_ids[image][1], near_block, near_block, core_dev).wait_recv()
         cross_block = block_of(image, x ^ 3)
         links.make(kv_ids[image][2], cross_block, cross_block, core_dev).wait_recv()
+        leaving.append(pltpu.make_async_copy(kv_ref.at[image], kv_hbm.at[image], lsem.at[2 + image]))
+        leaving[-1].start()
         bias = key_bias(c, len_ref, image)
 
         def pair_step(pair, carry):
@@ -325,10 +356,10 @@
         rows = slice(image * c.B, (image + 1) * c.B)
         first, second, kept, slot_first, slot_second, place = choices[image]
         here = router[rows]
-        gate_first = kept[:, 0:1] * jnp.sum(
+        gate_first = kept[0] * jnp.sum(
             jnp.where(lane == LOGIT_LANE + first, here, 0.0), axis=1, keepdims=True
         )
-        gate_second = kept[:, 1:2] * jnp.sum(
+        gate_second = kept[1] * jnp.sum(
             jnp.where(lane == LOGIT_LANE + second, here, 0.0), axis=1, keepdims=True
         )
         send_ref[image] = mm(place, mixed[rows], TN).astype(BF16).reshape(c.E, c.cap, c.D)
@@ -340,8 +371,8 @@
         columns = (
             slot_first.astype(F32),
             slot_second.astype(F32),
-            kept[:, 0:1],
-            kept[:, 1:2],
+            kept[0],
+            kept[1],
             gate_first,
             gate_second,
             first.astype(F32),
@@ -354,11 +385,13 @@
 
     for k, (at, device) in enumerate(zip(dy_ids, experts), 1):
         links.make(at, dyarr_ref.at[z ^ k], dyarr_ref.at[z ^ k], device).wait_recv()
+    for copy in leaving:
+        copy.wait()
     for copy in ends:
         copy.wait_send()
     if c.gather:
-        for condition, at, z_at, y_at, device in pending:
-            pl.when(condition)(lambda: copy_of(at, z_at, y_at, device).wait_send())
+        for stage in stages:
+            stage.close()
 
 
 def spec(space):
@@ -381,16 +414,27 @@
         shape((c.E, 8, c.cap), F32),
         shape((c.E, c.N, c.cap, c.D), BF16),
     ]
-    count = 96 if c.gather else 2 * c.E + 16
+    count = 112 if c.gather else 2 * c.E + 16
+    places = [spec(pltpu.VMEM)] * len(made)
+    places[-1] = places[-10] = spec(pl.ANY)
+    gather_scratch = []
+    if c.gather:
+        places[0] = spec(pl.ANY)
+        gather_scratch = [
+            pltpu.VMEM((c.E * c.Y, c.r8, 128), F32),
+            pltpu.VMEM((4, c.D, c.D), BF16),
+        ]
     out = pl.pallas_call(
         functools.partial(front_kernel, c),
         out_shape=made,
         in_specs=[spec(pltpu.SMEM)] + [spec(pltpu.VMEM)] * (4 + len(weights)),
-        out_specs=[spec(pltpu.VMEM)] * len(made),
-        scratch_shapes=[
-            pltpu.VMEM((c.E * c.Y, c.r8, 128), F32),
+        out_specs=places,
+        scratch_shapes=gather_scratch
+        + [
+            pltpu.VMEM((c.N, c.S, 2 * c.D), BF16),
             pltpu.VMEM((c.N, c.E, c.cap, c.D), BF16),
             pltpu.VMEM((c.T, c.D), BF16),
+            pltpu.SemaphoreType.DMA((2 + c.N,)),
             pltpu.SemaphoreType.DMA((count,)),
             pltpu.SemaphoreType.DMA((count,)),
         ],
@@ -420,7 +464,8 @@
     xback_ref,
     gback_ref,
     yloc_ref,
-    grad_ref,
+    grad_hbm,
+    gnext_hbm,
     win,
     wdown,
     arr,
@@ -431,6 +476,9 @@
     dxs,
     dgs,
     turned,
+    gsend,
+    grecv,
+    gown,
     wsem,
     ssem,
     rsem,
@@ -442,7 +490,7 @@
     load_down = pltpu.make_async_copy(wdown_hbm, wdown, wsem.at[1])
     load_in.start()
     load_down.start()
-    greet(experts)
+    greet(experts + [(z, x ^ 1, y), (z, x ^ 2, y), (z, x, 1 - y)])
     ids = [[links.new() for _ in range(4)] for _ in range(c.E)]
     ends = []
 
@@ -451,18 +499,32 @@
         copy.start()
         ends.append(copy)
 
-    for k in range(1, c.E):
-        go(ids[k][0], send_ref.at[:, z ^ k], arr.at[z], experts[k - 1])
-        go(ids[k][1], gsend_ref.at[z ^ k], garr.at[z], experts[k - 1])
+    group = c.E // c.chunks
+    height = group * c.N * c.cap
+
+    def dispatch(g):
+        started = len(ends)
+        for k in range(max(1, g * group), (g + 1) * group):
+            go(ids[k][1], gsend_ref.at[z ^ k], garr.at[z], experts[k - 1])
+            go(ids[k][0], send_ref.at[:, z ^ k], arr.at[z], experts[k - 1])
+        return ends[started:]
+
+    dispatch(0)
+    early = dispatch(c.chunks - 2)
+    for g in range(1, c.chunks - 2):
+        dispatch(g)
     for image in range(c.N):
         arr[z, image] = send_ref[image, z]
     garr[z] = gsend_ref[z]
     load_in.wait()
     load_down.wait()
     dgs[...] = jnp.zeros_like(dgs)
-    group = c.E // c.chunks
-    height = group * c.N * c.cap
     for g in range(c.chunks):
+        if g == 1:
+            for copy in early:
+                copy.wait_send()
+            ends[:] = [copy for copy in ends if all(copy is not other for other in early)]
+            dispatch(c.chunks - 1)
         slab = lax.div(z, group) ^ g
         for k in range(g * group, (g + 1) * group):
             if k:
@@ -516,13 +578,50 @@
     turned[0] = arr[...].reshape(total, c.D).T
     turned[1] = dout_all[...].T
 
-    def grad_step(step, carry):
-        lanes = pl.ds(pl.multiple_of(step * c.FB, 128), c.FB)
-        grad_ref[0, :, lanes] = mm(turned[0], dpre_all[:, lanes]).astype(BF16)
-        grad_ref[1, :, lanes] = mm(turned[1], act_all[:, lanes]).astype(BF16)
-        return carry
-
-    lax.fori_loop(0, c.FF // c.FB, grad_step, 0)
+    core = lax.rem(x, 2)
+    core_dev, far_dev, y_dev = (z, x ^ 1, y), (z, x ^ 2, y), (z, x, 1 - y)
+    half = c.FF // 4
+    grad_ids = [[links.new() for _ in range(2)] for _ in range(2)]
+    sources = (dpre_all, act_all)
+
+    def blocks(which, owner, into):
+        def block_step(part, carry):
+            lanes = pl.ds(pl.multiple_of((2 * part + owner) * half, 128), half)
+            into[part, which] = mm(turned[which], sources[which][:, lanes]).astype(BF16)
+            return carry
+
+        lax.fori_loop(0, 2, block_step, 0)
+
+    piece = half // 2
+    side = lax.div(x, 2)
+    other_piece = pl.ds(pl.multiple_of((1 - y) * piece, 128), piece)
+    next_ids = [links.new() for _ in range(2)]
+    leaving = []
+    for which in range(2):
+        blocks(which, 1 - core, gsend)
+        for part in range(2):
+            go(grad_ids[which][part], gsend.at[part, which], grecv.at[part, which], core_dev)
+        blocks(which, core, gown)
+        for part in range(2):
+            there = grecv.at[part, which]
+            links.make(grad_ids[which][part], there, there, core_dev).wait_recv()
+            gown[part, which] = (
+                gown[part, which].astype(F32) + grecv[part, which].astype(F32)
+            ).astype(BF16)
+        first = gown.at[1 - side, which, :, other_piece]
+        go(next_ids[which], first, gnext_hbm.at[which], y_dev if which == 0 else far_dev)
+        for part in range(2):
+            leaving.append(
+                pltpu.make_async_copy(
+                    gown.at[part, which], grad_hbm.at[part, which], wsem.at[2 + 2 * which + part]
+                )
+            )
+            leaving[-1].start()
+    for which in range(2):
+        there = gnext_hbm.at[which]
+        links.make(next_ids[which], there, there, core_dev).wait_recv()
+    for copy in leaving:
+        copy.wait()
     for k in range(1, c.E):
         there = z ^ k
         links.make(ids[k][2], xback_ref.at[:, there], xback_ref.at[:, there], experts[k - 1]).wait_recv()
@@ -534,17 +633,18 @@
 def run_experts(c, send, gsend, dyarr, w_in, w_down):
     shape = jax.ShapeDtypeStruct
     total = c.E * c.N * c.cap
-    count = 4 * c.E
+    count = 4 * c.E + 6
     return pl.pallas_call(
         functools.partial(expert_kernel, c),
         out_shape=[
             shape((c.N, c.E, c.cap, c.D), BF16),
             shape((c.E, 8, c.cap), F32),
             shape((c.E, c.N, c.cap, c.D), BF16),
-            shape((2, c.D, c.FF), BF16),
+            shape((2, 2, c.D, c.FF // 4), BF16),
+            shape((2, c.D, c.FF // 8), BF16),
         ],
         in_specs=[spec(pltpu.VMEM)] * 3 + [spec(pl.ANY)] * 2,
-        out_specs=[spec(pltpu.VMEM)] * 4,
+        out_specs=[spec(pltpu.VMEM)] * 3 + [spec(pl.ANY)] * 2,
         scratch_shapes=[
             pltpu.VMEM((c.D, c.FF), BF16),
             pltpu.VMEM((c.FF, c.D), BF16),
@@ -556,7 +656,10 @@
             pltpu.VMEM((c.E, c.N, c.cap, c.D), BF16),
             pltpu.VMEM((c.E, 8, c.cap), F32),
             pltpu.VMEM((2, c.D, total), BF16),
-            pltpu.SemaphoreType.DMA((2,)),
+            pltpu.VMEM((2, 2, c.D, c.FF // 4), BF16),
+            pltpu.VMEM((2, 2, c.D, c.FF // 4), BF16),
+            pltpu.VMEM((2, 2, c.D, c.FF // 4), BF16),
+            pltpu.SemaphoreType.DMA((6,)),
             pltpu.SemaphoreType.DMA((count,)),
             pltpu.SemaphoreType.DMA((count,)),
         ],
@@ -580,17 +683,16 @@
     take = lambda count: [refs.pop(0) for _ in range(count)]
     len_ref, tok_ref, cot_ref, vec_ref, q_ref, lse_ref, att_ref, hid_ref, mix_ref = take(9)
     meta_ref, router_ref, xback_ref, gback_ref = take(4)
-    w_hbm, kv_hbm, yloc_hbm, grad_hbm = take(4)
-    out_ref, gtok_ref, gin_ref, gdown_ref = take(4)
-    if c.gather:
-        gqkv_ref, gout_ref, gsmall_ref = take(3)
+    w_hbm, kv_hbm, yloc_hbm, grad_hbm, gnext_hbm = take(5)
+    gtok_hbm, made, gy, gx = take(4)
+    if c.gather:
+        whole, gsmall_ref = take(2)
     else:
         dd, gsmall_ref = take(2)
-    w_ref, kv_ref, made = take(3)
-    gsum, gcore, gy, gx = take(4)
+    w_ref, kv_ref, gtok_ref, gpart, gnext = take(5)
     dkv, kvcore, kvfar, dproj, datt, dhid, norm_t, router_sum = take(8)
     if c.gather:
-        dd, dcore, done_x, done_y, done_z, whole, small, small_in = take(8)
+        dd, dcore, done_x, done_y, done_z, small, small_in = take(7)
     lsem, ssem, rsem = take(3)
     links = Links(ssem, rsem)
     z, x, y = lax.axis_index("expert"), lax.axis_index("context"), lax.axis_index("dp")
@@ -613,13 +715,16 @@
         pltpu.make_async_copy(w_hbm, w_ref, lsem.at[0]),
         pltpu.make_async_copy(kv_hbm, kv_ref, lsem.at[1]),
     ]
-    own_start = pl.multiple_of(core * half, 128)
-    for part in range(2):
-        columns = pl.ds(pl.multiple_of(part * 2 * half + own_start, 128), half)
+    own_piece = pl.ds(pl.multiple_of(y * piece, 128), piece)
+    other_piece = pl.ds(pl.multiple_of((1 - y) * piece, 128), piece)
+    parts = (grad_hbm.at[1 - side, 0, :, own_piece], grad_hbm.at[side, 1, :, other_piece])
+    for which in range(2):
+        loads.append(pltpu.make_async_copy(parts[which], gpart.at[which], lsem.at[2 + which]))
         loads.append(
-            pltpu.make_async_copy(grad_hbm.at[:, :, columns], gsum.at[part], lsem.at[2 + part])
+            pltpu.make_async_copy(gnext_hbm.at[which], gnext.at[which], lsem.at[6 + which])
         )
-    loads.append(pltpu.make_async_copy(yloc_hbm.at[z], made.at[:, z], lsem.at[4]))
+    own_made = pltpu.make_async_copy(yloc_hbm.at[z], made.at[:, z], lsem.at[4])
+    loads.append(own_made)
     for load in loads:
         load.start()
     greet([core_dev, far_dev, y_dev] + experts)
@@ -627,136 +732,75 @@
     made_ids = [links.new() for _ in experts]
     for k, (at, device) in enumerate(zip(made_ids, experts), 1):
         go(at, yloc_hbm.at[z ^ k], made.at[:, z], device)
-    gcore_ids = [[links.new() for _ in range(2)] for _ in range(2)]
-    other_start = (1 - core) * half
-    for part in range(2):
-        columns = pl.ds(pl.multiple_of(part * 2 * half + other_start, 128), half)
-        for which in range(2):
-            go(
-                gcore_ids[part][which],
-                grad_hbm.at[which, :, columns],
-                gcore.at[part, which],
-                core_dev,
-            )
-    gy_ids = [[links.new() for _ in range(2)] for _ in range(2)]
+    gy_ids = [links.new() for _ in range(2)]
     gx_ids = [links.new() for _ in range(2)]
-    own_piece = pl.ds(pl.multiple_of(y * piece, 128), piece)
-    other_piece = pl.ds(pl.multiple_of((1 - y) * piece, 128), piece)
-
-    def grads_after_core():
-        loads[2].wait()
-        loads[3].wait()
-        for order in range(2):
-            part = 1 - side if order == 0 else side
-            for which in range(2):
-                for p in range(2):
-                    if order == 0:
-                        got(gcore_ids[p][which], gcore.at[p, which], core_dev)
-                gsum[part, which] = (
-                    gsum[part, which].astype(F32) + gcore[part, which].astype(F32)
-                ).astype(BF16)
-                go(
-                    gy_ids[order][which],
-                    gsum.at[part, which, :, other_piece],
-                    gy.at[order, which],
-                    y_dev,
-                )
-
-    def grads_after_y_far():
-        part = 1 - side
-        for which in range(2):
-            got(gy_ids[0][which], gy.at[0, which], y_dev)
-            gsum[part, which, :, own_piece] = (
-                gsum[part, which, :, own_piece].astype(F32) + gy[0, which].astype(F32)
-            ).astype(BF16)
-            go(gx_ids[which], gsum.at[part, which, :, own_piece], gx.at[which], far_dev)
+    go(gy_ids[0], grad_hbm.at[side, 0, :, other_piece], gy.at[0], y_dev)
+    go(gx_ids[1], grad_hbm.at[1 - side, 1, :, own_piece], gx.at[1], far_dev)
+    for which in range(2):
+        loads[2 + 2 * which].wait()
+        loads[3 + 2 * which].wait()
+        gpart[which] = (gpart[which].astype(F32) + gnext[which].astype(F32)).astype(BF16)
+        if which == 0:
+            go(gx_ids[0], gpart.at[0], gx.at[0], far_dev)
+        else:
+            go(gy_ids[1], gpart.at[1], gy.at[1], y_dev)
 
     def grads_end():
         for which in range(2):
-            got(gy_ids[1][which], gy.at[1, which], y_dev)
+            got(gy_ids[which], gy.at[which], y_dev)
             got(gx_ids[which], gx.at[which], far_dev)
-            total = gsum[side, which, :, own_piece].astype(F32) + gy[1, which].astype(F32)
-            total = total + gx[which].astype(F32)
-            if which == 0:
-                gin_ref[...] = total
-            else:
-                gdown_ref[...] = total.T
 
     if c.gather:
         n_dense = 4
         core_cols = c.D // 2
         keep_cols = pl.ds(pl.multiple_of(core * core_cols, 128), core_cols)
         give_cols = pl.ds(pl.multiple_of((1 - core) * core_cols, 128), core_cols)
-        rows_half = c.sh // 2
-        keep_rows = pl.ds(pl.multiple_of(side * rows_half, 16), rows_half)
-        give_rows = pl.ds(pl.multiple_of((1 - side) * rows_half, 16), rows_half)
         ids_core = [links.new() for _ in range(n_dense)]
         ids_x = [links.new() for _ in range(n_dense)]
         ids_y = [links.new() for _ in range(n_dense)]
         ids_z = [[links.new() for _ in experts] for _ in range(n_dense)]
-        ids_far = [links.new() for _ in range(n_dense)]
         ids_own = [links.new() for _ in range(n_dense)]
-        ids_cross = [links.new() for _ in range(n_dense)]
 
         def dense_start(m, value):
             dd[m] = value.astype(BF16).reshape(c.E, c.Y, c.sh, c.D)
             go(ids_core[m], dd.at[m, :, :, :, give_cols], dcore.at[m], core_dev)
 
-        def dense_x(m):
+        def dense_y(m):
             got(ids_core[m], dcore.at[m], core_dev)
             dd[m, :, :, :, keep_cols] = (
                 dd[m, :, :, :, keep_cols].astype(F32) + dcore[m].astype(F32)
             ).astype(BF16)
-            go(ids_x[m], dd.at[m, :, :, give_rows, keep_cols], done_x.at[m], far_dev)
-
-        def dense_y(m):
-            got(ids_x[m], done_x.at[m], far_dev)
-            dd[m, :, :, keep_rows, keep_cols] = (
-                dd[m, :, :, keep_rows, keep_cols].astype(F32) + done_x[m].astype(F32)
-            ).astype(BF16)
-            go(ids_y[m], dd.at[m, :, 1 - y, keep_rows, keep_cols], done_y.at[m], y_dev)
+            go(ids_y[m], dd.at[m, :, 1 - y, :, keep_cols], done_y.at[m], y_dev)
 
         def dense_z(m):
             got(ids_y[m], done_y.at[m], y_dev)
-            dd[m, :, y, keep_rows, keep_cols] = (
-                dd[m, :, y, keep_rows, keep_cols].astype(F32) + done_y[m].astype(F32)
+            dd[m, :, y, :, keep_cols] = (
+                dd[m, :, y, :, keep_cols].astype(F32) + done_y[m].astype(F32)
             ).astype(BF16)
             for k, device in enumerate(experts, 1):
                 go(
                     ids_z[m][k - 1],
-                    dd.at[m, z ^ k, y, keep_rows, keep_cols],
+                    dd.at[m, z ^ k, y, :, keep_cols],
                     done_z.at[m, z],
                     device,
                 )
 
-        def dense_share(m):
-            total = dd[m, z, y, keep_rows, keep_cols].astype(F32)
+        def dense_x(m):
+            total = dd[m, z, y, :, keep_cols].astype(F32)
             for k, device in enumerate(experts, 1):
                 got(ids_z[m][k - 1], done_z.at[m, z ^ k], device)
                 total = total + done_z[m, z ^ k].astype(F32)
-            whole[m, side, core] = total
-            own = whole.at[m, side, core]
-            go(ids_far[m], own, own, far_dev)
-            go(ids_own[m], own, own, core_dev)
-
-        def dense_cross(m):
-            there = whole.at[m, 1 - side, core]
-            got(ids_far[m], there, far_dev)
-            go(ids_cross[m], there, there, core_dev)
+            done_x[m, 0] = total.astype(BF16)
+            go(ids_x[m], done_x.at[m, 0], done_x.at[m, 1], far_dev)
+
+        def dense_share(m):
+            got(ids_x[m], done_x.at[m, 1], far_dev)
+            whole[m, core] = done_x[m, 0].astype(F32) + done_x[m, 1].astype(F32)
+            go(ids_own[m], whole.at[m, core], whole.at[m, core], core_dev)
 
         def dense_end(m):
-            there = whole.at[m, side, 1 - core]
+            there = whole.at[m, 1 - core]
             got(ids_own[m], there, core_dev)
-            there = whole.at[m, 1 - side, 1 - core]
-            got(ids_cross[m], there, core_dev)
-            for s in range(2):
-                for k in range(2):
-                    rows = slice(s * rows_half, (s + 1) * rows_half)
-                    if m == 3:
-                        gout_ref[rows, k * core_cols : (k + 1) * core_cols] = whole[m, s, k]
-                    else:
-                        start = m * c.D + k * core_cols
-                        gqkv_ref[rows, start : start + core_cols] = whole[m, s, k]
 
     else:
 
@@ -765,7 +809,7 @@
 
     vec = vec_ref[...]
     lane = lane_of((c.B, 128))
-    d_mixed, dy_rows, lives = [], [], []
+    d_mixed, dy_rows = [], []
     d_logits = []
     for image in range(c.N):
         rows = slice(image * c.B, (image + 1) * c.B)
@@ -790,7 +834,6 @@
         dot = jnp.sum(router * d_router, axis=1, keepdims=True)
         d_logits.append(router * (d_router - dot))
         live = jnp.where(row_of((c.B, 1)) < len_ref[image, x], 1.0, 0.0)
-        lives.append(live)
         dy_rows.append(cot_ref[rows, :].astype(F32) * live)
     d_mixed = jnp.concatenate(d_mixed, axis=0)
     d_logits = jnp.concatenate(d_logits, axis=0)
@@ -814,7 +857,6 @@
     datt[...] = mm(d_branch, w_ref[3], NT).astype(BF16)
     unit_one, inverse_one = normalize(tok_ref[...].astype(F32))
     norm_t[...] = (unit_one * vec[0:1] + vec[2:3]).astype(BF16).T
-    grads_after_core()
     loads[1].wait()
 
     kvcore_ids = [[links.new() for _ in range(2)] for _ in range(c.N)]
@@ -871,27 +913,27 @@
     attend_back(0, 0, pairs)
     kv_to_core(0)
     if c.gather:
-        dense_x(3)
+        dense_y(3)
     attend_back(1, 0, pairs // 2)
     kv_to_far(0)
-    if c.gather:
-        dense_y(3)
     attend_back(1, pairs // 2, pairs)
     kv_to_core(1)
     dense_start(0, mm(norm_t[...], dproj[:, 0 : c.D]))
-    grads_after_y_far()
     kv_to_far(1)
+    if c.gather:
+        dense_z(3)
     kv_end(0)
     if c.gather:
-        dense_x(0)
-        dense_z(3)
+        dense_y(0)
+        dense_x(3)
     kv_end(1)
     dense_start(1, mm(norm_t[...], dproj[:, c.D : 2 * c.D]))
     dense_start(2, mm(norm_t[...], dproj[:, 2 * c.D : 3 * c.D]))
     if c.gather:
-        dense_y(0)
-        dense_x(1)
-        dense_x(2)
+        dense_y(1)
+        dense_y(2)
+        dense_z(0)
+        dense_share(3)
     d_normed = mm(dproj[:, 0 : c.D], w_ref[0], NT)
     d_normed = d_normed + mm(dproj[:, c.D : 2 * c.D], w_ref[1], NT)
     d_normed = d_normed + mm(dproj[:, 2 * c.D : 3 * c.D], w_ref[2], NT)
@@ -908,23 +950,8 @@
         small_z = [links.new() for _ in experts]
         go(small_ids[0], small.at[0], small_in.at[0], core_dev)
     gtok_ref[...] = dhid[...] + normalize_back(d_normed, unit_one, inverse_one, vec[0:1])
-
-    def block_output():
-        loads[4].wait()
-        for k, (at, device) in enumerate(zip(made_ids, experts), 1):
-            got(at, made.at[:, z ^ k], device)
-        for image in range(c.N):
-            rows = slice(image * c.B, (image + 1) * c.B)
-            meta = meta_ref[rows, :]
-            slots = [meta[:, j : j + 1].astype(jnp.int32) for j in range(2)]
-            at = lane_of((c.B, c.E * c.cap))
-            gates = jnp.where(at == slots[0], meta[:, 4:5], 0.0)
-            gates = gates + jnp.where(at == slots[1], meta[:, 5:6], 0.0)
-            high, low = in_parts(gates, 2)
-            rows_made = made[image].reshape(c.E * c.cap, c.D)
-            mixture = mm(high, rows_made) + mm(low, rows_made)
-            out_ref[rows, :] = (lives[image] * (hid_ref[rows, :] + mixture)).astype(BF16)
-
+    leave = pltpu.make_async_copy(gtok_ref, gtok_hbm, lsem.at[5])
+    leave.start()
     if c.gather:
 
         def small_step(step, device):
@@ -935,69 +962,122 @@
                 go(small_ids[step + 1], small.at[step + 1], small_in.at[step + 1], device)
 
         small_step(0, far_dev)
-        dense_z(0)
-        dense_share(3)
-        dense_y(1)
-        dense_y(2)
+        dense_end(3)
+        dense_x(0)
         small_step(1, y_dev)
-        block_output()
+        dense_z(1)
+        dense_z(2)
         small_step(2, None)
         for k, (at, device) in enumerate(zip(small_z, experts), 1):
             go(at, small.at[3], small_in.at[3 + z], device)
-        dense_z(1)
-        dense_z(2)
-        dense_cross(3)
         dense_share(0)
-        dense_end(3)
+        dense_x(1)
+        dense_x(2)
         total = small[3]
         for k, (at, device) in enumerate(zip(small_z, experts), 1):
             got(at, small_in.at[3 + (z ^ k)], device)
             total = total + small_in[3 + (z ^ k)]
-        src, dst = row_of((c.D, 128)), lane_of((c.D, 128))
-        pick = jnp.logical_and(dst < c.sh, src == dst + (z * c.Y + y) * c.sh)
-        pick = jnp.where(pick, 1.0, 0.0).astype(BF16)
-        gsmall_ref[...] = sum(mm(part, pick) for part in in_parts(total, 3))
-        dense_cross(0)
+        gsmall_ref[...] = total
+        dense_end(0)
         dense_share(1)
         dense_share(2)
-        dense_end(0)
-        dense_cross(1)
-        dense_cross(2)
-        grads_end()
         dense_end(1)
         dense_end(2)
     else:
         gsmall_ref[...] = small_here
-        block_output()
-        grads_end()
+    for k, (at, device) in enumerate(zip(made_ids, experts), 1):
+        got(at, made.at[:, z ^ k], device)
+    grads_end()
+    leave.wait()
+    own_made.wait()
     for copy in ends:
         copy.wait_send()
 
 
-def run_back(c, tok, cot, lengths, weights, vec, q, kv, lse, att, hid, mix, meta, router, xback, gback, yloc, grads):
+def last_kernel(c, *refs):
+    refs = list(refs)
+    take = lambda count: [refs.pop(0) for _ in range(count)]
+    len_ref, hid_ref, meta_ref, gtok_in, made_in, grad_in, gy_in, gx_in = take(8)
+    if c.gather:
+        whole_ref, small_ref = take(2)
+    out_ref, gtok_out, gin_ref, gdown_ref = take(4)
+    if c.gather:
+        gqkv_ref, gout_ref, gains_ref, biases_ref, grouter_ref = take(5)
+    made, gown, gy, gx, sem = take(5)
+    z, x, y = lax.axis_index("expert"), lax.axis_index("context"), lax.axis_index("dp")
+    side = lax.div(x, 2)
+    piece = c.FF // 8
+    own_piece = pl.ds(pl.multiple_of(y * piece, 128), piece)
+    loads = []
+    for which in range(2):
+        for index, (src, dst) in enumerate((
+            (grad_in.at[side, which, :, own_piece], gown.at[which]),
+            (gy_in.at[which], gy.at[which]),
+            (gx_in.at[which], gx.at[which]),
+        )):
+            loads.append(pltpu.make_async_copy(src, dst, sem.at[3 * which + index]))
+    loads.append(pltpu.make_async_copy(made_in, made, sem.at[6]))
+    for load in loads:
+        load.start()
+    gtok_out[...] = gtok_in[...]
+    if c.gather:
+        core_cols = c.D // 2
+        for m in range(4):
+            for k in range(2):
+                if m == 3:
+                    gout_ref[:, k * core_cols : (k + 1) * core_cols] = whole_ref[m, k]
+                else:
+                    start = m * c.D + k * core_cols
+                    gqkv_ref[:, start : start + core_cols] = whole_ref[m, k]
+        src, dst = row_of((c.D, 128)), lane_of((c.D, 128))
+        pick = jnp.logical_and(dst < c.sh, src == dst + (z * c.Y + y) * c.sh)
+        pick = jnp.where(pick, 1.0, 0.0).astype(BF16)
+        small = sum(mm(part, pick) for part in in_parts(small_ref[...], 3))
+        gains_ref[...] = small[0:2, 0 : c.sh]
+        biases_ref[...] = small[2:4, 0 : c.sh]
+        grouter_ref[...] = small[LOGIT_LANE : LOGIT_LANE + c.E, 0 : c.sh]
+    for which in range(2):
+        for load in loads[3 * which : 3 * which + 3]:
+            load.wait()
+        total = gown[which].astype(F32) + gy[which].astype(F32) + gx[which].astype(F32)
+        if which == 0:
+            gin_ref[...] = total
+        else:
+            gdown_ref[...] = total.T
+    loads[6].wait()
+    for image in range(c.N):
+        rows = slice(image * c.B, (image + 1) * c.B)
+        meta = meta_ref[rows, :]
+        slots = [meta[:, j : j + 1].astype(jnp.int32) for j in range(2)]
+        at = lane_of((c.B, c.E * c.cap))
+        gates = jnp.where(at == slots[0], meta[:, 4:5], 0.0)
+        gates = gates + jnp.where(at == slots[1], meta[:, 5:6], 0.0)
+        high, low = in_parts(gates, 2)
+        rows_made = made[image].reshape(c.E * c.cap, c.D)
+        mixture = mm(high, rows_made) + mm(low, rows_made)
+        live = jnp.where(row_of((c.B, 1)) < len_ref[image, x], 1.0, 0.0)
+        out_ref[rows, :] = (live * (hid_ref[rows, :] + mixture)).astype(BF16)
+
+
+def run_back(c, tok, cot, lengths, weights, vec, q, kv, lse, att, hid, mix, meta, router, xback, gback, yloc, grads, gnext):
     shape = jax.ShapeDtypeStruct
     piece = c.FF // 8
     made = [
-        shape((c.T, c.D), BF16),
         shape((c.T, c.D), F32),
-        shape((c.D, piece), F32),
-        shape((piece, c.D), F32),
+        shape((c.N, c.E, c.cap, c.D), BF16),
+        shape((2, c.D, piece), BF16),
+        shape((2, c.D, piece), BF16),
     ]
     dense_scratch = []
     if c.gather:
-        made += [
-            shape((c.sh, 3 * c.D), F32),
-            shape((c.sh, c.D), F32),
-            shape((c.r8, 128), F32),
-        ]
-        half_rows, half_cols = c.sh // 2, c.D // 2
+        half_cols = c.D // 2
+        made += [shape((4, 2, c.sh, half_cols), F32), shape((c.r8, c.D), F32)]
         dense_scratch = [
             pltpu.VMEM((4, c.E, c.Y, c.sh, c.D), BF16),
             pltpu.VMEM((4, c.E, c.Y, c.sh, half_cols), BF16),
-            pltpu.VMEM((4, c.E, c.Y, half_rows, half_cols), BF16),
-            pltpu.VMEM((4, c.E, half_rows, half_cols), BF16),
-            pltpu.VMEM((4, c.E, half_rows, half_cols), BF16),
-            pltpu.VMEM((4, 2, 2, half_rows, half_cols), F32),
+            pltpu.VMEM((4, 2, c.sh, half_cols), BF16),
+            pltpu.VMEM((4, c.E, c.sh, half_cols), BF16),
+            pltpu.VMEM((4, c.E, c.sh, half_cols), BF16),
             pltpu.VMEM((4, c.r8, c.D), F32),
             pltpu.VMEM((3 + c.E, c.r8, c.D), F32),
         ]
@@ -1007,15 +1087,13 @@
     results = pl.pallas_call(
         functools.partial(back_kernel, c),
         out_shape=made,
-        in_specs=[spec(pltpu.SMEM)] + [spec(pltpu.VMEM)] * 12 + [spec(pl.ANY)] * 4,
-        out_specs=[spec(pltpu.VMEM)] * len(made),
+        in_specs=[spec(pltpu.SMEM)] + [spec(pltpu.VMEM)] * 12 + [spec(pl.ANY)] * 5,
+        out_specs=[spec(pl.ANY)] * 4 + [spec(pltpu.VMEM)] * 2,
         scratch_shapes=[
             pltpu.VMEM((4, c.D, c.D), BF16),
             pltpu.VMEM((c.N, c.S, 2 * c.D), BF16),
-            pltpu.VMEM((c.N, c.E, c.cap, c.D), BF16),
-            pltpu.VMEM((2, 2, c.D, 2 * piece), BF16),
-            pltpu.VMEM((2, 2, c.D, 2 * piece), BF16),
-            pltpu.VMEM((2, 2, c.D, piece), BF16),
+            pltpu.VMEM((c.T, c.D), F32),
+            pltpu.VMEM((2, c.D, piece), BF16),
             pltpu.VMEM((2, c.D, piece), BF16),
             pltpu.VMEM((c.N, c.S, 2 * c.D), BF16),
             pltpu.VMEM((c.N, 2, c.B, 2 * c.D), BF16),
@@ -1026,7 +1104,7 @@
             pltpu.VMEM((c.D, c.T), BF16),
             pltpu.VMEM((128, c.D), F32),
             *dense_scratch,
-            pltpu.SemaphoreType.DMA((5,)),
+            pltpu.SemaphoreType.DMA((8,)),
             pltpu.SemaphoreType.DMA((count,)),
             pltpu.SemaphoreType.DMA((count,)),
         ],
@@ -1034,28 +1112,53 @@
             collective_id=2, has_side_effects=True, vmem_limit_bytes=VMEM_LIMIT
         ),
         name="back",
-    )(lengths, tok, cot, vec, q, lse, att, hid, mix, meta, router, xback, gback, weights, kv, yloc, grads)
+    )(lengths, tok, cot, vec, q, lse, att, hid, mix, meta, router, xback, gback, weights, kv, yloc, grads, gnext)
+    g_tok, made_home, gy, gx, dense, small = results
+    last = [shape((c.T, c.D), BF16), shape((c.T, c.D), F32)]
+    last += [shape((c.D, piece), F32), shape((piece, c.D), F32)]
+    if c.gather:
+        last += [shape((c.sh, 3 * c.D), F32), shape((c.sh, c.D), F32)]
+        last += [shape((2, c.sh), F32), shape((2, c.sh), F32), shape((c.E, c.sh), F32)]
+    more = (dense, small) if c.gather else ()
+    results = pl.pallas_call(
+        functools.partial(last_kernel, c),
+        out_shape=last,
+        in_specs=[spec(pltpu.SMEM)]
+        + [spec(pltpu.VMEM)] * 3
+        + [spec(pl.ANY)] * 4
+        + [spec(pltpu.VMEM)] * len(more),
+        out_specs=[spec(pltpu.VMEM)] * len(last),
+        scratch_shapes=[
+            pltpu.VMEM((c.N, c.E, c.cap, c.D), BF16),
+            pltpu.VMEM((2, c.D, piece), BF16),
+            pltpu.VMEM((2, c.D, piece), BF16),
+            pltpu.VMEM((2, c.D, piece), BF16),
+            pltpu.SemaphoreType.DMA((7,)),
+        ],
+        compiler_params=pltpu.CompilerParams(vmem_limit_bytes=VMEM_LIMIT),
+        name="last",
+    )(lengths, hid, meta, g_tok, made_home, grads, gy, gx, *more)
     out, g_tok, g_in, g_down = results[:4]
     if c.gather:
-        g_qkv, g_out, small = results[4:]
-        small = small[:, : c.sh]
+        g_qkv, g_out, g_gains, g_biases, g_router = results[4:]
     else:
-        dense, small = results[4:]
         both = ("expert", "dp")
         flat = dense.astype(F32).transpose(1, 0, 2).reshape(c.D, 4 * c.D)
         flat = lax.psum_scatter(flat, both, scatter_dimension=0, tiled=True)
         small = lax.psum_scatter(small, both, scatter_dimension=1, tiled=True)
         flat, small = lax.psum((flat, small), "context")
         g_qkv, g_out = flat[:, : 3 * c.D], flat[:, 3 * c.D :]
+        g_gains, g_biases = small[0:2], small[2:4]
+        g_router = small[LOGIT_LANE : LOGIT_LANE + c.E]
     rows = (c.N, c.B, c.D)
     return (
         out.reshape(rows),
         g_tok.reshape(rows),
         g_qkv,
         g_out,
-        small[LOGIT_LANE : LOGIT_LANE + c.E].T,
-        small[0:2],
-        small[2:4],
+        g_router.T,
+        g_gains,
+        g_biases,
         g_in[None],
         g_down[None],
     )
@@ -1103,8 +1206,8 @@
     c.gather = c.sh % 32 == 0
     tok = tokens.reshape(c.T, width)
     cot = cotangent.reshape(c.T, width)
-    route = route_ids.reshape(c.T, 2)
-    keep = keep_mask.reshape(c.T, 2)
+    route = route_ids.transpose(0, 2, 1)
+    keep = keep_mask.transpose(0, 2, 1)
     both = ("expert", "dp")
     if c.gather:
         given = (w_qkv, w_attn_out, pack_small(c, w_router, norm_gains, norm_biases))

time: 293 us -> 256 us (0.87)
  Pallas kernels: 275 us -> 250 us
  local copies, waits for them, and re-layouts: 12.1 us -> 0 us
    pallas_call x1, Pallas kernels: 126 us -> 92.3 us  [run_back(): pl.pallas_call(functools.partial(back_kernel, c), out_shape=made, in_spec...]
    unnamed x18 -> x0, local copies, waits for them, and re-layouts: 9.45 us -> none
    pallas_call x0 -> x1, Pallas kernels: none -> 6.87 us  [run_back(): pl.pallas_call(functools.partial(last_kernel, c), out_shape=last, in_spec...]
where the time goes in v3:
time: 256 us; the launch traced here: 252 us
  Pallas kernels  250 us (98%)
    pallas_call x1, Pallas kernels, run_back(): pl.pallas_call(functools.partial(back_kernel, c), out_shape=made, in_spec...  92.3 us
    pallas_call x1, Pallas kernels, run_experts(): pl.pallas_call(functools.partial(expert_kernel, c), out_shape=[shape((c.N...  75.3 us
    pallas_call x1, Pallas kernels, run_front(): pl.pallas_call(functools.partial(front_kernel, c), out_shape=made, in_spe...  75.2 us
    pallas_call x1, Pallas kernels, run_back(): pl.pallas_call(functools.partial(last_kernel, c), out_shape=last, in_spec...  6.87 us

profile of v3, /device:TPU:0, one launch (start us, length us, event | category | flops | bytes accessed | tf_op | source)
XLA Modules:
  0.0 252.0 jit_solution(5227074211879737469)
XLA Ops:
  0.6 1.3 fusion.5.refs_7_
  1.9 75.2 %front.1 = (bf16[4,768,768]{2,1,0:T(8,128)(2,1)}, f32[8,768]{1,0:T(8,128)}, bf16[320,768]{1,0:T(8,128)(2,1)}, bf16[2,640,1536]{2,1,0:T(8,128)(2,1)}, f32[2,6,8,3...) custom-call(s32[2,4]{1,0:T(2,128)} %refs_0_.5, ...), custom_call_target="tpu_custom_call" | custom-call | tf_op jit(solution)/shard_map/front/pallas_call | solution.py:427
  77.1 75.3 %experts.1 = (bf16[2,4,128,768]{3,2,1,0:T(8,128)(2,1)}, f32[4,8,128]{2,1,0:T(8,128)}, bf16[4,2,128,768]{3,2,1,0:T(8,128)(2,1)}, bf16[2,2,768,768]{3,2,1,0:T(8,128)(2,1)}, bf16[2,768,384]{2,1,0:T(8,128)(2,1)}) custom-call(bf16[2,4,128,768]{3,2,1,0:T(8,128)(2,1)} %get-tuple-element.50.send_ref, f32[4,8,128]{2,1,0:T(8,128)} %get-tuple-element.51.gsend_ref, ...), custom_call_target="tpu_custom_call" | custom-call | tf_op jit(solution)/shard_map/experts/pallas_call | solution.py:637
  152.5 92.3 %back.1 = (f32[320,768]{1,0:T(8,128)}, bf16[2,4,128,768]{3,2,1,0:T(8,128)(2,1)}, bf16[2,768,384]{2,1,0:T(8,128)(2,1)}, bf16[2,768,384]{2,1,0:T(8,128)(2,1)}, f32...) custom-call(s32[2,4]{1,0:T(2,128)} %refs_0_.5, bf16[320,768]{1,0:T(8,128)(2,1)} %bitcast.15, bf16[320,768]{1,0:T(8,128)(2,1)} %bitcast.17, ...), custom_call_target="tpu_custom_call" | custom-call | tf_op jit(solution)/shard_map/back/pallas_call | solution.py:1087
  244.8 6.9 %last.1 = (bf16[320,768]{1,0:T(8,128)(2,1)}, f32[320,768]{1,0:T(8,128)}, f32[768,384]{1,0:T(8,128)}, f32[384,768]{1,0:T(8,128)}, f32[96,2304]{1,0:T(8,128)}, /*i...) custom-call(s32[2,4]{1,0:T(2,128)} %refs_0_.5, ...), custom_call_target="tpu_custom_call" | custom-call | tf_op jit(solution)/shard_map/last/pallas_call | solution.py:1123

commit v4 on v3

--- a/solution.py
+++ b/solution.py
@@ -191,7 +191,7 @@
     send_ref, gsend_ref, dyarr_ref = take(3)
     if c.gather:
         smalls, w_ref = take(2)
-    kv_ref, dysend, norm_ref, lsem, ssem, rsem = take(6)
+    kv_ref, dysend, lsem, ssem, rsem = take(5)
     links = Links(ssem, rsem)
     z, x, y = lax.axis_index("expert"), lax.axis_index("context"), lax.axis_index("dp")
     core = lax.rem(x, 2)
@@ -266,10 +266,15 @@
         pick = jnp.logical_and(inside < c.sh, lax.div(src, 128) * c.sh + inside == dst)
         vec_ref[...] = mm(wide, jnp.where(pick, 1.0, 0.0).astype(BF16))
     vec = vec_ref[...]
+    own_at = pl.ds(pl.multiple_of(x * c.B, 32), c.B)
+    norm_ids = [[links.new() for _ in range(3)] for _ in range(c.N)]
     for image in range(c.N):
         rows = slice(image * c.B, (image + 1) * c.B)
         unit_one, _ = normalize(tok_ref[rows, :].astype(F32))
-        norm_ref[rows, :] = (unit_one * vec[0:1] + vec[2:3]).astype(BF16)
+        kv_ref[image, own_at, 2 * c.D : 3 * c.D] = (unit_one * vec[0:1] + vec[2:3]).astype(BF16)
+        block = kv_ref.at[image, own_at, 2 * c.D : 3 * c.D]
+        go(norm_ids[image][0], block, block, far_dev)
+        go(norm_ids[image][1], block, block, core_dev)
 
     if c.gather:
         stages[0].step(1)
@@ -278,8 +283,9 @@
             stages[0].step(j)
         stages[0].finish()
 
-    normed = norm_ref[...]
-    own_at = pl.ds(pl.multiple_of(x * c.B, 32), c.B)
+    normed = jnp.concatenate(
+        [kv_ref[image, own_at, 2 * c.D : 3 * c.D] for image in range(c.N)], axis=0
+    )
     kv_ids = [[links.new() for _ in range(3)] for _ in range(c.N)]
     keys = mm(normed, w_ref[1]).astype(BF16)
     values = mm(normed, w_ref[2]).astype(BF16)
@@ -287,7 +293,7 @@
         rows = slice(image * c.B, (image + 1) * c.B)
         kv_ref[image, own_at, 0 : c.D] = keys[rows]
         kv_ref[image, own_at, c.D : 2 * c.D] = values[rows]
-        block = kv_ref.at[image, own_at, :]
+        block = kv_ref.at[image, own_at, 0 : 2 * c.D]
         go(kv_ids[image][0], block, block, far_dev)
         go(kv_ids[image][1], block, block, core_dev)
     if c.gather:
@@ -305,7 +311,14 @@
         leaving[-1].start()
     q_ref[...] = mm(normed, w_ref[0]).astype(BF16)
 
-    block_of = lambda image, who: kv_ref.at[image, pl.ds(pl.multiple_of(who * c.B, 32), c.B), :]
+    def block_of(image, who, first=0, last=2):
+        rows_at = pl.ds(pl.multiple_of(who * c.B, 32), c.B)
+        return kv_ref.at[image, rows_at, first * c.D : last * c.D]
+
+    for image in range(c.N):
+        far_block = block_of(image, x ^ 2, 2, 3)
+        links.make(norm_ids[image][0], far_block, far_block, far_dev).wait_recv()
+        go(norm_ids[image][2], far_block, far_block, core_dev)
 
     for image in range(c.N):
         rows = pl.ds(image * c.B, c.B)
@@ -316,6 +329,9 @@
         links.make(kv_ids[image][1], near_block, near_block, core_dev).wait_recv()
         cross_block = block_of(image, x ^ 3)
         links.make(kv_ids[image][2], cross_block, cross_block, core_dev).wait_recv()
+        for at, who in ((1, x ^ 1), (2, x ^ 3)):
+            there = block_of(image, who, 2, 3)
+            links.make(norm_ids[image][at], there, there, core_dev).wait_recv()
         leaving.append(pltpu.make_async_copy(kv_ref.at[image], kv_hbm.at[image], lsem.at[2 + image]))
         leaving[-1].start()
         bias = key_bias(c, len_ref, image)
@@ -403,7 +419,7 @@
     made = [shape((4, c.D, c.D), BF16), shape((c.r8, c.D), F32)] if c.gather else []
     made += [
         shape((c.T, c.D), BF16),
-        shape((c.N, c.S, 2 * c.D), BF16),
+        shape((c.N, c.S, 3 * c.D), BF16),
         shape((c.N, c.D // 128, 8, 2 * c.B), F32),
         shape((c.T, c.D), BF16),
         shape((c.T, c.D), F32),
@@ -414,7 +430,7 @@
         shape((c.E, 8, c.cap), F32),
         shape((c.E, c.N, c.cap, c.D), BF16),
     ]
-    count = 112 if c.gather else 2 * c.E + 16
+    count = 112 if c.gather else 2 * c.E + 32
     places = [spec(pltpu.VMEM)] * len(made)
     places[-1] = places[-10] = spec(pl.ANY)
     gather_scratch = []
@@ -431,9 +447,8 @@
         out_specs=places,
         scratch_shapes=gather_scratch
         + [
-            pltpu.VMEM((c.N, c.S, 2 * c.D), BF16),
+            pltpu.VMEM((c.N, c.S, 3 * c.D), BF16),
             pltpu.VMEM((c.N, c.E, c.cap, c.D), BF16),
-            pltpu.VMEM((c.T, c.D), BF16),
             pltpu.SemaphoreType.DMA((2 + c.N,)),
             pltpu.SemaphoreType.DMA((count,)),
             pltpu.SemaphoreType.DMA((count,)),
@@ -690,9 +705,9 @@
     else:
         dd, gsmall_ref = take(2)
     w_ref, kv_ref, gtok_ref, gpart, gnext = take(5)
-    dkv, kvcore, kvfar, dproj, datt, dhid, norm_t, router_sum = take(8)
-    if c.gather:
-        dd, dcore, done_x, done_y, done_z, small, small_in = take(7)
+    dkv, kvcore, kvfar, dproj, datt, dhid, norm_t, norm_all, router_sum = take(9)
+    if c.gather:
+        dd, dcore, done_x, done_y, done_z, small_four, small_y, small_z = take(8)
     lsem, ssem, rsem = take(3)
     links = Links(ssem, rsem)
     z, x, y = lax.axis_index("expert"), lax.axis_index("context"), lax.axis_index("dp")
@@ -727,7 +742,8 @@
     loads.append(own_made)
     for load in loads:
         load.start()
-    greet([core_dev, far_dev, y_dev] + experts)
+    cross_dev = [(z, x ^ 3, y)] if c.gather else []
+    greet([core_dev, far_dev, y_dev] + experts + cross_dev)
 
     made_ids = [links.new() for _ in experts]
     for k, (at, device) in enumerate(zip(made_ids, experts), 1):
@@ -858,6 +874,8 @@
     unit_one, inverse_one = normalize(tok_ref[...].astype(F32))
     norm_t[...] = (unit_one * vec[0:1] + vec[2:3]).astype(BF16).T
     loads[1].wait()
+    for image in range(c.N):
+        norm_all[:, image * c.S : (image + 1) * c.S] = kv_ref[image, :, 2 * c.D : 3 * c.D].T
 
     kvcore_ids = [[links.new() for _ in range(2)] for _ in range(c.N)]
     kvfar_ids = [links.new() for _ in range(c.N)]
@@ -897,10 +915,10 @@
         for s in range(2):
             got(kvcore_ids[image][s], kvcore.at[image, s], core_dev)
         rows = block_rows(2 * (1 - side) + core)
-        dkv[image, rows, :] = (
+        kvcore[image, 1 - side] = (
             dkv[image, rows, :].astype(F32) + kvcore[image, 1 - side].astype(F32)
         ).astype(BF16)
-        go(kvfar_ids[image], dkv.at[image, rows, :], kvfar.at[image], far_dev)
+        go(kvfar_ids[image], kvcore.at[image, 1 - side], kvfar.at[image], far_dev)
 
     def kv_end(image):
         got(kvfar_ids[image], kvfar.at[image], far_dev)
@@ -919,21 +937,22 @@
     attend_back(1, pairs // 2, pairs)
     kv_to_core(1)
     dense_start(0, mm(norm_t[...], dproj[:, 0 : c.D]))
+    for m in (1, 2):
+        columns = slice((m - 1) * c.D, m * c.D)
+        dense_start(m, mm(norm_all[...], dkv[:, :, columns].reshape(c.N * c.S, c.D)))
     kv_to_far(1)
     if c.gather:
-        dense_z(3)
-    kv_end(0)
-    if c.gather:
         dense_y(0)
-        dense_x(3)
-    kv_end(1)
-    dense_start(1, mm(norm_t[...], dproj[:, c.D : 2 * c.D]))
-    dense_start(2, mm(norm_t[...], dproj[:, 2 * c.D : 3 * c.D]))
-    if c.gather:
         dense_y(1)
         dense_y(2)
+        dense_z(3)
+        kv_end(0)
         dense_z(0)
-        dense_share(3)
+        dense_x(3)
+        dense_z(1)
+    else:
+        kv_end(0)
+    kv_end(1)
     d_normed = mm(dproj[:, 0 : c.D], w_ref[0], NT)
     d_normed = d_normed + mm(dproj[:, c.D : 2 * c.D], w_ref[1], NT)
     d_normed = d_normed + mm(dproj[:, 2 * c.D : 3 * c.D], w_ref[2], NT)
@@ -945,41 +964,37 @@
         [small_here, router_sum[LOGIT_LANE : LOGIT_LANE + c.r8 - 4]], axis=0
     )
     if c.gather:
-        small[0] = small_here
         small_ids = [links.new() for _ in range(3)]
-        small_z = [links.new() for _ in experts]
-        go(small_ids[0], small.at[0], small_in.at[0], core_dev)
+        small_y_id = links.new()
+        small_z_ids = [links.new() for _ in experts]
+        small_four[x] = small_here
+        for k, at in enumerate(small_ids, 1):
+            go(at, small_four.at[x], small_four.at[x], (z, x ^ k, y))
     gtok_ref[...] = dhid[...] + normalize_back(d_normed, unit_one, inverse_one, vec[0:1])
     leave = pltpu.make_async_copy(gtok_ref, gtok_hbm, lsem.at[5])
     leave.start()
     if c.gather:
 
-        def small_step(step, device):
-            source = core_dev if step == 0 else far_dev if step == 1 else y_dev
-            got(small_ids[step], small_in.at[step], source)
-            small[step + 1] = small[step] + small_in[step]
-            if step < 2:
-                go(small_ids[step + 1], small.at[step + 1], small_in.at[step + 1], device)
-
-        small_step(0, far_dev)
+        dense_x(0)
+        dense_share(3)
+        dense_z(2)
+        for k, at in enumerate(small_ids, 1):
+            got(at, small_four.at[x ^ k], (z, x ^ k, y))
+        small_y[0] = (small_four[0] + small_four[1]) + (small_four[2] + small_four[3])
+        go(small_y_id, small_y.at[0], small_y.at[1], y_dev)
+        dense_x(1)
+        dense_share(0)
+        got(small_y_id, small_y.at[1], y_dev)
+        small_z[z] = small_y[0] + small_y[1]
+        for at, device in zip(small_z_ids, experts):
+            go(at, small_z.at[z], small_z.at[z], device)
         dense_end(3)
-        dense_x(0)
-        small_step(1, y_dev)
-        dense_z(1)
-        dense_z(2)
-        small_step(2, None)
-        for k, (at, device) in enumerate(zip(small_z, experts), 1):
-            go(at, small.at[3], small_in.at[3 + z], device)
-        dense_share(0)
-        dense_x(1)
         dense_x(2)
-        total = small[3]
-        for k, (at, device) in enumerate(zip(small_z, experts), 1):
-            got(at, small_in.at[3 + (z ^ k)], device)
-            total = total + small_in[3 + (z ^ k)]
-        gsmall_ref[...] = total
+        dense_share(1)
         dense_end(0)
-        dense_share(1)
+        for k, (at, device) in enumerate(zip(small_z_ids, experts), 1):
+            got(at, small_z.at[z ^ k], device)
+        gsmall_ref[...] = sum((small_z[k] for k in range(1, c.E)), small_z[0])
         dense_share(2)
         dense_end(1)
         dense_end(2)
@@ -1078,8 +1093,9 @@
             pltpu.VMEM((4, 2, c.sh, half_cols), BF16),
             pltpu.VMEM((4, c.E, c.sh, half_cols), BF16),
             pltpu.VMEM((4, c.E, c.sh, half_cols), BF16),
-            pltpu.VMEM((4, c.r8, c.D), F32),
-            pltpu.VMEM((3 + c.E, c.r8, c.D), F32),
+            pltpu.VMEM((c.C, c.r8, c.D), F32),
+            pltpu.VMEM((2, c.r8, c.D), F32),
+            pltpu.VMEM((c.E, c.r8, c.D), F32),
         ]
     else:
         made += [shape((4, c.D, c.D), BF16), shape((c.r8, c.D), F32)]
@@ -1091,7 +1107,7 @@
         out_specs=[spec(pl.ANY)] * 4 + [spec(pltpu.VMEM)] * 2,
         scratch_shapes=[
             pltpu.VMEM((4, c.D, c.D), BF16),
-            pltpu.VMEM((c.N, c.S, 2 * c.D), BF16),
+            pltpu.VMEM((c.N, c.S, 3 * c.D), BF16),
             pltpu.VMEM((c.T, c.D), F32),
             pltpu.VMEM((2, c.D, piece), BF16),
             pltpu.VMEM((2, c.D, piece), BF16),
@@ -1102,6 +1118,7 @@
             pltpu.VMEM((c.T, c.D), BF16),
             pltpu.VMEM((c.T, c.D), F32),
             pltpu.VMEM((c.D, c.T), BF16),
+            pltpu.VMEM((c.D, c.N * c.S), BF16),
             pltpu.VMEM((128, c.D), F32),
             *dense_scratch,
             pltpu.SemaphoreType.DMA((8,)),

time: 256 us -> 243 us (0.949)
  Pallas kernels: 250 us -> 238 us
    pallas_call x1, Pallas kernels: 92.3 us -> 80.4 us  [run_back(): pl.pallas_call(functools.partial(back_kernel, c), out_shape=made, in_spec...]
where the time goes in v4:
time: 243 us; the launch traced here: 240 us
  Pallas kernels  238 us (98%)
    pallas_call x1, Pallas kernels, run_back(): pl.pallas_call(functools.partial(back_kernel, c), out_shape=made, in_spec...  80.4 us
    pallas_call x1, Pallas kernels, run_front(): pl.pallas_call(functools.partial(front_kernel, c), out_shape=made, in_spe...  75.3 us
    pallas_call x1, Pallas kernels, run_experts(): pl.pallas_call(functools.partial(expert_kernel, c), out_shape=[shape((c.N...  75.3 us
    pallas_call x1, Pallas kernels, run_back(): pl.pallas_call(functools.partial(last_kernel, c), out_shape=last, in_spec...  6.87 us

profile of v4, /device:TPU:0, one launch (start us, length us, event | category | flops | bytes accessed | tf_op | source)
XLA Modules:
  0.0 240.2 jit_solution(9096116160309451159)
XLA Ops:
  0.6 1.3 fusion.5.refs_7_
  1.9 75.3 %front.1 = (bf16[4,768,768]{2,1,0:T(8,128)(2,1)}, f32[8,768]{1,0:T(8,128)}, bf16[320,768]{1,0:T(8,128)(2,1)}, bf16[2,640,2304]{2,1,0:T(8,128)(2,1)}, f32[2,6,8,3...) custom-call(s32[2,4]{1,0:T(2,128)} %refs_0_.5, ...), custom_call_target="tpu_custom_call" | custom-call | tf_op jit(solution)/shard_map/front/pallas_call | solution.py:443
  77.3 75.3 %experts.1 = (bf16[2,4,128,768]{3,2,1,0:T(8,128)(2,1)}, f32[4,8,128]{2,1,0:T(8,128)}, bf16[4,2,128,768]{3,2,1,0:T(8,128)(2,1)}, bf16[2,2,768,768]{3,2,1,0:T(8,128)(2,1)}, bf16[2,768,384]{2,1,0:T(8,128)(2,1)}) custom-call(bf16[2,4,128,768]{3,2,1,0:T(8,128)(2,1)} %get-tuple-element.50.send_ref, f32[4,8,128]{2,1,0:T(8,128)} %get-tuple-element.51.gsend_ref, ...), custom_call_target="tpu_custom_call" | custom-call | tf_op jit(solution)/shard_map/experts/pallas_call | solution.py:652
  152.6 80.4 %back.1 = (f32[320,768]{1,0:T(8,128)}, bf16[2,4,128,768]{3,2,1,0:T(8,128)(2,1)}, bf16[2,768,384]{2,1,0:T(8,128)(2,1)}, bf16[2,768,384]{2,1,0:T(8,128)(2,1)}, f32...) custom-call(s32[2,4]{1,0:T(2,128)} %refs_0_.5, bf16[320,768]{1,0:T(8,128)(2,1)} %bitcast.15, bf16[320,768]{1,0:T(8,128)(2,1)} %bitcast.17, ...), custom_call_target="tpu_custom_call" | custom-call | tf_op jit(solution)/shard_map/back/pallas_call | solution.py:1103
  233.0 6.9 %last.1 = (bf16[320,768]{1,0:T(8,128)(2,1)}, f32[320,768]{1,0:T(8,128)}, f32[768,384]{1,0:T(8,128)}, f32[384,768]{1,0:T(8,128)}, f32[96,2304]{1,0:T(8,128)}, /*i...) custom-call(s32[2,4]{1,0:T(2,128)} %refs_0_.5, ...), custom_call_target="tpu_custom_call" | custom-call | tf_op jit(solution)/shard_map/last/pallas_call | solution.py:1140

commit v5 on v4

--- a/solution.py
+++ b/solution.py
@@ -192,6 +192,8 @@
     if c.gather:
         smalls, w_ref = take(2)
     kv_ref, dysend, lsem, ssem, rsem = take(5)
+    if c.relay:
+        dy_info, far_info, far_rows, dypack = take(4)
     links = Links(ssem, rsem)
     z, x, y = lax.axis_index("expert"), lax.axis_index("context"), lax.axis_index("dp")
     core = lax.rem(x, 2)
@@ -227,6 +229,11 @@
         for stage in stages:
             stage.route(above, below, y_dev, core_dev)
         stages[0].open()
+
+    if c.relay:
+        dy_info_id = links.new()
+        dy_far_ids = [links.new() for _ in range(c.N)]
+        dy_relay_ids = [links.new() for _ in range(c.N)]
 
     unit_rows = [None] * c.N
     choices = []
@@ -253,6 +260,9 @@
         )
         place = place.astype(BF16)
         choices.append((first, second, kept, slot_first, slot_second, place))
+        if c.relay:
+            info = [to_row(column) for column in (slot_first.astype(F32), slot_second.astype(F32), *kept)]
+            dy_info[image] = jnp.concatenate(info + [jnp.zeros((4, c.B), F32)], axis=0)
         dysend[image] = mm(place, cot_ref[rows, :], TN).astype(BF16).reshape(c.E, c.cap, c.D)
 
     if c.gather:
@@ -301,10 +311,40 @@
             stages[1].step(j)
     dy_ids = [links.new() for _ in experts]
     for k, (at, device) in enumerate(zip(dy_ids, experts), 1):
-        go(at, dysend.at[:, z ^ k], dyarr_ref.at[z], device)
+        if k == 1 or not c.relay:
+            go(at, dysend.at[:, z ^ k], dyarr_ref.at[z], device)
     own_dy = pltpu.make_async_copy(dysend.at[:, z], dyarr_ref.at[z], lsem.at[0])
     own_dy.start()
+    if c.relay:
+        go(dy_info_id, dy_info, far_info, experts[1])
+
+    def dy_to_far(image):
+        rows = pl.ds(image * c.B, c.B)
+        go(dy_far_ids[image], cot_ref.at[rows, :], far_rows.at[image], experts[1])
+
+    def dy_pass_on(image):
+        if image == 0:
+            links.make(dy_info_id, far_info, far_info, experts[1]).wait_recv()
+        here = far_rows.at[image]
+        links.make(dy_far_ids[image], here, here, experts[1]).wait_recv()
+        info = far_info[image]
+        at = row_of((c.cap, c.B)).astype(F32)
+        for index in range(2):
+            first = ((z ^ index) * c.cap).astype(F32)
+            kept = jnp.where(at == info[0:1] - first, info[2:3], 0.0)
+            kept = kept + jnp.where(at == info[1:2] - first, info[3:4], 0.0)
+            dypack[index, image] = mm(kept.astype(BF16), far_rows[image]).astype(BF16)
+        go(dy_relay_ids[image], dypack.at[1, image], dyarr_ref.at[z ^ 2, image], experts[0])
+        leaving.append(
+            pltpu.make_async_copy(
+                dypack.at[0, image], dyarr_ref.at[z ^ 2, image], lsem.at[2 + c.N + image]
+            )
+        )
+        leaving[-1].start()
+
     leaving = [own_dy]
+    if c.relay:
+        dy_to_far(0)
     if c.gather:
         stages[1].finish()
         leaving.append(pltpu.make_async_copy(w_ref, w_hbm, lsem.at[1]))
@@ -334,6 +374,8 @@
             links.make(norm_ids[image][at], there, there, core_dev).wait_recv()
         leaving.append(pltpu.make_async_copy(kv_ref.at[image], kv_hbm.at[image], lsem.at[2 + image]))
         leaving[-1].start()
+        if c.relay and image == 0:
+            dy_to_far(1)
         bias = key_bias(c, len_ref, image)
 
         def pair_step(pair, carry):
@@ -351,6 +393,8 @@
             return carry
 
         lax.fori_loop(0, c.D // 128, pair_step, 0)
+        if c.relay:
+            dy_pass_on(image)
 
     branch = mm(att_ref[...], w_ref[3])
     hidden = tok_ref[...].astype(F32) + branch
@@ -400,7 +444,12 @@
         meta_ref[rows, :] = meta
 
     for k, (at, device) in enumerate(zip(dy_ids, experts), 1):
-        links.make(at, dyarr_ref.at[z ^ k], dyarr_ref.at[z ^ k], device).wait_recv()
+        if k == 1 or not c.relay:
+            links.make(at, dyarr_ref.at[z ^ k], dyarr_ref.at[z ^ k], device).wait_recv()
+    if c.relay:
+        for image in range(c.N):
+            there = dyarr_ref.at[z ^ 3, image]
+            links.make(dy_relay_ids[image], there, there, experts[0]).wait_recv()
     for copy in leaving:
         copy.wait()
     for copy in ends:
@@ -440,6 +489,14 @@
             pltpu.VMEM((c.E * c.Y, c.r8, 128), F32),
             pltpu.VMEM((4, c.D, c.D), BF16),
         ]
+    relay_scratch = []
+    if c.relay:
+        relay_scratch = [
+            pltpu.VMEM((c.N, 8, c.B), F32),
+            pltpu.VMEM((c.N, 8, c.B), F32),
+            pltpu.VMEM((c.N, c.B, c.D), BF16),
+            pltpu.VMEM((2, c.N, c.cap, c.D), BF16),
+        ]
     out = pl.pallas_call(
         functools.partial(front_kernel, c),
         out_shape=made,
@@ -449,10 +506,11 @@
         + [
             pltpu.VMEM((c.N, c.S, 3 * c.D), BF16),
             pltpu.VMEM((c.N, c.E, c.cap, c.D), BF16),
-            pltpu.SemaphoreType.DMA((2 + c.N,)),
+            pltpu.SemaphoreType.DMA((2 + 2 * c.N,)),
             pltpu.SemaphoreType.DMA((count,)),
             pltpu.SemaphoreType.DMA((count,)),
-        ],
+        ]
+        + relay_scratch,
         compiler_params=pltpu.CompilerParams(
             collective_id=0, has_side_effects=True, vmem_limit_bytes=VMEM_LIMIT
         ),
@@ -1221,6 +1279,7 @@
         chunks=4,
     )
     c.gather = c.sh % 32 == 0
+    c.relay = experts == 4 and c.cap % 128 == 0
     tok = tokens.reshape(c.T, width)
     cot = cotangent.reshape(c.T, width)
     route = route_ids.transpose(0, 2, 1)

time: 243 us -> 241 us (level)
  Pallas kernels: 238 us -> 235 us
    pallas_call x1, Pallas kernels: 75.3 us -> 72.8 us  [run_experts(): pl.pallas_call(functools.partial(expert_kernel, c), out_shape=[shape((c.N...]
where the time goes in v5:
time: 241 us; the launch traced here: 237 us
  Pallas kernels  235 us (98%)
    pallas_call x1, Pallas kernels, run_back(): pl.pallas_call(functools.partial(back_kernel, c), out_shape=made, in_spec...  79.6 us
    pallas_call x1, Pallas kernels, run_front(): pl.pallas_call(functools.partial(front_kernel, c), out_shape=made, in_spe...  75.8 us
    pallas_call x1, Pallas kernels, run_experts(): pl.pallas_call(functools.partial(expert_kernel, c), out_shape=[shape((c.N...  72.8 us
    pallas_call x1, Pallas kernels, run_back(): pl.pallas_call(functools.partial(last_kernel, c), out_shape=last, in_spec...  6.87 us

profile of v5, /device:TPU:0, one launch (start us, length us, event | category | flops | bytes accessed | tf_op | source)
XLA Modules:
  0.0 237.3 jit_solution(3686593887333991971)
XLA Ops:
  0.6 1.3 fusion.5.refs_7_
  1.9 75.8 %front.1 = (bf16[4,768,768]{2,1,0:T(8,128)(2,1)}, f32[8,768]{1,0:T(8,128)}, bf16[320,768]{1,0:T(8,128)(2,1)}, bf16[2,640,2304]{2,1,0:T(8,128)(2,1)}, f32[2,6,8,3...) custom-call(s32[2,4]{1,0:T(2,128)} %refs_0_.5, ...), custom_call_target="tpu_custom_call" | custom-call | tf_op jit(solution)/shard_map/front/pallas_call | solution.py:500
  77.8 72.8 %experts.1 = (bf16[2,4,128,768]{3,2,1,0:T(8,128)(2,1)}, f32[4,8,128]{2,1,0:T(8,128)}, bf16[4,2,128,768]{3,2,1,0:T(8,128)(2,1)}, bf16[2,2,768,768]{3,2,1,0:T(8,128)(2,1)}, bf16[2,768,384]{2,1,0:T(8,128)(2,1)}) custom-call(bf16[2,4,128,768]{3,2,1,0:T(8,128)(2,1)} %get-tuple-element.50.send_ref, f32[4,8,128]{2,1,0:T(8,128)} %get-tuple-element.51.gsend_ref, ...), custom_call_target="tpu_custom_call" | custom-call | tf_op jit(solution)/shard_map/experts/pallas_call | solution.py:710
  150.6 79.6 %back.1 = (f32[320,768]{1,0:T(8,128)}, bf16[2,4,128,768]{3,2,1,0:T(8,128)(2,1)}, bf16[2,768,384]{2,1,0:T(8,128)(2,1)}, bf16[2,768,384]{2,1,0:T(8,128)(2,1)}, f32...) custom-call(s32[2,4]{1,0:T(2,128)} %refs_0_.5, bf16[320,768]{1,0:T(8,128)(2,1)} %bitcast.15, bf16[320,768]{1,0:T(8,128)(2,1)} %bitcast.17, ...), custom_call_target="tpu_custom_call" | custom-call | tf_op jit(solution)/shard_map/back/pallas_call | solution.py:1161
  230.2 6.9 %last.1 = (bf16[320,768]{1,0:T(8,128)(2,1)}, f32[320,768]{1,0:T(8,128)}, f32[768,384]{1,0:T(8,128)}, f32[384,768]{1,0:T(8,128)}, f32[96,2304]{1,0:T(8,128)}, /*i...) custom-call(s32[2,4]{1,0:T(2,128)} %refs_0_.5, ...), custom_call_target="tpu_custom_call" | custom-call | tf_op jit(solution)/shard_map/last/pallas_call | solution.py:1198

commit v6 on v5

--- a/solution.py
+++ b/solution.py
@@ -1073,10 +1073,10 @@
     len_ref, hid_ref, meta_ref, gtok_in, made_in, grad_in, gy_in, gx_in = take(8)
     if c.gather:
         whole_ref, small_ref = take(2)
-    out_ref, gtok_out, gin_ref, gdown_ref = take(4)
+    out_ref, gtok_out, gin_out, gdown_out = take(4)
     if c.gather:
         gqkv_ref, gout_ref, gains_ref, biases_ref, grouter_ref = take(5)
-    made, gown, gy, gx, sem = take(5)
+    made, gown, gy, gx, gin_ref, gdown_ref, sem = take(7)
     z, x, y = lax.axis_index("expert"), lax.axis_index("context"), lax.axis_index("dp")
     side = lax.div(x, 2)
     piece = c.FF // 8
@@ -1092,7 +1092,8 @@
     loads.append(pltpu.make_async_copy(made_in, made, sem.at[6]))
     for load in loads:
         load.start()
-    gtok_out[...] = gtok_in[...]
+    leaving = [pltpu.make_async_copy(gtok_in, gtok_out, sem.at[7])]
+    leaving[0].start()
     if c.gather:
         core_cols = c.D // 2
         for m in range(4):
@@ -1117,6 +1118,9 @@
             gin_ref[...] = total
         else:
             gdown_ref[...] = total.T
+        src, dst = ((gin_ref, gin_out), (gdown_ref, gdown_out))[which]
+        leaving.append(pltpu.make_async_copy(src, dst, sem.at[8 + which]))
+        leaving[-1].start()
     loads[6].wait()
     for image in range(c.N):
         rows = slice(image * c.B, (image + 1) * c.B)
@@ -1130,6 +1134,8 @@
         mixture = mm(high, rows_made) + mm(low, rows_made)
         live = jnp.where(row_of((c.B, 1)) < len_ref[image, x], 1.0, 0.0)
         out_ref[rows, :] = (live * (hid_ref[rows, :] + mixture)).astype(BF16)
+    for copy in leaving:
+        copy.wait()
 
 
 def run_back(c, tok, cot, lengths, weights, vec, q, kv, lse, att, hid, mix, meta, router, xback, gback, yloc, grads, gnext):
@@ -1202,13 +1208,15 @@
         + [spec(pltpu.VMEM)] * 3
         + [spec(pl.ANY)] * 4
         + [spec(pltpu.VMEM)] * len(more),
-        out_specs=[spec(pltpu.VMEM)] * len(last),
+        out_specs=[spec(pltpu.VMEM)] + [spec(pl.ANY)] * 3 + [spec(pltpu.VMEM)] * (len(last) - 4),
         scratch_shapes=[
             pltpu.VMEM((c.N, c.E, c.cap, c.D), BF16),
             pltpu.VMEM((2, c.D, piece), BF16),
             pltpu.VMEM((2, c.D, piece), BF16),
             pltpu.VMEM((2, c.D, piece), BF16),
-            pltpu.SemaphoreType.DMA((7,)),
+            pltpu.VMEM((c.D, piece), F32),
+            pltpu.VMEM((piece, c.D), F32),
+            pltpu.SemaphoreType.DMA((10,)),
         ],
         compiler_params=pltpu.CompilerParams(vmem_limit_bytes=VMEM_LIMIT),
         name="last",

time: 241 us -> 241 us (level)
  no operation moved by 1% of the time
where the time goes in v6:
time: 241 us; the launch traced here: 237 us
  Pallas kernels  235 us (98%)
    pallas_call x1, Pallas kernels, run_back(): pl.pallas_call(functools.partial(back_kernel, c), out_shape=made, in_spec...  79.6 us
    pallas_call x1, Pallas kernels, run_front(): pl.pallas_call(functools.partial(front_kernel, c), out_shape=made, in_spe...  75.8 us
    pallas_call x1, Pallas kernels, run_experts(): pl.pallas_call(functools.partial(expert_kernel, c), out_shape=[shape((c.N...  72.8 us
    pallas_call x1, Pallas kernels, run_back(): pl.pallas_call(functools.partial(last_kernel, c), out_shape=last, in_spec...  6.94 us

profile of v6, /device:TPU:0, one launch (start us, length us, event | category | flops | bytes accessed | tf_op | source)
XLA Modules:
  0.0 237.4 jit_solution(6811841106175198273)
XLA Ops:
  0.6 1.3 fusion.5.refs_7_
  1.9 75.8 %front.1 = (bf16[4,768,768]{2,1,0:T(8,128)(2,1)}, f32[8,768]{1,0:T(8,128)}, bf16[320,768]{1,0:T(8,128)(2,1)}, bf16[2,640,2304]{2,1,0:T(8,128)(2,1)}, f32[2,6,8,3...) custom-call(s32[2,4]{1,0:T(2,128)} %refs_0_.5, ...), custom_call_target="tpu_custom_call" | custom-call | tf_op jit(solution)/shard_map/front/pallas_call | solution.py:500
  77.8 72.8 %experts.1 = (bf16[2,4,128,768]{3,2,1,0:T(8,128)(2,1)}, f32[4,8,128]{2,1,0:T(8,128)}, bf16[4,2,128,768]{3,2,1,0:T(8,128)(2,1)}, bf16[2,2,768,768]{3,2,1,0:T(8,128)(2,1)}, bf16[2,768,384]{2,1,0:T(8,128)(2,1)}) custom-call(bf16[2,4,128,768]{3,2,1,0:T(8,128)(2,1)} %get-tuple-element.50.send_ref, f32[4,8,128]{2,1,0:T(8,128)} %get-tuple-element.51.gsend_ref, ...), custom_call_target="tpu_custom_call" | custom-call | tf_op jit(solution)/shard_map/experts/pallas_call | solution.py:710
  150.6 79.6 %back.1 = (f32[320,768]{1,0:T(8,128)}, bf16[2,4,128,768]{3,2,1,0:T(8,128)(2,1)}, bf16[2,768,384]{2,1,0:T(8,128)(2,1)}, bf16[2,768,384]{2,1,0:T(8,128)(2,1)}, f32...) custom-call(s32[2,4]{1,0:T(2,128)} %refs_0_.5, bf16[320,768]{1,0:T(8,128)(2,1)} %bitcast.15, bf16[320,768]{1,0:T(8,128)(2,1)} %bitcast.17, ...), custom_call_target="tpu_custom_call" | custom-call | tf_op jit(solution)/shard_map/back/pallas_call | solution.py:1167
  230.2 6.9 %last.1 = (bf16[320,768]{1,0:T(8,128)(2,1)}, f32[320,768]{1,0:T(8,128)}, f32[768,384]{1,0:T(8,128)}, f32[384,768]{1,0:T(8,128)}, f32[96,2304]{1,0:T(8,128)}, /*i...) custom-call(s32[2,4]{1,0:T(2,128)} %refs_0_.5, ...), custom_call_target="tpu_custom_call" | custom-call | tf_op jit(solution)/shard_map/last/pallas_call | solution.py:1204
